TPU v7x, 32 devices: a whole 2x2x4 slice. The times are simulated.
32 devices in a mesh: batch: 2 (over x), blk: 16 (over z, y, core).
Axes of the slice: x: 2, y: 2, z: 4, core: 2. Of those that a mesh axis runs over, the one named last changes fastest.
Arguments:
- tokens: bfloat16 [5120, 1024], P(('batch', 'blk')), may hold values from -6 to 6
- grad_out: bfloat16 [5120, 1024], P(('batch', 'blk')), may hold values from -6 to 6
- first_rows: int32 [2], P('batch'), may hold values from 64 to 160, as said below
- span_of: int32 [16], replicated, may hold values from 0 to 15, each once
- w_qkv: bfloat16 [2, 1024, 3072], P(None, 'blk'), may hold values from -0.1875 to 0.1875
- w_out: bfloat16 [2, 1024, 1024], P(None, 'blk'), may hold values from -0.1875 to 0.1875
- w_up: bfloat16 [2, 1024, 4096], P(None, 'blk'), may hold values from -0.1875 to 0.1875
- w_down: bfloat16 [2, 4096, 1024], P(None, 'blk'), may hold values from -0.09375 to 0.09375
- vec_gain: float32 [2, 3, 1024], replicated, may hold values from 0.5 to 1.5
- vec_bias: float32 [2, 7, 1024], replicated, may hold values from -2 to 2
- mid_gain: float32 [2, 4096], replicated, may hold values from 0.5 to 1.5
- mid_bias: float32 [2, 2, 4096], replicated, may hold values from -2 to 2
- head_scale: float32 [2, 16], replicated, may hold values from 0.25 to 1.75
Outputs:
- outputs: bfloat16 [5120, 1024], P(('batch', 'blk'))
- grad_tokens: float32 [5120, 1024], P(('batch', 'blk'))
- grad_w_qkv: float32 [2, 1024, 3072], P(None, 'blk')
- grad_w_out: float32 [2, 1024, 1024], P(None, 'blk')
- grad_w_up: float32 [2, 1024, 4096], P(None, 'blk')
- grad_w_down: float32 [2, 4096, 1024], P(None, 'blk')
- grad_vec_gain: float32 [2, 3, 1024], replicated
- grad_vec_bias: float32 [2, 7, 1024], replicated
- grad_mid_gain: float32 [2, 4096], replicated
- grad_mid_bias: float32 [2, 2, 4096], replicated
- grad_head_scale: float32 [2, 16], replicated
Inputs may be any that keep to these rules, and one draw needn't show every extreme that they name: Every one of the 16 devices of group b holds first_rows[b] rows of the group's first sequence, then the rest of its 160 rows, if any, of a second sequence; first_rows[b] is 2, 3 or 5 times 32, and some group holds 160. Index j of blk holds span span_of[j], counted from a sequence's start, of every sequence of its group.
All inputs are finite; a program needn't handle non-finite values.
Results may differ from a plain program's by a relative error of at most 0.034.
Values may be sent and summed in bfloat16 or wider, within the bound.
A program may use at most 320 MiB of HBM per device.

v0:
```python
import jax
import jax.numpy as jnp
from jax import lax
from jax.sharding import PartitionSpec as P

HEAD_DIM = 64


EPSILON = 1e-05
NEGATIVE = -1e30


def shifted(x, axis, by):
    devices = lax.axis_size(axis)
    return lax.ppermute(x, axis, [(i, (i + by) % devices) for i in range(devices)])


def norm_rows(values, gains, shifts):
    average = jnp.mean(values, axis=-1, keepdims=True)
    centered = values - average
    spread = jnp.mean(centered * centered, axis=-1, keepdims=True)
    return centered * lax.rsqrt(spread + EPSILON) * gains + shifts


def mid_piece(upper, gains, shifts):
    return norm_rows(jax.nn.gelu(upper, approximate=False), gains, shifts)


def split_heads(matrix):
    return matrix.reshape(matrix.shape[0], -1, HEAD_DIM)


def block_rows(total_rows):
    chosen = total_rows
    while chosen > 1024 and chosen % 2 == 0:
        chosen = chosen // 2
    return chosen


def row_layout(first_rows, rows_here):
    within = jnp.arange(rows_here, dtype=jnp.int32)
    first_len = first_rows[0]
    second = (within >= first_len).astype(jnp.int32)
    return (second, within - second * first_len)


def visible_pairs(query_seq, query_off, query_span, key_seq, key_off, key_span):
    earlier = key_span[None, :] < query_span[:, None]
    same_span = (key_span[None, :] == query_span[:, None]) & (
        key_off[None, :] <= query_off[:, None]
    )
    return (query_seq[:, None] == key_seq[None, :]) & (earlier | same_span)


def merge_block(state_in, query_heads, keys_block, values_block, visible):
    run_peak, run_total, accumulated = state_in
    query_rows = query_heads.shape[0]
    scores = jnp.einsum(
        "qhd,khd->hqk", query_heads, split_heads(keys_block), preferred_element_type=jnp.float32
    ) * HEAD_DIM ** (-0.5)
    masked = jnp.where(visible[None], scores, NEGATIVE)
    new_peak = jnp.maximum(run_peak, jnp.max(masked, axis=-1))
    weights = jnp.where(visible[None], jnp.exp(masked - new_peak[:, :, None]), 0.0)
    factor = jnp.exp(run_peak - new_peak)
    new_total = run_total * factor + jnp.sum(weights, axis=-1)
    update = jnp.einsum(
        "hqk,khd->qhd",
        weights.astype(jnp.bfloat16),
        split_heads(values_block),
        preferred_element_type=jnp.float32,
    )
    rescaled = split_heads(accumulated) * jnp.transpose(factor)[:, :, None]
    return (new_peak, new_total, (rescaled + update).reshape(query_rows, -1))


def grad_block(query_heads, log_total, delta, dout_heads, keys_block, values_block, visible):
    key_heads = split_heads(keys_block)
    value_heads = split_heads(values_block)
    scores = jnp.einsum(
        "qhd,khd->hqk", query_heads, key_heads, preferred_element_type=jnp.float32
    ) * HEAD_DIM ** (-0.5)
    probs = jnp.where(visible[None], jnp.exp(scores - log_total[:, :, None]), 0.0)
    dprobs = jnp.einsum("qhd,khd->hqk", dout_heads, value_heads, preferred_element_type=jnp.float32)
    dscores = (probs * (dprobs - delta[:, :, None])).astype(jnp.bfloat16)
    add_query = jnp.einsum("hqk,khd->qhd", dscores, key_heads, preferred_element_type=jnp.float32)
    add_keys = jnp.einsum("hqk,qhd->khd", dscores, query_heads, preferred_element_type=jnp.float32)
    add_values = jnp.einsum(
        "hqk,qhd->khd", probs.astype(jnp.bfloat16), dout_heads, preferred_element_type=jnp.float32
    )
    return (
        add_query.reshape(query_heads.shape[0], -1),
        add_keys.reshape(key_heads.shape[0], -1),
        add_values.reshape(key_heads.shape[0], -1),
    )


def unchanged(state_in):
    return state_in


def attention_forward(query_low, keys_low, values_low, layout):
    seq_ids, offsets, span_of, my_span, my_index = layout
    rows_here, row_width = query_low.shape
    heads_here = row_width // HEAD_DIM
    query_heads = split_heads(query_low)
    query_span = jnp.full((rows_here,), my_span, jnp.int32)
    initial = (
        jnp.full((heads_here, rows_here), NEGATIVE, jnp.float32),
        jnp.zeros((heads_here, rows_here), jnp.float32),
        jnp.zeros((rows_here, row_width), jnp.float32),
    )
    running = initial
    key_part = lax.all_gather(keys_low, "blk", axis=0, tiled=True)
    value_part = lax.all_gather(values_low, "blk", axis=0, tiled=True)
    part_rows = key_part.shape[0]
    step_rows = block_rows(part_rows)

    def one_step(state_in, step_index):
        block_start = step_index * step_rows
        global_rows = block_start + jnp.arange(step_rows, dtype=jnp.int32)
        key_span = span_of[global_rows // rows_here]
        local_rows = global_rows % rows_here
        visible = visible_pairs(
            seq_ids, offsets, query_span, seq_ids[local_rows], offsets[local_rows], key_span
        )
        keys_block = lax.dynamic_slice_in_dim(key_part, block_start, step_rows, 0)
        values_block = lax.dynamic_slice_in_dim(value_part, block_start, step_rows, 0)

        def one_compute(inner_state):
            return merge_block(inner_state, query_heads, keys_block, values_block, visible)

        return (lax.cond(jnp.any(key_span <= my_span), one_compute, unchanged, state_in), None)

    running, _ = lax.scan(one_step, running, jnp.arange(part_rows // step_rows, dtype=jnp.int32))
    run_peak, run_total, accumulated = running
    mixed_heads = (split_heads(accumulated) / jnp.transpose(run_total)[:, :, None]).reshape(
        rows_here, row_width
    )
    return (mixed_heads, run_peak + jnp.log(run_total))


def cycle_backward(query_low, keys_low, values_low, log_total, delta, dout_low, layout):
    seq_ids, offsets, span_of, my_span, my_index = layout
    rows_here, row_width = query_low.shape
    blocks_total = lax.axis_size("blk")
    query_heads = split_heads(query_low)
    dout_heads = split_heads(dout_low)
    query_span = jnp.full((rows_here,), my_span, jnp.int32)

    def turn(turn_index, carried):
        keys_now, values_now, dkeys, dvalues, dquery = carried
        source = (my_index - turn_index) % blocks_total
        source_span = span_of[source]
        key_span = jnp.full((rows_here,), source_span, jnp.int32)
        visible = visible_pairs(seq_ids, offsets, query_span, seq_ids, offsets, key_span)

        def turn_compute(inner_state):
            add_query, add_keys, add_values = grad_block(
                query_heads, log_total, delta, dout_heads, keys_now, values_now, visible
            )
            return (
                inner_state[0] + add_query,
                inner_state[1] + add_keys,
                inner_state[2] + add_values,
            )

        dquery, dkeys, dvalues = lax.cond(
            source_span <= my_span, turn_compute, unchanged, (dquery, dkeys, dvalues)
        )
        keys_now, values_now = shifted((keys_now, values_now), "blk", 1)
        dkeys, dvalues = (
            shifted(dkeys.astype(jnp.bfloat16), "blk", 1).astype(dkeys.dtype),
            shifted(dvalues.astype(jnp.bfloat16), "blk", 1).astype(dvalues.dtype),
        )
        return (keys_now, values_now, dkeys, dvalues, dquery)

    zeros_rows = jnp.zeros((rows_here, row_width), jnp.float32)
    result = lax.fori_loop(
        0, blocks_total, turn, (keys_low, values_low, zeros_rows, zeros_rows, zeros_rows)
    )
    return (result[4], result[2], result[3])


def layer_forward(inputs, weights, gains, biases, middle_gain, middle_bias, heads_scale, layout):
    weight_qkv, weight_out, weight_up, weight_down = weights
    row_width = inputs.shape[1]
    normed, pre_pull = jax.vjp(norm_rows, inputs, gains[0], biases[0])
    normed_low = normed.astype(jnp.bfloat16)
    projected = jnp.dot(normed_low, weight_qkv, preferred_element_type=jnp.float32)
    query_low = (projected[:, :row_width] + biases[3]).astype(jnp.bfloat16)
    keys_low = projected[:, row_width : 2 * row_width].astype(jnp.bfloat16)
    values_low = (projected[:, 2 * row_width :] + biases[4]).astype(jnp.bfloat16)
    mixed_heads, log_total = attention_forward(query_low, keys_low, values_low, layout)
    scaled_low = (mixed_heads * jnp.repeat(heads_scale, HEAD_DIM)).astype(jnp.bfloat16)
    branch = jnp.dot(scaled_low, weight_out, preferred_element_type=jnp.float32) + biases[5]
    post_normed, post_pull = jax.vjp(norm_rows, branch, gains[1], biases[1])
    middle_res = inputs + post_normed
    ffn_normed, ffn_pull = jax.vjp(norm_rows, middle_res, gains[2], biases[2])
    ffn_low = ffn_normed.astype(jnp.bfloat16)
    upper = jnp.dot(ffn_low, weight_up, preferred_element_type=jnp.float32) + middle_bias[1]
    middle, mid_pull = jax.vjp(mid_piece, upper, middle_gain, middle_bias[0])
    middle_low = middle.astype(jnp.bfloat16)
    results = middle_res + (
        jnp.dot(middle_low, weight_down, preferred_element_type=jnp.float32) + biases[6]
    )
    record = {
        "pre_pull": pre_pull,
        "normed_low": normed_low,
        "query_low": query_low,
        "keys_low": keys_low,
        "values_low": values_low,
        "log_total": log_total,
        "mixed_heads": mixed_heads,
        "scaled_low": scaled_low,
        "post_pull": post_pull,
        "ffn_pull": ffn_pull,
        "ffn_low": ffn_low,
        "mid_pull": mid_pull,
        "middle_low": middle_low,
        "weights": weights,
    }
    return (results, record)


def layer_backward(d_results, record, weights, heads_scale, layout):
    weight_qkv, weight_out, weight_up, weight_down = weights
    rows_here, row_width = d_results.shape
    d_results_low = d_results.astype(jnp.bfloat16)
    grad_down = jnp.einsum(
        "tf,td->fd", record["middle_low"], d_results_low, preferred_element_type=jnp.float32
    )
    grad_down_bias = jnp.sum(d_results_low, axis=0, dtype=jnp.float32)
    d_middle = jnp.einsum(
        "td,fd->tf", d_results_low, weight_down, preferred_element_type=jnp.float32
    )
    d_upper, grad_mid_gain, grad_mid_shift = record["mid_pull"](d_middle)
    d_upper_low = d_upper.astype(jnp.bfloat16)
    grad_up = jnp.einsum(
        "td,tf->df", record["ffn_low"], d_upper_low, preferred_element_type=jnp.float32
    )
    grad_up_bias = jnp.sum(d_upper_low, axis=0, dtype=jnp.float32)
    d_ffn = jnp.einsum("tf,df->td", d_upper_low, weight_up, preferred_element_type=jnp.float32)
    d_res_part, grad_gain_ffn, grad_shift_ffn = record["ffn_pull"](d_ffn)
    d_middle_res = d_results + d_res_part
    d_branch, grad_gain_post, grad_shift_post = record["post_pull"](d_middle_res)
    d_branch_low = d_branch.astype(jnp.bfloat16)
    grad_out_w = jnp.einsum(
        "tc,td->cd", record["scaled_low"], d_branch_low, preferred_element_type=jnp.float32
    )
    grad_out_bias = jnp.sum(d_branch_low, axis=0, dtype=jnp.float32)
    d_scaled = jnp.einsum("td,cd->tc", d_branch_low, weight_out, preferred_element_type=jnp.float32)
    mixed_heads = record["mixed_heads"]
    grad_heads = jnp.sum((d_scaled * mixed_heads).reshape(rows_here, -1, HEAD_DIM), axis=(0, 2))
    d_mixed_low = (d_scaled * jnp.repeat(heads_scale, HEAD_DIM)).astype(jnp.bfloat16)
    delta = jnp.transpose(
        jnp.sum(
            (d_mixed_low.astype(jnp.float32) * mixed_heads).reshape(rows_here, -1, HEAD_DIM), axis=2
        )
    )
    dquery, dkeys, dvalues = cycle_backward(
        record["query_low"],
        record["keys_low"],
        record["values_low"],
        record["log_total"],
        delta,
        d_mixed_low,
        layout,
    )
    scale_factor = HEAD_DIM ** (-0.5)
    d_proj_low = jnp.concatenate(
        [dquery * scale_factor, dkeys * scale_factor, dvalues], axis=1
    ).astype(jnp.bfloat16)
    grad_qkv = jnp.einsum(
        "tc,te->ce", record["normed_low"], d_proj_low, preferred_element_type=jnp.float32
    )
    grad_q_bias = jnp.sum(d_proj_low[:, :row_width], axis=0, dtype=jnp.float32)
    grad_v_bias = jnp.sum(d_proj_low[:, 2 * row_width :], axis=0, dtype=jnp.float32)
    d_normed = jnp.einsum("te,ce->tc", d_proj_low, weight_qkv, preferred_element_type=jnp.float32)
    d_in_part, grad_gain_pre, grad_shift_pre = record["pre_pull"](d_normed)
    d_inputs = d_middle_res + d_in_part
    big_grads = (grad_qkv, grad_out_w, grad_up, grad_down)
    gain_grads = jnp.stack([grad_gain_pre, grad_gain_post, grad_gain_ffn])
    bias_grads = jnp.stack(
        [
            grad_shift_pre,
            grad_shift_post,
            grad_shift_ffn,
            grad_q_bias,
            grad_v_bias,
            grad_out_bias,
            grad_down_bias,
        ]
    )
    small_grads = (
        gain_grads,
        bias_grads,
        grad_mid_gain,
        jnp.stack([grad_mid_shift, grad_up_bias]),
        grad_heads,
    )
    return (d_inputs, big_grads, small_grads)


def local(
    tokens,
    grad_out,
    first_rows,
    span_of,
    w_qkv,
    w_out,
    w_up,
    w_down,
    vec_gain,
    vec_bias,
    mid_gain,
    mid_bias,
    head_scale,
):
    rows_here = tokens.shape[0]
    my_index = lax.axis_index("blk")
    my_span = span_of[my_index]
    seq_ids, offsets = row_layout(first_rows, rows_here)
    layout = (seq_ids, offsets, span_of, my_span, my_index)
    current = tokens.astype(jnp.float32)
    records = []
    for layer_index in range(2):
        weights = (
            lax.all_gather(w_qkv[layer_index], "blk", axis=0, tiled=True),
            lax.all_gather(w_out[layer_index], "blk", axis=0, tiled=True),
            lax.all_gather(w_up[layer_index], "blk", axis=0, tiled=True),
            lax.all_gather(w_down[layer_index], "blk", axis=0, tiled=True),
        )
        current, record = layer_forward(
            current,
            weights,
            vec_gain[layer_index],
            vec_bias[layer_index],
            mid_gain[layer_index],
            mid_bias[layer_index],
            head_scale[layer_index],
            layout,
        )
        records.append(record)
    results_low = current.astype(jnp.bfloat16)
    d_current = grad_out.astype(jnp.float32)
    shard_grads = [None, None]
    small_grads = [None, None]
    for layer_index in (1, 0):
        weights = (
            lax.all_gather(w_qkv[layer_index], "blk", axis=0, tiled=True),
            lax.all_gather(w_out[layer_index], "blk", axis=0, tiled=True),
            lax.all_gather(w_up[layer_index], "blk", axis=0, tiled=True),
            lax.all_gather(w_down[layer_index], "blk", axis=0, tiled=True),
        )
        d_current, big_grads, small_part = layer_backward(
            d_current, records[layer_index], weights, head_scale[layer_index], layout
        )
        shard_grads[layer_index] = (
            lax.psum_scatter(
                big_grads[0].astype(jnp.bfloat16), "blk", scatter_dimension=0, tiled=True
            ).astype(jnp.float32),
            lax.psum_scatter(
                big_grads[1].astype(jnp.bfloat16), "blk", scatter_dimension=0, tiled=True
            ).astype(jnp.float32),
            lax.psum_scatter(
                big_grads[2].astype(jnp.bfloat16), "blk", scatter_dimension=0, tiled=True
            ).astype(jnp.float32),
            lax.psum_scatter(
                big_grads[3].astype(jnp.bfloat16), "blk", scatter_dimension=0, tiled=True
            ).astype(jnp.float32),
        )
        small_grads[layer_index] = small_part
    stacked_small = [
        jnp.stack([small_grads[0][item_index], small_grads[1][item_index]])
        for item_index in range(5)
    ]
    summed_small = (
        lax.psum(stacked_small[0].astype(jnp.bfloat16), "blk").astype(jnp.float32),
        lax.psum(stacked_small[1].astype(jnp.bfloat16), "blk").astype(jnp.float32),
        lax.psum(stacked_small[2].astype(jnp.bfloat16), "blk").astype(jnp.float32),
        lax.psum(stacked_small[3].astype(jnp.bfloat16), "blk").astype(jnp.float32),
        lax.psum(stacked_small[4].astype(jnp.bfloat16), "blk").astype(jnp.float32),
    )
    stacked_big = [
        jnp.stack([shard_grads[0][item_index], shard_grads[1][item_index]])
        for item_index in range(4)
    ]
    totals = (
        lax.psum(stacked_big[0].astype(jnp.bfloat16), "batch").astype(jnp.float32),
        lax.psum(stacked_big[1].astype(jnp.bfloat16), "batch").astype(jnp.float32),
        lax.psum(stacked_big[2].astype(jnp.bfloat16), "batch").astype(jnp.float32),
        lax.psum(stacked_big[3].astype(jnp.bfloat16), "batch").astype(jnp.float32),
        lax.psum(summed_small[0].astype(jnp.bfloat16), "batch").astype(jnp.float32),
        lax.psum(summed_small[1].astype(jnp.bfloat16), "batch").astype(jnp.float32),
        lax.psum(summed_small[2].astype(jnp.bfloat16), "batch").astype(jnp.float32),
        lax.psum(summed_small[3].astype(jnp.bfloat16), "batch").astype(jnp.float32),
        lax.psum(summed_small[4].astype(jnp.bfloat16), "batch").astype(jnp.float32),
    )
    return (
        results_low,
        d_current,
        totals[0],
        totals[1],
        totals[2],
        totals[3],
        totals[4],
        totals[5],
        totals[6],
        totals[7],
        totals[8],
    )


def solution(mesh):
    placed = (
        P(("batch", "blk"), None),
        P(("batch", "blk"), None),
        P("batch"),
        P(),
        P(None, "blk", None),
        P(None, "blk", None),
        P(None, "blk", None),
        P(None, "blk", None),
        P(),
        P(),
        P(),
        P(),
        P(),
    )
    return jax.shard_map(
        local,
        mesh=mesh,
        in_specs=placed,
        out_specs=(
            P(("batch", "blk"), None),
            P(("batch", "blk"), None),
            P(None, "blk", None),
            P(None, "blk", None),
            P(None, "blk", None),
            P(None, "blk", None),
            P(),
            P(),
            P(),
            P(),
            P(),
        ),
        check_vma=False,
    )
```

profile of v0, /device:TPU:0, one launch (start us, length us, event | category | flops | bytes accessed | tf_op | source)
XLA Modules:
  0.0 3349.9 jit_solution(2456715998389180856)
XLA Ops:
  13.1 62.4 %all-gather.29.cloned.1.call-done = bf16[1,1024,3072]{2,1,0:T(8,128)(2,1)} async-done(((bf16[1,64,3072]{2,1,0:T(8,128)(2,1)}), bf16[1,1024,3072]{2,1,0:T(8,128)(2,1)}) %all-gather.29.cloned.1.call-update) | async-done | bytes 6291472 | tf_op jit(solution)/shard_map/all_gather | solution.py:328
  89.2 46.0 %all-gather.21.cloned.1.call-done = bf16[2560,1024]{1,0:T(8,128)(2,1)} async-done(((bf16[160,1024]{1,0:T(8,128)(2,1)}), bf16[2560,1024]{1,0:T(8,128)(2,1)}) %all-gather.21.cloned.1.call-update) | async-done | bytes 5242896 | tf_op jit(solution)/shard_map/all_gather | solution.py:113
  143.2 48.9 %all-gather.23.cloned.1.call-done = bf16[2560,1024]{1,0:T(8,128)(2,1)} async-done(((bf16[160,1024]{1,0:T(8,128)(2,1)}), bf16[2560,1024]{1,0:T(8,128)(2,1)}) %all-gather.23.cloned.1.call-update) | async-done | bytes 5242896 | tf_op jit(solution)/shard_map/all_gather | solution.py:114
  200.0 134.2 %while.88 = (s32[]{:T(128)}, f32[16,160]{1,0:T(8,128)S(1)}, f32[16,160]{1,0:T(8,128)S(1)}, f32[160,1024]{0,1:T(8,128)S(1)}, s32[4]{0:T(128)S(1)}, /*index=5*/s32...) while((s32[]{:T(128)}, f32[16,160]{1,0:T(8,128)S(1)}, ...), condition=%wide.region_8.9_spmd.clone.clone, body=%wide.region_2.8_spmd.clone.clone.sunk | while | flops 441650944 | bytes 29812436 | solution.py:134
  214.4 19.2 conditional.18
  248.0 19.2 conditional.18
  281.6 19.2 conditional.18
  315.1 19.0 conditional.18
  353.6 32.5 all-gather.35.cloned.1.call-done
  392.3 56.8 %all-gather.37.cloned.1.call-done = bf16[1,1024,3072]{2,1,0:T(8,128)(2,1)} async-done(((bf16[1,64,3072]{2,1,0:T(8,128)(2,1)}), bf16[1,1024,3072]{2,1,0:T(8,128)(2,1)}) %all-gather.37.cloned.1.call-update) | async-done | bytes 6291472 | tf_op jit(solution)/shard_map/all_gather | solution.py:328
  463.1 45.9 %all-gather.25.cloned.1.call-done = bf16[2560,1024]{1,0:T(8,128)(2,1)} async-done(((bf16[160,1024]{1,0:T(8,128)(2,1)}), bf16[2560,1024]{1,0:T(8,128)(2,1)}) %all-gather.25.cloned.1.call-update) | async-done | bytes 5242896 | tf_op jit(solution)/shard_map/all_gather | solution.py:113
  517.0 48.8 %all-gather.27.cloned.1.call-done = bf16[2560,1024]{1,0:T(8,128)(2,1)} async-done(((bf16[160,1024]{1,0:T(8,128)(2,1)}), bf16[2560,1024]{1,0:T(8,128)(2,1)}) %all-gather.27.cloned.1.call-update) | async-done | bytes 5242896 | tf_op jit(solution)/shard_map/all_gather | solution.py:114
  573.7 136.4 %while.89 = (s32[]{:T(128)}, f32[16,160]{1,0:T(8,128)S(1)}, f32[16,160]{1,0:T(8,128)S(1)}, f32[160,1024]{0,1:T(8,128)S(1)}, s32[4]{0:T(128)S(1)}, /*index=5*/s32...) while((s32[]{:T(128)}, f32[16,160]{1,0:T(8,128)S(1)}, ...), condition=%wide.region_23.24_spmd.clone.clone, body=%wide.region_17.23_spmd.clone.clone.sunk | while | flops 441650944 | bytes 29812436 | solution.py:134
  588.6 19.2 conditional.19
  622.7 19.2 conditional.19
  656.8 19.4 conditional.19
  691.1 19.0 conditional.19
  727.6 32.0 all-gather.43.cloned.1.call-done
  784.1 777.4 %while.90 = (s32[]{:T(128)}, bf16[160,1024]{0,1:T(8,128)(2,1)S(1)}, bf16[160,1024]{0,1:T(8,128)(2,1)}, f32[160,1024]{0,1:T(8,128)S(1)}, f32[160,1024]{0,1:T(8,12...) while((s32[]{:T(128)}, bf16[160,1024]{0,1:T(8,128)(2,1)S(1)}, ...), condition=%wide.region_40.41_spmd.clone.clone.clone, body=%wide.region_37.40_spmd.clone.clone.clone.sunk | while | flops 267843216 | bytes 42547112 | solution.py:178
  790.6 14.4 conditional.20
  997.4 14.4 conditional.20
  1344.9 14.4 conditional.20
  1396.6 14.4 conditional.20
  1527.2 16.9 collective-permute-start.3
  1593.0 783.9 %while.91 = (s32[]{:T(128)}, bf16[160,1024]{0,1:T(8,128)(2,1)S(1)}, bf16[160,1024]{0,1:T(8,128)(2,1)}, f32[160,1024]{0,1:T(8,128)S(1)}, f32[160,1024]{0,1:T(8,12...) while((s32[]{:T(128)}, bf16[160,1024]{0,1:T(8,128)(2,1)S(1)}, ...), condition=%wide.region_53.54_spmd.clone.clone.clone, body=%wide.region_50.53_spmd.clone.clone.clone.sunk | while | flops 267843216 | bytes 42547112 | solution.py:178
  1599.6 14.4 conditional.21
  1651.8 14.4 conditional.21
  1703.5 14.4 conditional.21
  1755.3 14.4 conditional.21
  1807.0 14.4 conditional.21
  1897.1 14.4 conditional.21
  1948.8 14.4 conditional.21
  2000.6 14.4 conditional.21
  2052.3 14.4 conditional.21
  2104.1 14.4 conditional.21
  2155.8 14.4 conditional.21
  2207.6 14.4 conditional.21
  2342.7 16.9 collective-permute-start.7
  2437.8 41.0 %all-reduce.7.cloned.1.call-done = (bf16[2,3,1024]{2,1,0:T(4,128)(2,1)}, bf16[2,7,1024]{2,1,0:T(8,128)(2,1)}, bf16[2,4096]{1,0:T(2,128)(2,1)}, bf16[2,2,4096]{2,1,0:T(2,128)(2,1)}, bf16[2,16]{1,0:T(2,128)(2,1)}) async-done(((bf16[2,3,1024]{2,1,0:T(4,128)(2,1)}, bf16[2,7,1024]{2,1,0:T(8,128)(2,1)}, bf16[2,4096]{1,0:T(2,128)(2,1)}, bf16[2,2,4096]{2,1,0:T(2,128)(2,1)}, bf16[2,16]{1,0:T(2,128)(2,1)}), ...) | async-done | bytes 90192 | tf_op jit(solution)/shard_map/psum | solution.py:378
  2478.9 68.2 %reduce-scatter.15.cloned.1.call-done = bf16[64,1024]{1,0:T(8,128)(2,1)} async-done(((bf16[1024,1024]{1,0:T(8,128)(2,1)}), bf16[64,1024]{1,0:T(8,128)(2,1)}) %reduce-scatter.15.cloned.1.call-update) | async-done | bytes 131088 | tf_op jit(solution)/shard_map/reduce_scatter | solution.py:362
  2547.0 65.2 %reduce-scatter.13.cloned.1.call-done = bf16[64,1024]{1,0:T(8,128)(2,1)} async-done(((bf16[1024,1024]{1,0:T(8,128)(2,1)}), bf16[64,1024]{1,0:T(8,128)(2,1)}) %reduce-scatter.13.cloned.1.call-update) | async-done | bytes 131088 | tf_op jit(solution)/shard_map/reduce_scatter | solution.py:362
  2613.9 86.4 %reduce-scatter.11.cloned.1.call-done = bf16[64,3072]{1,0:T(8,128)(2,1)} async-done(((bf16[1024,3072]{1,0:T(8,128)(2,1)}), bf16[64,3072]{1,0:T(8,128)(2,1)}) %reduce-scatter.11.cloned.1.call-update) | async-done | bytes 393232 | tf_op jit(solution)/shard_map/reduce_scatter | solution.py:359
  2700.3 88.8 %reduce-scatter.9.cloned.1.call-done = bf16[64,3072]{1,0:T(8,128)(2,1)} async-done(((bf16[1024,3072]{1,0:T(8,128)(2,1)}), bf16[64,3072]{1,0:T(8,128)(2,1)}) %reduce-scatter.9.cloned.1.call-update) | async-done | bytes 393232 | tf_op jit(solution)/shard_map/reduce_scatter | solution.py:359
  2791.2 105.8 %reduce-scatter.19.cloned.1.call-done = bf16[64,4096]{1,0:T(8,128)(2,1)} async-done(((bf16[1024,4096]{1,0:T(8,128)(2,1)}), bf16[64,4096]{1,0:T(8,128)(2,1)}) %reduce-scatter.19.cloned.1.call-update) | async-done | bytes 524304 | tf_op jit(solution)/shard_map/reduce_scatter | solution.py:365
  2896.9 108.4 %reduce-scatter.17.cloned.1.call-done = bf16[64,4096]{1,0:T(8,128)(2,1)} async-done(((bf16[1024,4096]{1,0:T(8,128)(2,1)}), bf16[64,4096]{1,0:T(8,128)(2,1)}) %reduce-scatter.17.cloned.1.call-update) | async-done | bytes 524304 | tf_op jit(solution)/shard_map/reduce_scatter | solution.py:365
  3007.6 106.0 %reduce-scatter.23.cloned.1.call-done = bf16[256,1024]{1,0:T(8,128)(2,1)} async-done(((bf16[4096,1024]{1,0:T(8,128)(2,1)}), bf16[256,1024]{1,0:T(8,128)(2,1)}) %reduce-scatter.23.cloned.1.call-update) | async-done | bytes 524304 | tf_op jit(solution)/shard_map/reduce_scatter | solution.py:368
  3113.6 108.4 %reduce-scatter.21.cloned.1.call-done = bf16[256,1024]{1,0:T(8,128)(2,1)} async-done(((bf16[4096,1024]{1,0:T(8,128)(2,1)}), bf16[256,1024]{1,0:T(8,128)(2,1)}) %reduce-scatter.21.cloned.1.call-update) | async-done | bytes 524304 | tf_op jit(solution)/shard_map/reduce_scatter | solution.py:368
  3252.2 83.5 %all-reduce.11.cloned.1.call-done = (bf16[2,64,3072]{2,1,0:T(8,128)(2,1)}, bf16[2,64,1024]{2,1,0:T(8,128)(2,1)}, bf16[2,64,4096]{2,1,0:T(8,128)(2,1)}, bf16[2,256,1024]{2,1,0:T(8,128)(2,1)}) async-done(((bf16[2,64,3072]{2,1,0:T(8,128)(2,1)}, bf16[2,64,1024]{2,1,0:T(8,128)(2,1)}, bf16[2,64,4096]{2,1,0:T(8,128)(2,1)}, bf16[2,256,1024]{2,1,0:T(8,128)(2,1)}), (bf16[2,64,3072]{2,1,0:T(8,128)(2,1)}, ...) | async-done | bytes 3145744 | tf_op jit(solution)/shard_map/psum | solution.py:389
  (1882 shorter events, 2075.4 us)
Async XLA Ops:
  7.2 68.3 %all-gather.29.cloned.1.call-start = ((), (), s32[]{:S(2)}) async-start(), calls=%async_computation.20 | async-start | bytes 6684672 | tf_op jit(solution)/shard_map/all_gather | solution.py:328
  9.4 125.8 %all-gather.21.cloned.1.call-start = ((), (), s32[]{:S(2)}) async-start(), calls=%async_computation.8 | async-start | bytes 5570560 | tf_op jit(solution)/shard_map/all_gather | solution.py:113
  80.4 111.6 %all-gather.23.cloned.1.call-start = ((), (), s32[]{:S(2)}) async-start(), calls=%async_computation.9 | async-start | bytes 5570560 | tf_op jit(solution)/shard_map/all_gather | solution.py:114
  81.3 256.1 %all-gather.31.cloned.1.call-start = ((), (), s32[]{:S(2)}) async-start(), calls=%async_computation.21 | async-start | bytes 2228224 | tf_op jit(solution)/shard_map/all_gather | solution.py:329
  82.2 259.2 %all-gather.33.cloned.1.call-start = ((), (), s32[]{:S(2)}) async-start(), calls=%async_computation.22 | async-start | bytes 8912896 | tf_op jit(solution)/shard_map/all_gather | solution.py:330
  84.5 301.6 %all-gather.35.cloned.1.call-start = ((), (), s32[]{:S(2)}) async-start(), calls=%async_computation.23 | async-start | bytes 8912896 | tf_op jit(solution)/shard_map/all_gather | solution.py:331
  85.6 363.4 %all-gather.37.cloned.1.call-start = ((), (), s32[]{:S(2)}) async-start(), calls=%async_computation.24 | async-start | bytes 6684672 | tf_op jit(solution)/shard_map/all_gather | solution.py:328
  86.4 422.5 %all-gather.25.cloned.1.call-start = ((), (), s32[]{:S(2)}) async-start(), calls=%async_computation.10 | async-start | bytes 5570560 | tf_op jit(solution)/shard_map/all_gather | solution.py:113
  454.2 111.6 %all-gather.27.cloned.1.call-start = ((), (), s32[]{:S(2)}) async-start(), calls=%async_computation.11 | async-start | bytes 5570560 | tf_op jit(solution)/shard_map/all_gather | solution.py:114
  455.3 256.2 %all-gather.39.cloned.1.call-start = ((), (), s32[]{:S(2)}) async-start(), calls=%async_computation.25 | async-start | bytes 2228224 | tf_op jit(solution)/shard_map/all_gather | solution.py:329
  455.9 259.9 %all-gather.41.cloned.1.call-start = ((), (), s32[]{:S(2)}) async-start(), calls=%async_computation.26 | async-start | bytes 8912896 | tf_op jit(solution)/shard_map/all_gather | solution.py:330
  456.6 303.0 %all-gather.43.cloned.1.call-start = ((), (), s32[]{:S(2)}) async-start(), calls=%async_computation.27 | async-start | bytes 8912896 | tf_op jit(solution)/shard_map/all_gather | solution.py:331
  457.2 2021.6 %all-reduce.7.cloned.1.call-start = ((), (), s32[]{:S(2)}) async-start(), calls=%async_computation.28 | async-start | bytes 197632 | tf_op jit(solution)/shard_map/psum | solution.py:378
  809.3 25.3 collective-permute-start.1
  860.1 26.2 collective-permute-start.1
  911.8 26.2 collective-permute-start.1
  963.5 26.2 collective-permute-start.1
  1015.2 26.2 collective-permute-start.1
  1054.1 24.6 collective-permute-start.1
  1104.2 26.2 collective-permute-start.1
  1155.9 26.2 collective-permute-start.1
  1207.6 26.2 collective-permute-start.1
  1259.3 26.2 collective-permute-start.1
  1311.0 26.2 collective-permute-start.1
  1362.7 26.2 collective-permute-start.1
  1414.4 26.2 collective-permute-start.1
  1451.7 26.2 collective-permute-start.1
  1672.7 23.1 collective-permute-start.5
  1721.8 25.7 collective-permute-start.5
  1773.1 26.2 collective-permute-start.5
  1824.9 26.2 collective-permute-start.5
  1967.1 25.7 collective-permute-start.5
  2018.4 26.2 collective-permute-start.5
  2070.2 26.2 collective-permute-start.5
  2121.9 26.2 collective-permute-start.5
  2173.7 26.2 collective-permute-start.5
  2225.5 26.2 collective-permute-start.5
  2262.8 26.2 collective-permute-start.5
  2389.7 157.3 %reduce-scatter.15.cloned.1.call-start = ((), (), s32[]{:S(2)}) async-start(), calls=%async_computation.15 | async-start | bytes 2228224 | tf_op jit(solution)/shard_map/reduce_scatter | solution.py:362
  2391.9 220.3 %reduce-scatter.13.cloned.1.call-start = ((), (), s32[]{:S(2)}) async-start(), calls=%async_computation.14 | async-start | bytes 2228224 | tf_op jit(solution)/shard_map/reduce_scatter | solution.py:362
  2394.1 306.2 %reduce-scatter.11.cloned.1.call-start = ((), (), s32[]{:S(2)}) async-start(), calls=%async_computation.13 | async-start | bytes 6684672 | tf_op jit(solution)/shard_map/reduce_scatter | solution.py:359
  2400.1 389.0 %reduce-scatter.9.cloned.1.call-start = ((), (), s32[]{:S(2)}) async-start(), calls=%async_computation.12 | async-start | bytes 6684672 | tf_op jit(solution)/shard_map/reduce_scatter | solution.py:359
  2406.1 490.9 %reduce-scatter.19.cloned.1.call-start = ((), (), s32[]{:S(2)}) async-start(), calls=%async_computation.17 | async-start | bytes 8912896 | tf_op jit(solution)/shard_map/reduce_scatter | solution.py:365
  2413.4 592.0 %reduce-scatter.17.cloned.1.call-start = ((), (), s32[]{:S(2)}) async-start(), calls=%async_computation.16 | async-start | bytes 8912896 | tf_op jit(solution)/shard_map/reduce_scatter | solution.py:365
  2420.7 692.9 %reduce-scatter.23.cloned.1.call-start = ((), (), s32[]{:S(2)}) async-start(), calls=%async_computation.19 | async-start | bytes 8912896 | tf_op jit(solution)/shard_map/reduce_scatter | solution.py:368
  2429.2 792.8 %reduce-scatter.21.cloned.1.call-start = ((), (), s32[]{:S(2)}) async-start(), calls=%async_computation.18 | async-start | bytes 8912896 | tf_op jit(solution)/shard_map/reduce_scatter | solution.py:368
  2437.7 807.8 %all-reduce.9.cloned.1.call-start = ((), (), s32[]{:S(2)}) async-start(), calls=%async_computation.29 | async-start | bytes 197632 | tf_op jit(solution)/shard_map/psum | solution.py:393
  2478.8 856.9 %all-reduce.11.cloned.1.call-start = ((), (), s32[]{:S(2)}) async-start(), calls=%async_computation.30 | async-start | bytes 6291456 | tf_op jit(solution)/shard_map/psum | solution.py:389
  (405 other events, 6163.5 us)
Sparse Core Ops, SparseCore 0:
  10.9 64.5 all-gather.28
  80.5 54.5 all-gather.20
  137.4 54.5 all-gather.22
  194.1 39.8 all-gather.30
  236.6 73.6 all-gather.32
  312.9 73.1 all-gather.34
  388.9 60.0 all-gather.36
  454.3 54.5 all-gather.24
  511.2 54.5 all-gather.26
  567.8 40.0 all-gather.38
  610.1 73.7 all-gather.40
  686.4 73.1 all-gather.42
  2389.9 88.9 all-reduce.6
  2483.0 64.0 reduce-scatter.14
  2551.6 60.5 reduce-scatter.12
  2616.0 84.2 reduce-scatter.10
  2704.6 84.4 reduce-scatter.8
  2793.0 103.8 reduce-scatter.18
  2901.0 104.3 reduce-scatter.16
  3009.3 104.3 reduce-scatter.22
  3117.7 104.3 reduce-scatter.20
  3224.6 20.8 all-reduce.8
  3248.5 87.1 all-reduce.10
where the time goes:
time: 3370 us; the launch traced here: 3350 us
  waiting for transfers between devices  1930 us (57%)
  other arithmetic  595 us (18%)
  matrix products  313 us (9%)
  local copies, waits for them, and re-layouts  311 us (9%)
  loops' own time  104 us (3%)
  starting transfers between devices  83.4 us (2%)
    ppermute x128, waiting for transfers between devices, shifted(): lax.ppermute(x, axis, [(i, (i + by) % devices) for i in range(devices)])  677 us
    reduce_scatter x2, waiting for transfers between devices, local(): lax.psum_scatter(big_grads[3].astype(jnp.bfloat16), 'blk', scatter_dimens...  214 us
    reduce_scatter x2, waiting for transfers between devices, local(): lax.psum_scatter(big_grads[2].astype(jnp.bfloat16), 'blk', scatter_dimens...  214 us
    reduce_scatter x2, waiting for transfers between devices, local(): lax.psum_scatter(big_grads[0].astype(jnp.bfloat16), 'blk', scatter_dimens...  175 us
    reduce_scatter x2, waiting for transfers between devices, local(): lax.psum_scatter(big_grads[1].astype(jnp.bfloat16), 'blk', scatter_dimens...  133 us
    all_gather x2, waiting for transfers between devices, local(): lax.all_gather(w_qkv[layer_index], 'blk', axis=0, tiled=True)  119 us
    all_gather x2, waiting for transfers between devices, attention_forward(): value_part = lax.all_gather(values_low, 'blk', axis=0, tiled=True)  97.7 us
    all_gather x2, waiting for transfers between devices, attention_forward(): key_part = lax.all_gather(keys_low, 'blk', axis=0, tiled=True)  91.8 us
  transfers between devices with their start and end apart: 151, of which 144 were waited for; matrix products, arithmetic and copies ran while one was open for 17% of the time, Pallas kernels for 0%

commit v1 on v0

--- a/solution.py
+++ b/solution.py
@@ -1,6 +1,10 @@
+import functools
+
 import jax
 import jax.numpy as jnp
 from jax import lax
+from jax.experimental import pallas as pl
+from jax.experimental.pallas import tpu as pltpu
 from jax.sharding import PartitionSpec as P
 
 HEAD_DIM = 64
@@ -301,7 +305,7 @@
     return (d_inputs, big_grads, small_grads)
 
 
-def local(
+def general(
     tokens,
     grad_out,
     first_rows,
@@ -411,6 +415,954 @@
     )
 
 
+MESH = pl.DeviceIdType.MESH
+LINE = 4
+HALVES = 2
+CHUNK = 32
+TILE = 512
+
+
+def place():
+    k = lax.axis_index("blk")
+    return k // 4, lax.rem(k // 2, 2), lax.rem(k, 2)
+
+
+def index_of(z, y, c):
+    return (z * 2 + y) * 2 + c
+
+
+def device(z, y, c):
+    return {"blk": index_of(z, y, c)}
+
+
+def hail(where):
+    pl.semaphore_signal(pltpu.get_barrier_semaphore(), inc=1, device_id=where, device_id_type=MESH)
+
+
+def greet_neighbours(z, y, c):
+    hail(device(z, y, 1 - c))
+    hail(device(z, 1 - y, c))
+
+    @pl.when(z > 0)
+    def _():
+        hail(device(z - 1, y, c))
+
+    @pl.when(z < LINE - 1)
+    def _():
+        hail(device(z + 1, y, c))
+
+    pl.semaphore_wait(pltpu.get_barrier_semaphore(), 3 + jnp.where((z > 0) & (z < LINE - 1), 1, 0))
+
+
+def remote(src, dst, send, recv, where):
+    return pltpu.make_async_remote_copy(
+        src_ref=src, dst_ref=dst, send_sem=send, recv_sem=recv, device_id=where, device_id_type=MESH
+    )
+
+
+def gather_kernel(x_ref, o_ref, sr, rr, sl, rl, sy, ry, sc, rc, own_sem):
+    z, y, c = place()
+    rows = x_ref.shape[0]
+    half = rows // HALVES
+    greet_neighbours(z, y, c)
+
+    def block(zz, yy, h):
+        return o_ref.at[pl.ds(index_of(zz, yy, c) * rows + h * half, half)]
+
+    def source(zz, yy, h, own):
+        return x_ref.at[pl.ds(h * half, half)] if own else block(zz, yy, h)
+
+    def right(s, h):
+        zz = z - s + 1
+        return remote(source(zz, y, h, s == 1), block(zz, y, h), sr.at[s, h], rr.at[s, h], device(z + 1, y, c))
+
+    def left(s, h):
+        zz = z + s - 1
+        return remote(source(zz, y, h, s == 1), block(zz, y, h), sl.at[s, h], rl.at[s, h], device(z - 1, y, c))
+
+    def across(zz, h, own=False):
+        return remote(source(zz, y, h, own), block(zz, y, h), sy.at[zz, h], ry.at[zz, h], device(z, 1 - y, c))
+
+    def twin(zz, yy, h, own=False):
+        slot = zz * 2 + yy
+        return remote(source(zz, yy, h, own), block(zz, yy, h), sc.at[slot, h], rc.at[slot, h], device(z, y, 1 - c))
+
+    def arrival(ref, send, recv):
+        remote(ref, ref, send, recv, device(z, y, 1 - c)).wait_recv()
+
+    own = pltpu.make_async_copy(x_ref, o_ref.at[pl.ds(index_of(z, y, c) * rows, rows)], own_sem)
+    own.start()
+    for h in range(HALVES):
+
+        @pl.when(z < LINE - 1)
+        def _():
+            right(1, h).start()
+
+        @pl.when(z > 0)
+        def _():
+            left(1, h).start()
+
+        across(z, h, True).start()
+    for h in range(HALVES):
+        twin(z, y, h, True).start()
+
+    def from_line(zz, h, send, recv):
+        arrival(block(zz, y, h), send, recv)
+
+    def pass_on(zz, h):
+        across(zz, h).start()
+        twin(zz, y, h).start()
+
+    def from_across(zz, h):
+        arrival(block(zz, 1 - y, h), sy.at[zz, h], ry.at[zz, h])
+        twin(zz, 1 - y, h).start()
+
+    for s in range(1, LINE):
+        for h in range(HALVES):
+
+            @pl.when(z >= s)
+            def _():
+                from_line(z - s, h, sr.at[s, h], rr.at[s, h])
+                if s < LINE - 1:
+
+                    @pl.when(z < LINE - 1)
+                    def _():
+                        right(s + 1, h).start()
+
+                pass_on(z - s, h)
+
+            @pl.when(z + s <= LINE - 1)
+            def _():
+                from_line(z + s, h, sl.at[s, h], rl.at[s, h])
+                if s < LINE - 1:
+
+                    @pl.when(z > 0)
+                    def _():
+                        left(s + 1, h).start()
+
+                pass_on(z + s, h)
+
+            if s == 1:
+                from_across(z, h)
+            else:
+
+                @pl.when(z >= s - 1)
+                def _():
+                    from_across(z - s + 1, h)
+
+                @pl.when(z + s - 1 <= LINE - 1)
+                def _():
+                    from_across(z + s - 1, h)
+
+    for h in range(HALVES):
+
+        @pl.when(z >= LINE - 1)
+        def _():
+            from_across(z - LINE + 1, h)
+
+        @pl.when(z <= 0)
+        def _():
+            from_across(z + LINE - 1, h)
+
+    own.wait()
+    for h in range(HALVES):
+        for zz in range(LINE):
+            for yy in range(2):
+                slot = zz * 2 + yy
+                rows_there = o_ref.at[pl.ds(index_of(zz, yy, 1 - c) * rows + h * half, half)]
+                arrival(rows_there, sc.at[slot, h], rc.at[slot, h])
+                twin(zz, yy, h).wait_send()
+            across(zz, h).wait_send()
+        for s in range(1, LINE):
+
+            @pl.when((z < LINE - 1) & (z >= s - 1))
+            def _():
+                right(s, h).wait_send()
+
+            @pl.when((z > 0) & (z + s - 1 <= LINE - 1))
+            def _():
+                left(s, h).wait_send()
+
+
+def gather_rows(x, collective_id):
+    rows, columns = x.shape
+    dma = pltpu.SemaphoreType.DMA
+    return pl.pallas_call(
+        gather_kernel,
+        out_shape=jax.ShapeDtypeStruct((4 * LINE * rows, columns), x.dtype),
+        in_specs=[pl.BlockSpec(memory_space=pl.ANY)],
+        out_specs=pl.BlockSpec(memory_space=pl.ANY),
+        scratch_shapes=[dma((LINE, HALVES))] * 6 + [dma((2 * LINE, HALVES))] * 2 + [dma],
+        compiler_params=pltpu.CompilerParams(collective_id=collective_id, has_side_effects=True),
+        name="gather_rows",
+    )(x)
+
+
+def order_at(z, t):
+    table = ((3, 2, 1, 0), (3, 0, 2, 1), (0, 3, 1, 2), (0, 1, 2, 3))
+    low = jnp.where(z == 0, table[0][t], table[1][t])
+    high = jnp.where(z == 2, table[2][t], table[3][t])
+    return jnp.where(z < 2, low, high)
+
+
+def scatter_kernel(p_ref, o_ref, mine, twins, ysend, yrecv, zsend, zright, zleft, sm, sc, rc, sy, ry, sz, rzr, rzl):
+    z, y, c = place()
+    rows = mine.shape[1]
+    half = rows // HALVES
+    greet_neighbours(z, y, c)
+
+    def part(h):
+        return pl.ds(h * half, half)
+
+    def source(t, own_y, cc, h):
+        yy = y if own_y else 1 - y
+        return p_ref.at[pl.ds(index_of(order_at(z, t), yy, cc) * rows + h * half, half)]
+
+    def twin(t, own_y, h):
+        slot = t * 2 + own_y
+        return remote(source(t, own_y, 1 - c, h), twins.at[slot, part(h)], sc.at[slot, h], rc.at[slot, h], device(z, y, 1 - c))
+
+    def local_copy(t, own_y, h):
+        slot = t * 2 + own_y
+        return pltpu.make_async_copy(source(t, own_y, c, h), mine.at[slot, part(h)], sm.at[slot, h])
+
+    def across(t, h):
+        return remote(ysend.at[t, part(h)], yrecv.at[t, part(h)], sy.at[t, h], ry.at[t, h], device(z, 1 - y, c))
+
+    def wide(ref, slot, h):
+        return ref[slot, part(h)].astype(jnp.float32)
+
+    for own_y in (0, 1):
+        for t in range(LINE):
+            for h in range(HALVES):
+                twin(t, own_y, h).start()
+                local_copy(t, own_y, h).start()
+    for t in range(LINE):
+        for h in range(HALVES):
+            twin(t, 0, h).wait_recv()
+            local_copy(t, 0, h).wait()
+            ysend[t, part(h)] = (wide(mine, 2 * t, h) + wide(twins, 2 * t, h)).astype(jnp.bfloat16)
+            across(t, h).start()
+
+    def along(d, t, h, to_right):
+        buf, sem = (zright, rzr) if to_right else (zleft, rzl)
+        where = device(z + 1, y, c) if to_right else device(z - 1, y, c)
+        return remote(zsend.at[t, part(h)], buf.at[d, part(h)], sz.at[t, h], sem.at[d, h], where)
+
+    def arrived(d, h, to_right):
+        buf, sem = (zright, rzr) if to_right else (zleft, rzl)
+        remote(buf.at[d, part(h)], buf.at[d, part(h)], sz.at[0, h], sem.at[d, h], device(z, y, 1 - c)).wait_recv()
+
+    for t in range(LINE):
+        d = order_at(z, t)
+        for h in range(HALVES):
+            twin(t, 1, h).wait_recv()
+            local_copy(t, 1, h).wait()
+            across(t, h).wait_recv()
+
+            def summed(t=t, h=h):
+                return wide(mine, 2 * t + 1, h) + wide(twins, 2 * t + 1, h) + wide(yrecv, t, h)
+
+            if t < LINE - 1:
+                for to_right in (True, False):
+
+                    @pl.when((d > z) if to_right else (d < z))
+                    def _():
+                        first = (z == 0) if to_right else (z == LINE - 1)
+                        buf = zright if to_right else zleft
+
+                        @pl.when(first)
+                        def _():
+                            zsend[t, part(h)] = summed().astype(jnp.bfloat16)
+
+                        @pl.when(jnp.logical_not(first))
+                        def _():
+                            arrived(d, h, to_right)
+                            zsend[t, part(h)] = (summed() + wide(buf, d, h)).astype(jnp.bfloat16)
+
+                        along(d, t, h, to_right).start()
+            else:
+
+                @pl.when(z > 0)
+                def _():
+                    arrived(z, h, True)
+
+                @pl.when(z < LINE - 1)
+                def _():
+                    arrived(z, h, False)
+
+                @pl.when(z == 0)
+                def _():
+                    o_ref[part(h)] = summed() + wide(zleft, z, h)
+
+                @pl.when(z == LINE - 1)
+                def _():
+                    o_ref[part(h)] = summed() + wide(zright, z, h)
+
+                @pl.when((z > 0) & (z < LINE - 1))
+                def _():
+                    o_ref[part(h)] = summed() + wide(zright, z, h) + wide(zleft, z, h)
+
+    for h in range(HALVES):
+        for t in range(LINE):
+            across(t, h).wait_send()
+            twin(t, 0, h).wait_send()
+            twin(t, 1, h).wait_send()
+        for t in range(LINE - 1):
+            along(0, t, h, True).wait_send()
+
+
+def scatter_rows(parts, collective_id):
+    rows, columns = parts.shape[0] // (4 * LINE), parts.shape[1]
+    dma = pltpu.SemaphoreType.DMA
+
+    def blocks(n):
+        return pltpu.VMEM((n, rows, columns), parts.dtype)
+
+    return pl.pallas_call(
+        scatter_kernel,
+        out_shape=jax.ShapeDtypeStruct((rows, columns), jnp.float32),
+        in_specs=[pl.BlockSpec(memory_space=pl.ANY)],
+        out_specs=pl.BlockSpec(memory_space=pltpu.VMEM),
+        scratch_shapes=[blocks(2 * LINE), blocks(2 * LINE), blocks(LINE), blocks(LINE), blocks(LINE - 1), blocks(LINE), blocks(LINE)]
+        + [dma((2 * LINE, HALVES))] * 3
+        + [dma((LINE, HALVES))] * 5,
+        compiler_params=pltpu.CompilerParams(
+            collective_id=collective_id, has_side_effects=True, vmem_limit_bytes=40 << 20
+        ),
+        name="scatter_rows",
+    )(parts)
+
+
+def swap_kernel(x_ref, o_ref, ss, rs, own_sem):
+    k = lax.axis_index("blk")
+    n = x_ref.shape[0]
+
+    def greet(i, carry):
+        hail({"blk": lax.rem(k + i, n)})
+        return carry
+
+    lax.fori_loop(1, n, greet, 0)
+    pl.semaphore_wait(pltpu.get_barrier_semaphore(), n - 1)
+
+    def send(i):
+        to = lax.rem(k + i, n)
+        return remote(x_ref.at[to], o_ref.at[k], ss.at[i], rs.at[i], {"blk": to})
+
+    def receive(i):
+        at = lax.rem(k - i + n, n)
+        return remote(x_ref.at[at], o_ref.at[at], ss.at[i], rs.at[i], {"blk": at})
+
+    def begin(i, carry):
+        send(i).start()
+        return carry
+
+    lax.fori_loop(1, n, begin, 0)
+    own = pltpu.make_async_copy(x_ref.at[k], o_ref.at[k], own_sem)
+    own.start()
+    own.wait()
+
+    def finish(i, carry):
+        receive(i).wait_recv()
+        send(i).wait_send()
+        return carry
+
+    lax.fori_loop(1, n, finish, 0)
+
+
+def swap_blocks(x, collective_id):
+    n = x.shape[0]
+    dma = pltpu.SemaphoreType.DMA
+    return pl.pallas_call(
+        swap_kernel,
+        out_shape=jax.ShapeDtypeStruct(x.shape, x.dtype),
+        in_specs=[pl.BlockSpec(memory_space=pl.ANY)],
+        out_specs=pl.BlockSpec(memory_space=pl.ANY),
+        scratch_shapes=[dma((n,)), dma((n,)), dma],
+        compiler_params=pltpu.CompilerParams(collective_id=collective_id, has_side_effects=True),
+        name="swap_blocks",
+    )(x)
+
+
+def pool_kernel(count, x_ref, o_ref, sent, got, ss, rs):
+    z, y, c = place()
+    hail(device(z, y, 1 - c))
+    hail(device(z, 1 - y, c))
+    for s in range(1, LINE):
+        hail(device(lax.rem(z + s, LINE), y, c))
+    pl.semaphore_wait(pltpu.get_barrier_semaphore(), LINE + 1)
+
+    def pooled(values, share):
+        if count is None:
+            return functools.reduce(jnp.add, values)
+        means = [v[0:1] for v in values]
+        mean = functools.reduce(jnp.add, means) * (1.0 / len(values))
+        squares = functools.reduce(jnp.add, [v[1:2] for v in values])
+        apart = functools.reduce(jnp.add, [(m - mean) * (m - mean) for m in means])
+        return jnp.concatenate([mean, squares + apart * share], axis=0)
+
+    def exchange(slot, where):
+        return remote(sent.at[slot], got.at[slot], ss.at[slot], rs.at[slot], where)
+
+    value = x_ref[...]
+    share = count
+    for stage, where in enumerate((device(z, y, 1 - c), device(z, 1 - y, c))):
+        sent[stage] = value
+        copy = exchange(stage, where)
+        copy.start()
+        copy.wait()
+        value = pooled([value, got[stage]], share)
+        share = None if count is None else 2 * share
+    sent[2] = value
+    copies = []
+    for s in range(1, LINE):
+        where = device(lax.rem(z + s, LINE), y, c)
+        copies.append(remote(sent.at[2], got.at[1 + s], ss.at[1 + s], rs.at[1 + s], where))
+    for copy in copies:
+        copy.start()
+    for copy in copies:
+        copy.wait()
+    o_ref[...] = pooled([value] + [got[1 + s] for s in range(1, LINE)], share)
+
+
+def pool_rows(x, count, collective_id):
+    dma = pltpu.SemaphoreType.DMA
+    return pl.pallas_call(
+        functools.partial(pool_kernel, count),
+        out_shape=jax.ShapeDtypeStruct(x.shape, x.dtype),
+        in_specs=[pl.BlockSpec(memory_space=pltpu.VMEM)],
+        out_specs=pl.BlockSpec(memory_space=pltpu.VMEM),
+        scratch_shapes=[
+            pltpu.VMEM((3,) + x.shape, x.dtype),
+            pltpu.VMEM((LINE + 1,) + x.shape, x.dtype),
+            dma((LINE + 1,)),
+            dma((LINE + 1,)),
+        ],
+        compiler_params=pltpu.CompilerParams(collective_id=collective_id, has_side_effects=True),
+        name="pool_rows",
+    )(x)
+
+
+NN = (((1,), (0,)), ((), ()))
+NT = (((1,), (1,)), ((), ()))
+TN = (((0,), (0,)), ((), ()))
+
+
+def mul(a, b, dims=NN):
+    return lax.dot_general(a, b, dims, preferred_element_type=jnp.float32)
+
+
+def tile_at(t):
+    return pl.ds(pl.multiple_of(t * TILE, TILE), TILE)
+
+
+def chunk_at(index, rows=CHUNK):
+    return pl.ds(pl.multiple_of(index * rows, rows), rows)
+
+
+def diagonal(p):
+    key = lax.broadcasted_iota(jnp.int32, p.shape, 0)
+    query = lax.broadcasted_iota(jnp.int32, p.shape, 1)
+    return key <= query
+
+
+def attend_kernel(table, x_ref, w_ref, b_ref, scale_ref, qvk_ref, lse_ref, out_ref, packed_ref, flat, keys, values_t):
+    total = x_ref.shape[0]
+    tiles = total // TILE
+    chunks = total // CHUNK
+
+    def project(t, carry):
+        flat[tile_at(t)] = (mul(x_ref[tile_at(t)], w_ref[...]) + b_ref[...]).astype(jnp.bfloat16)
+        return carry
+
+    lax.fori_loop(0, tiles, project, 0)
+
+    def arrange(p, carry):
+        qvk_ref[chunk_at(p)] = flat[chunk_at(table[p])]
+        return carry
+
+    lax.fori_loop(0, chunks, arrange, 0)
+
+    def prepare(t, carry):
+        keys[tile_at(t)] = qvk_ref[tile_at(t), 128:192]
+        values_t[:, tile_at(t)] = jnp.transpose(qvk_ref[tile_at(t), 0:128].astype(jnp.float32))[64:128].astype(jnp.bfloat16)
+        return carry
+
+    lax.fori_loop(0, tiles, prepare, 0)
+    cut = table[chunks]
+    for i in range(tiles):
+        at = slice(i * TILE, (i + 1) * TILE)
+        query = qvk_ref[at, 0:64] * 0.125
+
+        def block(j, state, masked):
+            peak, part, mixed = state
+            scores = mul(keys[tile_at(j)], query, NT)
+            if masked:
+                keep = diagonal(scores)
+                scores = jnp.where(keep, scores, -1e30)
+            new_peak = jnp.maximum(peak, jnp.max(scores, axis=0, keepdims=True))
+            weights = jnp.exp(scores - new_peak)
+            if masked:
+                weights = jnp.where(keep, weights, 0.0)
+            factor = jnp.exp(peak - new_peak)
+            part = part * factor + jnp.sum(weights, axis=0, keepdims=True)
+            mixed = mixed * factor + mul(values_t[:, tile_at(j)], weights.astype(jnp.bfloat16))
+            return (new_peak, part, mixed)
+
+        state = (
+            jnp.full((1, TILE), -1e30, jnp.float32),
+            jnp.zeros((1, TILE), jnp.float32),
+            jnp.zeros((64, TILE), jnp.float32),
+        )
+        state = block(i, state, True)
+        state = lax.fori_loop(jnp.where(i >= cut, cut, 0), i, functools.partial(block, masked=False), state)
+        peak, part, mixed = state
+        mixed = mixed / part
+        lse_ref[:, at] = peak + jnp.log(part)
+        out_ref[:, at] = mixed
+        heads_out = jnp.transpose(mixed) * scale_ref[0, 0]
+        pairs = heads_out.reshape(TILE // CHUNK, 2, CHUNK // 2, 64)
+        pairs = jnp.concatenate([pairs[:, 0], pairs[:, 1]], axis=-1).astype(jnp.bfloat16)
+        for q in range(TILE // CHUNK):
+            packed_ref[chunk_at(table[i * (TILE // CHUNK) + q], CHUNK // 2)] = pairs[q]
+
+
+def attend(table, x, w, b, scale):
+    total = x.shape[0]
+    vmem = pl.BlockSpec(memory_space=pltpu.VMEM)
+    smem = pl.BlockSpec(memory_space=pltpu.SMEM)
+    return pl.pallas_call(
+        attend_kernel,
+        out_shape=(
+            jax.ShapeDtypeStruct((total, 192), jnp.bfloat16),
+            jax.ShapeDtypeStruct((1, total), jnp.float32),
+            jax.ShapeDtypeStruct((64, total), jnp.float32),
+            jax.ShapeDtypeStruct((total // 2, 128), jnp.bfloat16),
+        ),
+        in_specs=[smem, vmem, vmem, vmem, smem],
+        out_specs=(vmem, vmem, vmem, vmem),
+        scratch_shapes=[
+            pltpu.VMEM((total, 192), jnp.bfloat16),
+            pltpu.VMEM((total, 64), jnp.bfloat16),
+            pltpu.VMEM((64, total), jnp.bfloat16),
+        ],
+        compiler_params=pltpu.CompilerParams(vmem_limit_bytes=50 << 20),
+        name="attend",
+    )(table, x, w, b, scale)
+
+
+def attend_back_kernel(
+    table, da_ref, x_ref, w_ref, scale_ref, qvk_ref, lse_ref, out_ref,
+    part_ref, gw_ref, gb_ref, gs_ref,
+    packed, dout, delta, query, keys, values, keys_t, dkeys, dvalues, dquery_t, flat,
+):
+    total = x_ref.shape[0]
+    tiles = total // TILE
+    chunks = total // CHUNK
+    per_tile = TILE // CHUNK
+
+    def arrange(p, carry):
+        packed[chunk_at(p, CHUNK // 2)] = da_ref[chunk_at(table[p], CHUNK // 2)]
+        return carry
+
+    lax.fori_loop(0, chunks, arrange, 0)
+    scale = scale_ref[0, 0]
+
+    def prepare(t, carry):
+        at = tile_at(t)
+        pairs = packed[chunk_at(t, TILE // 2)].astype(jnp.float32).reshape(per_tile, CHUNK // 2, 128)
+        pairs = jnp.concatenate([pairs[:, :, 0:64], pairs[:, :, 64:128]], axis=1).reshape(TILE, 64)
+        low = (pairs * scale).astype(jnp.bfloat16)
+        dout[at] = low
+        delta[:, at] = jnp.sum(jnp.transpose(low.astype(jnp.float32)) * out_ref[:, at], axis=0, keepdims=True)
+        query[at] = qvk_ref[at, 0:64] * 0.125
+        values[at] = qvk_ref[at, 64:128]
+        key = qvk_ref[at, 128:192]
+        keys[at] = key
+        keys_t[:, at] = jnp.transpose(key.astype(jnp.float32)).astype(jnp.bfloat16)
+        dkeys[at] = jnp.zeros((TILE, 64), jnp.float32)
+        dvalues[at] = jnp.zeros((TILE, 64), jnp.float32)
+        return carry
+
+    lax.fori_loop(0, tiles, prepare, 0)
+    gs_ref[...] = jnp.sum(delta[...], axis=1, keepdims=True) / scale
+    cut = table[chunks]
+    for i in range(tiles):
+        at = slice(i * TILE, (i + 1) * TILE)
+        query_i, dout_i, lse_i, delta_i = query[at], dout[at], lse_ref[:, at], delta[:, at]
+
+        def block(j, total_dq, masked):
+            there = tile_at(j)
+            scores = mul(keys[there], query_i, NT)
+            weights = jnp.exp(scores - lse_i)
+            if masked:
+                weights = jnp.where(diagonal(scores), weights, 0.0)
+            dweights = mul(values[there], dout_i, NT)
+            dscores = (weights * (dweights - delta_i)).astype(jnp.bfloat16)
+            dvalues[there] += mul(weights.astype(jnp.bfloat16), dout_i)
+            dkeys[there] += mul(dscores, query_i)
+            return total_dq + mul(keys_t[:, there], dscores)
+
+        total_dq = block(i, jnp.zeros((64, TILE), jnp.float32), True)
+        total_dq = lax.fori_loop(jnp.where(i >= cut, cut, 0), i, functools.partial(block, masked=False), total_dq)
+        dquery_t[:, at] = total_dq * 0.125
+
+    gb_ref[...] = jnp.zeros_like(gb_ref)
+    for i in range(tiles):
+        at = slice(i * TILE, (i + 1) * TILE)
+        joined = jnp.concatenate([jnp.transpose(dquery_t[:, at]), dvalues[at], dkeys[at]], axis=1).astype(jnp.bfloat16)
+        gb_ref[...] += jnp.sum(joined.astype(jnp.float32), axis=0, keepdims=True)
+        for q in range(per_tile):
+            flat[chunk_at(table[i * per_tile + q])] = joined[q * CHUNK : (q + 1) * CHUNK]
+    gw_ref[...] = jnp.zeros_like(gw_ref)
+
+    def finish(t, carry):
+        rows = flat[tile_at(t)]
+        part_ref[tile_at(t)] = mul(rows, w_ref[...], NT).astype(jnp.bfloat16)
+        gw_ref[...] += mul(rows, x_ref[tile_at(t)], TN)
+        return carry
+
+    lax.fori_loop(0, tiles, finish, 0)
+
+
+def attend_back(table, da, x, w, scale, qvk, lse, out):
+    total, width = x.shape
+    vmem = pl.BlockSpec(memory_space=pltpu.VMEM)
+    smem = pl.BlockSpec(memory_space=pltpu.SMEM)
+    low = lambda *shape: pltpu.VMEM(shape, jnp.bfloat16)
+    full = lambda *shape: pltpu.VMEM(shape, jnp.float32)
+    return pl.pallas_call(
+        attend_back_kernel,
+        out_shape=(
+            jax.ShapeDtypeStruct((total, width), jnp.bfloat16),
+            jax.ShapeDtypeStruct((192, width), jnp.float32),
+            jax.ShapeDtypeStruct((1, 192), jnp.float32),
+            jax.ShapeDtypeStruct((1, 1), jnp.float32),
+        ),
+        in_specs=[smem, vmem, vmem, vmem, smem, vmem, vmem, vmem],
+        out_specs=(vmem, vmem, vmem, vmem),
+        scratch_shapes=[
+            low(total // 2, 128), low(total, 64), full(1, total), low(total, 64), low(total, 64), low(total, 64),
+            low(64, total), full(total, 64), full(total, 64), full(64, total), low(total, 192),
+        ],
+        compiler_params=pltpu.CompilerParams(vmem_limit_bytes=56 << 20),
+        name="attend_back",
+    )(table, da, x, w, scale, qvk, lse, out)
+
+
+def up_kernel(x_ref, w_ref, b_ref, act_ref, slope_ref, stat_ref):
+    def step(t, carry):
+        at = tile_at(t)
+        upper = mul(w_ref[...], x_ref[at], NT) + b_ref[...]
+        chance = 0.5 * (1.0 + lax.erf(upper * (0.5**0.5)))
+        act = upper * chance
+        act_ref[:, at] = act
+        slope_ref[:, at] = chance + upper * (jnp.exp(-0.5 * upper * upper) * 0.3989422804014327)
+        mean = jnp.mean(act, axis=0, keepdims=True)
+        apart = act - mean
+        stat_ref[0:1, at] = mean
+        stat_ref[1:2, at] = jnp.sum(apart * apart, axis=0, keepdims=True)
+        return carry
+
+    lax.fori_loop(0, x_ref.shape[0] // TILE, step, 0)
+
+
+def up(x, w, b):
+    total, hidden = x.shape[0], w.shape[0]
+    vmem = pl.BlockSpec(memory_space=pltpu.VMEM)
+    return pl.pallas_call(
+        up_kernel,
+        out_shape=(
+            jax.ShapeDtypeStruct((hidden, total), jnp.float32),
+            jax.ShapeDtypeStruct((hidden, total), jnp.float32),
+            jax.ShapeDtypeStruct((2, total), jnp.float32),
+        ),
+        in_specs=[vmem] * 3,
+        out_specs=(vmem,) * 3,
+        compiler_params=pltpu.CompilerParams(vmem_limit_bytes=50 << 20),
+        name="up",
+    )(x, w, b)
+
+
+def centred(act, stat, hidden_all):
+    return (act - stat[0:1]) * lax.rsqrt(stat[1:2] * (1.0 / hidden_all) + EPSILON)
+
+
+def down_kernel(hidden_all, act_ref, stat_ref, gain_ref, shift_ref, w_ref, part_ref, mid_ref):
+    def step(t, carry):
+        at = tile_at(t)
+        vh = centred(act_ref[:, at], stat_ref[:, at], hidden_all)
+        low = (vh * gain_ref[...] + shift_ref[...]).astype(jnp.bfloat16)
+        mid_ref[:, at] = low
+        part_ref[at] = mul(low, w_ref[...], TN).astype(jnp.bfloat16)
+        return carry
+
+    lax.fori_loop(0, act_ref.shape[1] // TILE, step, 0)
+
+
+def down(hidden_all, act, stat, gain, shift, w):
+    hidden, total = act.shape
+    vmem = pl.BlockSpec(memory_space=pltpu.VMEM)
+    return pl.pallas_call(
+        functools.partial(down_kernel, hidden_all),
+        out_shape=(
+            jax.ShapeDtypeStruct((total, w.shape[1]), jnp.bfloat16),
+            jax.ShapeDtypeStruct((hidden, total), jnp.bfloat16),
+        ),
+        in_specs=[vmem] * 5,
+        out_specs=(vmem,) * 2,
+        compiler_params=pltpu.CompilerParams(vmem_limit_bytes=50 << 20),
+        name="down",
+    )(act, stat, gain, shift, w)
+
+
+def down_back_kernel(hidden_all, dy_ref, w_ref, act_ref, stat_ref, gain_ref, mid_ref, dmid_ref, sums_ref, gw_ref, gg_ref, gs_ref):
+    gw_ref[...] = jnp.zeros_like(gw_ref)
+    gg_ref[...] = jnp.zeros_like(gg_ref)
+    gs_ref[...] = jnp.zeros_like(gs_ref)
+
+    def step(t, carry):
+        at = tile_at(t)
+        dmid = mul(w_ref[...], dy_ref[at], NT)
+        dmid_ref[:, at] = dmid
+        vh = centred(act_ref[:, at], stat_ref[:, at], hidden_all)
+        gg_ref[...] += jnp.sum(dmid * vh, axis=1, keepdims=True)
+        gs_ref[...] += jnp.sum(dmid, axis=1, keepdims=True)
+        scaled = dmid * gain_ref[...]
+        sums_ref[0:1, at] = jnp.sum(scaled, axis=0, keepdims=True)
+        sums_ref[1:2, at] = jnp.sum(scaled * vh, axis=0, keepdims=True)
+        gw_ref[...] += mul(mid_ref[:, at], dy_ref[at])
+        return carry
+
+    lax.fori_loop(0, act_ref.shape[1] // TILE, step, 0)
+
+
+def down_back(hidden_all, dy, w, act, stat, gain, mid):
+    hidden, total = act.shape
+    vmem = pl.BlockSpec(memory_space=pltpu.VMEM)
+    return pl.pallas_call(
+        functools.partial(down_back_kernel, hidden_all),
+        out_shape=(
+            jax.ShapeDtypeStruct((hidden, total), jnp.float32),
+            jax.ShapeDtypeStruct((2, total), jnp.float32),
+            jax.ShapeDtypeStruct(w.shape, jnp.float32),
+            jax.ShapeDtypeStruct((hidden, 1), jnp.float32),
+            jax.ShapeDtypeStruct((hidden, 1), jnp.float32),
+        ),
+        in_specs=[vmem] * 6,
+        out_specs=(vmem,) * 5,
+        compiler_params=pltpu.CompilerParams(vmem_limit_bytes=50 << 20),
+        name="down_back",
+    )(dy, w, act, stat, gain, mid)
+
+
+def up_back_kernel(hidden_all, dmid_ref, act_ref, slope_ref, stat_ref, sums_ref, gain_ref, x_ref, w_ref, part_ref, gw_ref, gb_ref):
+    gw_ref[...] = jnp.zeros_like(gw_ref)
+    gb_ref[...] = jnp.zeros_like(gb_ref)
+
+    def step(t, carry):
+        at = tile_at(t)
+        stat = stat_ref[:, at]
+        vh = centred(act_ref[:, at], stat, hidden_all)
+        rate = lax.rsqrt(stat[1:2] * (1.0 / hidden_all) + EPSILON)
+        sums = sums_ref[:, at] * (1.0 / hidden_all)
+        dact = rate * (dmid_ref[:, at] * gain_ref[...] - sums[0:1] - vh * sums[1:2])
+        low = (dact * slope_ref[:, at]).astype(jnp.bfloat16)
+        gb_ref[...] += jnp.sum(low.astype(jnp.float32), axis=1, keepdims=True)
+        gw_ref[...] += mul(low, x_ref[at])
+        part_ref[at] = mul(low, w_ref[...], TN).astype(jnp.bfloat16)
+        return carry
+
+    lax.fori_loop(0, act_ref.shape[1] // TILE, step, 0)
+
+
+def up_back(hidden_all, dmid, act, slope, stat, sums, gain, x, w):
+    hidden, total = act.shape
+    vmem = pl.BlockSpec(memory_space=pltpu.VMEM)
+    return pl.pallas_call(
+        functools.partial(up_back_kernel, hidden_all),
+        out_shape=(
+            jax.ShapeDtypeStruct((total, w.shape[1]), jnp.bfloat16),
+            jax.ShapeDtypeStruct(w.shape, jnp.float32),
+            jax.ShapeDtypeStruct((hidden, 1), jnp.float32),
+        ),
+        in_specs=[vmem] * 8,
+        out_specs=(vmem,) * 3,
+        compiler_params=pltpu.CompilerParams(vmem_limit_bytes=56 << 20),
+        name="up_back",
+    )(dmid, act, slope, stat, sums, gain, x, w)
+
+
+def chunk_table(first_rows, span_of, rows_here):
+    blocks = span_of.shape[0]
+    device_of = jnp.zeros((blocks,), jnp.int32).at[span_of].set(jnp.arange(blocks, dtype=jnp.int32))
+    first = first_rows[0]
+    second = rows_here - first
+    row = jnp.arange(blocks * rows_here // CHUNK, dtype=jnp.int32) * CHUNK
+    later = row >= first * blocks
+    inside = jnp.where(later, row - first * blocks, row)
+    length = jnp.where(later, jnp.maximum(second, 1), first)
+    span = jnp.minimum(inside // length, blocks - 1)
+    source = device_of[span] * rows_here + jnp.where(later, first, 0) + inside - span * length
+    return jnp.concatenate([source // CHUNK, (first * blocks // TILE)[None]]).astype(jnp.int32)
+
+
+def pack_rows(matrix):
+    rows = matrix.shape[0]
+    split = matrix.reshape(rows // CHUNK, 2, CHUNK // 2, -1, HEAD_DIM)
+    return split.transpose(3, 0, 2, 1, 4).reshape(-1, rows // 2, 2 * HEAD_DIM)
+
+
+def unpack_rows(blocks):
+    heads, half_rows, _ = blocks.shape
+    split = blocks.reshape(heads, half_rows // (CHUNK // 2), CHUNK // 2, 2, HEAD_DIM)
+    return split.transpose(1, 3, 2, 0, 4).reshape(2 * half_rows, heads * HEAD_DIM)
+
+
+def own_share(vector, index, size):
+    return lax.dynamic_slice_in_dim(vector, index * size, size, 0)
+
+
+def spread(vector, index, whole):
+    return lax.dynamic_update_slice_in_dim(jnp.zeros((whole,), jnp.float32), vector, index * vector.shape[0], 0)
+
+
+def exchange_weights(w_qkv, w_up, blocks):
+    layers, rows, _ = w_qkv.shape
+    width = rows * blocks
+    by_head = w_qkv.reshape(layers, rows, 3, blocks, HEAD_DIM).transpose(3, 1, 0, 2, 4)
+    by_head = by_head[:, :, :, jnp.array([0, 2, 1])].reshape(blocks, rows, -1)
+    by_unit = w_up.reshape(layers, rows, blocks, -1).transpose(2, 1, 0, 3).reshape(blocks, rows, -1)
+    by_head = swap_blocks(by_head, 2).reshape(width, layers, -1)
+    by_unit = lax.all_to_all(by_unit, "blk", 0, 0, tiled=True).reshape(width, layers, -1)
+    return by_head.transpose(1, 0, 2), by_unit.transpose(1, 2, 0)
+
+
+def travel(
+    tokens, grad_out, first_rows, span_of, w_qkv, w_out, w_up, w_down, vec_gain, vec_bias, mid_gain, mid_bias, head_scale
+):
+    blocks = lax.axis_size("blk")
+    rows_here, row_width = tokens.shape
+    index = lax.axis_index("blk")
+    hidden_all = mid_gain.shape[1]
+    hidden = hidden_all // blocks
+    table = chunk_table(first_rows, span_of, rows_here)
+    head_w, unit_w = exchange_weights(w_qkv, w_up, blocks)
+    out_w = [lax.all_gather(w_out[layer], "blk", axis=0, tiled=True) for layer in range(2)]
+    scales = [own_share(head_scale[layer], index, 1).reshape(1, 1) for layer in range(2)]
+    middle_gain = [own_share(mid_gain[layer], index, hidden)[:, None] for layer in range(2)]
+    middle_shift = [own_share(mid_bias[layer, 0], index, hidden)[:, None] for layer in range(2)]
+    middle_bias = [own_share(mid_bias[layer, 1], index, hidden)[:, None] for layer in range(2)]
+    current = tokens.astype(jnp.float32)
+    records = []
+    for layer in range(2):
+        gains, biases = vec_gain[layer], vec_bias[layer]
+        normed, pre_pull = jax.vjp(norm_rows, current, gains[0], biases[0])
+        normed_all = gather_rows(normed.astype(jnp.bfloat16), 0)
+        head_bias = jnp.concatenate(
+            [
+                own_share(biases[3], index, HEAD_DIM),
+                own_share(biases[4], index, HEAD_DIM),
+                jnp.zeros((HEAD_DIM,), jnp.float32),
+            ]
+        )[None]
+        qvk, lse, head_out, packed = attend(table, normed_all, head_w[layer], head_bias, scales[layer])
+        scaled_low = unpack_rows(swap_blocks(packed.reshape(blocks, rows_here // 2, 128), 3))
+        branch = jnp.dot(scaled_low, out_w[layer], preferred_element_type=jnp.float32) + biases[5]
+        post_normed, post_pull = jax.vjp(norm_rows, branch, gains[1], biases[1])
+        middle_res = current + post_normed
+        ffn_normed, ffn_pull = jax.vjp(norm_rows, middle_res, gains[2], biases[2])
+        ffn_all = gather_rows(ffn_normed.astype(jnp.bfloat16), 0)
+        act, slope, stat = up(ffn_all, unit_w[layer], middle_bias[layer])
+        stat = pool_rows(stat, hidden, 4)
+        parts, mid_low = down(hidden_all, act, stat, middle_gain[layer], middle_shift[layer], w_down[layer])
+        current = middle_res + (scatter_rows(parts, 1) + biases[6])
+        records.append(
+            (pre_pull, post_pull, ffn_pull, normed_all, ffn_all, qvk, lse, head_out, scaled_low, act, slope, stat, mid_low)
+        )
+    results_low = current.astype(jnp.bfloat16)
+    d_current = grad_out.astype(jnp.float32)
+    head_grads, unit_grads, out_grads, down_grads = [None] * 2, [None] * 2, [None] * 2, [None] * 2
+    small = [None] * 2
+    for layer in (1, 0):
+        pre_pull, post_pull, ffn_pull, normed_all, ffn_all, qvk, lse, head_out, scaled_low, act, slope, stat, mid_low = records[layer]
+        d_low = d_current.astype(jnp.bfloat16)
+        d_all = gather_rows(d_low, 0)
+        dmid, sums, down_grads[layer], grad_mid_gain, grad_mid_shift = down_back(
+            hidden_all, d_all, w_down[layer], act, stat, middle_gain[layer], mid_low
+        )
+        sums = pool_rows(sums, None, 5)
+        parts, unit_grads[layer], grad_up_bias = up_back(
+            hidden_all, dmid, act, slope, stat, sums, middle_gain[layer], ffn_all, unit_w[layer]
+        )
+        d_res_part, grad_gain_ffn, grad_shift_ffn = ffn_pull(scatter_rows(parts, 1))
+        d_middle_res = d_current + d_res_part
+        d_branch, grad_gain_post, grad_shift_post = post_pull(d_middle_res)
+        d_branch_low = d_branch.astype(jnp.bfloat16)
+        d_scaled = jnp.einsum("td,cd->tc", d_branch_low, out_w[layer], preferred_element_type=jnp.float32)
+        out_grad = jnp.einsum("tc,td->cd", scaled_low, d_branch_low, preferred_element_type=jnp.float32)
+        out_grads[layer] = lax.psum_scatter(out_grad.astype(jnp.bfloat16), "blk", scatter_dimension=0, tiled=True)
+        d_heads = swap_blocks(pack_rows(d_scaled.astype(jnp.bfloat16)), 3).reshape(-1, 128)
+        parts, head_grads[layer], head_bias, grad_scale = attend_back(
+            table, d_heads, normed_all, head_w[layer], scales[layer], qvk, lse, head_out
+        )
+        d_in_part, grad_gain_pre, grad_shift_pre = pre_pull(scatter_rows(parts, 1))
+        d_current = d_middle_res + d_in_part
+        small[layer] = jnp.concatenate(
+            [
+                grad_gain_pre,
+                grad_gain_post,
+                grad_gain_ffn,
+                grad_shift_pre,
+                grad_shift_post,
+                grad_shift_ffn,
+                spread(head_bias[0, :HEAD_DIM], index, row_width),
+                spread(head_bias[0, HEAD_DIM : 2 * HEAD_DIM], index, row_width),
+                jnp.sum(d_branch_low, axis=0, dtype=jnp.float32),
+                jnp.sum(d_low, axis=0, dtype=jnp.float32),
+                spread(grad_mid_gain[:, 0], index, hidden_all),
+                spread(grad_mid_shift[:, 0], index, hidden_all),
+                spread(grad_up_bias[:, 0], index, hidden_all),
+                spread(grad_scale[0], index, blocks),
+            ]
+        )
+    small = lax.psum(jnp.stack(small), ("batch", "blk"))
+    turned = [jnp.concatenate([head_grads[layer], unit_grads[layer]], axis=0).astype(jnp.bfloat16) for layer in range(2)]
+    turned = lax.psum(jnp.stack(turned), "batch")
+    turned = turned.reshape(2, -1, blocks, row_width // blocks).transpose(2, 0, 3, 1)
+    turned = lax.all_to_all(turned, "blk", 0, 0, tiled=True).astype(jnp.float32)
+    heads_back = turned[..., : 3 * HEAD_DIM].reshape(blocks, 2, -1, 3, HEAD_DIM)[:, :, :, jnp.array([0, 2, 1])]
+    grad_qkv = heads_back.transpose(1, 2, 3, 0, 4).reshape(w_qkv.shape)
+    grad_up = turned[..., 3 * HEAD_DIM :].transpose(1, 2, 0, 3).reshape(w_up.shape)
+    grad_out_w = lax.psum(jnp.stack(out_grads), "batch").astype(jnp.float32)
+    grad_down = lax.psum(jnp.stack(down_grads).astype(jnp.bfloat16), "batch").astype(jnp.float32)
+    vec_end = 10 * row_width
+    vectors = small[:, :vec_end].reshape(2, 10, row_width)
+    middles = small[:, vec_end : vec_end + 3 * hidden_all].reshape(2, 3, hidden_all)
+    return (
+        results_low,
+        d_current,
+        grad_qkv,
+        grad_out_w,
+        grad_up,
+        grad_down,
+        vectors[:, :3],
+        vectors[:, 3:],
+        middles[:, 0],
+        middles[:, 1:],
+        small[:, vec_end + 3 * hidden_all :],
+    )
+
+
+def local(*args):
+    tokens, w_qkv = args[0], args[4]
+    blocks = lax.axis_size("blk")
+    heads = w_qkv.shape[2] // (3 * HEAD_DIM)
+    if blocks == heads and blocks == 4 * LINE and tokens.shape[0] * blocks % TILE == 0:
+        return travel(*args)
+    return general(*args)
+
+
 def solution(mesh):
     placed = (
         P(("batch", "blk"), None),

time: 3370 us -> 1180 us (0.35)
  waiting for transfers between devices: 1930 us -> 268 us
  Pallas kernels: 0 us -> 707 us
  other arithmetic: 595 us -> 35.2 us
  matrix products: 313 us -> 12.4 us
  local copies, waits for them, and re-layouts: 311 us -> 119 us
  loops' own time: 104 us -> 0 us
  starting transfers between devices: 83.4 us -> 13.5 us
    pallas_call x0 -> x33, Pallas kernels: none -> 707 us  [the longest x6 233 us: gather_rows(): pl.pallas_call(gather_kernel, out_shape=jax.ShapeDtypeStruct((4 * LINE *...]
    reduce_scatter x8 -> x2, waiting for transfers between devices: 737 us -> 36.7 us  [travel(): lax.psum_scatter(out_grad.astype(jnp.bfloat16), 'blk', scatter_dimension=...]
    ppermute x128 -> x0, waiting for transfers between devices: 677 us -> none  [shifted(): lax.ppermute(x, axis, [(i, (i + by) % devices) for i in range(devices)])]
    all_gather x12 -> x2, waiting for transfers between devices: 373 us -> 0.04 us  [travel(): lax.all_gather(w_out[layer], 'blk', axis=0, tiled=True)]
    dot_general x160 -> x6, matrix products: 313 us -> 12.4 us  [the longest x2 5.01 us: travel(): jnp.dot(scaled_low, out_w[layer], preferred_element_type=jnp.float32)]
    convert_element_type x137 -> x7, other arithmetic: 224 us -> 9.18 us  [the longest x1 3.05 us: travel(): turned = lax.all_to_all(turned, 'blk', 0, 0, tiled=True).astype(jnp.float32)]
    another operation x44 -> x0, loops' own time: 104 us -> none  [the longest x32 55.3 us: turn(): lax.cond(source_span <= my_span, turn_compute, unchanged, (dquery, dkeys,...]
    psum x3 -> x2, waiting for transfers between devices: 137 us -> 231 us  [the longest x1 142 us: travel(): small = lax.psum(jnp.stack(small), ('batch', 'blk'))]
  transfers between devices with their start and end apart: 151 -> 8, of which waited for: 144 -> 3; matrix products, arithmetic and copies ran while one was open for 17% -> 7% of each run, Pallas kernels for 0% -> 32%
where the time goes in v1:
time: 1180 us; the launch traced here: 1170 us
  Pallas kernels  707 us (60%)
  waiting for transfers between devices  268 us (23%)
  local copies, waits for them, and re-layouts  119 us (10%)
  other arithmetic  35.2 us (3%)
  between operations  17.1 us (1%)
  starting transfers between devices  13.5 us (1%)
  matrix products  12.4 us (1%)
    pallas_call x6, Pallas kernels, gather_rows(): pl.pallas_call(gather_kernel, out_shape=jax.ShapeDtypeStruct((4 * LINE *...  233 us
    pallas_call x6, Pallas kernels, scatter_rows(): pl.pallas_call(scatter_kernel, out_shape=jax.ShapeDtypeStruct((rows, colu...  214 us
    psum x1, waiting for transfers between devices, travel(): small = lax.psum(jnp.stack(small), ('batch', 'blk'))  142 us
    psum x1, waiting for transfers between devices, travel(): turned = lax.psum(jnp.stack(turned), 'batch')  89 us
    pallas_call x5, Pallas kernels, swap_blocks(): pl.pallas_call(swap_kernel, out_shape=jax.ShapeDtypeStruct(x.shape, x.dty...  64.2 us
    pallas_call x2, Pallas kernels, attend_back(): pl.pallas_call(attend_back_kernel, out_shape=(jax.ShapeDtypeStruct((total...  49.2 us
    pallas_call x4, Pallas kernels, pool_rows(): pl.pallas_call(functools.partial(pool_kernel, count), out_shape=jax.Shape...  44.2 us
    unnamed x228, local copies, waits for them, and re-layouts  39 us
  transfers between devices with their start and end apart: 8, of which 3 were waited for; matrix products, arithmetic and copies ran while one was open for 7% of the time, Pallas kernels for 32%

profile of v1, /device:TPU:0, one launch (start us, length us, event | category | flops | bytes accessed | tf_op | source)
XLA Modules:
  0.0 1172.7 jit_solution(15700326305754283144)
XLA Ops:
  13.1 7.4 all-to-all-start
  24.9 62.5 %gather_rows.6.x_ref = bf16[2560,1024]{1,0:T(8,128)(2,1)} custom-call(bf16[160,1024]{1,0:T(8,128)(2,1)} %fusion.27.x_ref), custom_call_target="tpu_custom_call" | custom-call | tf_op jit(solution)/shard_map/gather_rows/pallas_call | solution.py:590
  93.1 2.8 copy.80
  98.4 17.9 %swap_blocks.5 = bf16[16,64,384]{2,1,0:T(8,128)(2,1)} custom-call(bf16[16,64,384]{2,1,0:T(8,128)(2,1)} %reshape.457.x_ref), custom_call_target="tpu_custom_call" | custom-call | tf_op jit(solution)/shard_map/swap_blocks/pallas_call | solution.py:776
  116.3 3.1 reshape.458
  120.4 10.3 and_select_fusion
  131.6 16.4 %attend.2 = (bf16[2560,192]{1,0:T(8,128)(2,1)S(1)}, f32[1,2560]{1,0:T(1,128)S(1)}, f32[64,2560]{1,0:T(8,128)S(1)}, bf16[1280,128]{1,0:T(8,128)(2,1)S(1)}) custom-call(s32[81]{0:T(128)S(1)} %pad_add_fusion.table, bf16[2560,1024]{1,0:T(8,128)(2,1)} %gather_rows.6.x_ref, bf16[1024,192]{1,0:T(8,128)(2,1)S(1)} %get-tuple-element.179.w_ref, ...), custom_call_target="tpu_custom_call" | custom-call | tf_op jit(solution)/shard_map/attend/pallas_call | solution.py:934
  151.3 15.1 %swap_blocks.6 = bf16[16,80,128]{2,1,0:T(8,128)(2,1)} custom-call(bf16[16,80,128]{2,1,0:T(8,128)(2,1)} %bitcast.277), custom_call_target="tpu_custom_call" | custom-call | tf_op jit(solution)/shard_map/swap_blocks/pallas_call | solution.py:776
  170.2 36.1 %gather_rows.10.dy_ref = bf16[2560,1024]{1,0:T(8,128)(2,1)} custom-call(bf16[160,1024]{1,0:T(8,128)(2,1)} %x_ref), custom_call_target="tpu_custom_call" | custom-call | tf_op jit(solution)/shard_map/gather_rows/pallas_call | solution.py:590
  217.2 33.5 %gather_rows.7.x_ref = bf16[2560,1024]{1,0:T(8,128)(2,1)} custom-call(bf16[160,1024]{1,0:T(8,128)(2,1)} %add_convert_fusion.5.x_ref), custom_call_target="tpu_custom_call" | custom-call | tf_op jit(solution)/shard_map/gather_rows/pallas_call | solution.py:590
  250.8 7.5 up.2
  260.4 11.1 pool_rows.4.stat_ref
  272.3 7.1 down.2
  279.4 3.0 copy-done.6
  282.3 34.5 %scatter_rows.6 = f32[160,1024]{1,0:T(8,128)S(1)} custom-call(bf16[2560,1024]{1,0:T(8,128)(2,1)S(1)} %copy-done.6), custom_call_target="tpu_custom_call" | custom-call | tf_op jit(solution)/shard_map/scatter_rows/pallas_call | solution.py:722
  318.8 33.3 %gather_rows.8.x_ref = bf16[2560,1024]{1,0:T(8,128)(2,1)} custom-call(bf16[160,1024]{1,0:T(8,128)(2,1)} %add_convert_fusion.4.x_ref), custom_call_target="tpu_custom_call" | custom-call | tf_op jit(solution)/shard_map/gather_rows/pallas_call | solution.py:590
  352.1 16.2 %attend.3 = (bf16[2560,192]{1,0:T(8,128)(2,1)S(1)}, f32[1,2560]{1,0:T(1,128)S(1)}, f32[64,2560]{1,0:T(8,128)S(1)}, bf16[1280,128]{1,0:T(8,128)(2,1)S(1)}) custom-call(s32[81]{0:T(128)S(1)} %pad_add_fusion.table, bf16[2560,1024]{1,0:T(8,128)(2,1)} %gather_rows.8.x_ref, bf16[1024,192]{1,0:T(8,128)(2,1)S(1)} %copy-done.10, f32[1,192]{1,0:T(1,128)S(1)} %bitcast.279, ...), custom_call_target="tpu_custom_call" | custom-call | tf_op jit(solution)/shard_map/attend/pallas_call | solution.py:934
  371.5 10.3 swap_blocks.7
  390.8 34.9 %gather_rows.9.x_ref = bf16[2560,1024]{1,0:T(8,128)(2,1)} custom-call(bf16[160,1024]{1,0:T(8,128)(2,1)} %add_convert_fusion.3.x_ref), custom_call_target="tpu_custom_call" | custom-call | tf_op jit(solution)/shard_map/gather_rows/pallas_call | solution.py:590
  425.7 7.6 up.3
  435.4 10.8 pool_rows.5.stat_ref
  446.9 7.0 down.3
  453.9 8.9 down_back.2
  464.4 11.1 pool_rows.6.sums_ref
  475.5 11.7 up_back.2
  489.7 34.9 %scatter_rows.8 = f32[160,1024]{1,0:T(8,128)S(1)} custom-call(bf16[2560,1024]{1,0:T(8,128)(2,1)S(1)} %copy-done.3), custom_call_target="tpu_custom_call" | custom-call | tf_op jit(solution)/shard_map/scatter_rows/pallas_call | solution.py:722
  525.0 35.1 %scatter_rows.7 = f32[160,1024]{1,0:T(8,128)S(1)} custom-call(bf16[2560,1024]{1,0:T(8,128)(2,1)S(1)} %bitcast.276), custom_call_target="tpu_custom_call" | custom-call | tf_op jit(solution)/shard_map/scatter_rows/pallas_call | solution.py:722
  568.0 10.4 swap_blocks.8
  578.5 24.6 %attend_back.2 = (bf16[2560,1024]{1,0:T(8,128)(2,1)}, f32[192,1024]{1,0:T(8,128)}, f32[1,192]{1,0:T(1,128)}, f32[1,1]{1,0:T(1,128)}) custom-call(s32[81]{0:T(128)} %copy-done.34, bf16[1280,128]{1,0:T(8,128)(2,1)} %bitcast.294, bf16[2560,1024]{1,0:T(8,128)(2,1)} %gather_rows.8.x_ref, bf16[1024,192]{1,0:T(8,128)(2,1)} %get-tuple-element.178.w_ref, ...), custom_call_target="tpu_custom_call" | custom-call | tf_op jit(solution)/shard_map/attend_back/pallas_call | solution.py:1034
  605.6 37.4 %scatter_rows.9 = f32[160,1024]{1,0:T(8,128)S(1)} custom-call(bf16[2560,1024]{1,0:T(8,128)(2,1)S(1)} %copy-done.4), custom_call_target="tpu_custom_call" | custom-call | tf_op jit(solution)/shard_map/scatter_rows/pallas_call | solution.py:722
  644.6 32.5 %gather_rows.11.dy_ref = bf16[2560,1024]{1,0:T(8,128)(2,1)} custom-call(bf16[160,1024]{1,0:T(8,128)(2,1)} %get-tuple-element.151.x_ref), custom_call_target="tpu_custom_call" | custom-call | tf_op jit(solution)/shard_map/gather_rows/pallas_call | solution.py:590
  677.1 8.8 down_back.3
  687.6 11.2 pool_rows.7.sums_ref
  698.8 11.7 up_back.3
  713.0 35.1 %scatter_rows.10 = f32[160,1024]{1,0:T(8,128)S(1)} custom-call(bf16[2560,1024]{1,0:T(8,128)(2,1)S(1)} %copy-done.5), custom_call_target="tpu_custom_call" | custom-call | tf_op jit(solution)/shard_map/scatter_rows/pallas_call | solution.py:722
  760.3 10.4 swap_blocks.9
  770.7 24.6 %attend_back.3 = (bf16[2560,1024]{1,0:T(8,128)(2,1)}, f32[192,1024]{1,0:T(8,128)}, f32[1,192]{1,0:T(1,128)}, f32[1,1]{1,0:T(1,128)}) custom-call(s32[81]{0:T(128)} %copy-done.34, bf16[1280,128]{1,0:T(8,128)(2,1)} %bitcast.293, bf16[2560,1024]{1,0:T(8,128)(2,1)} %gather_rows.6.x_ref, bf16[1024,192]{1,0:T(8,128)(2,1)} %copy-done.9, ...), custom_call_target="tpu_custom_call" | custom-call | tf_op jit(solution)/shard_map/attend_back/pallas_call | solution.py:1034
  797.8 37.0 %scatter_rows.11 = f32[160,1024]{1,0:T(8,128)S(1)} custom-call(bf16[2560,1024]{1,0:T(8,128)(2,1)S(1)} %copy-done.2), custom_call_target="tpu_custom_call" | custom-call | tf_op jit(solution)/shard_map/scatter_rows/pallas_call | solution.py:722
  837.9 4.0 copy.98
  844.2 36.7 %reduce-scatter.5.cloned.1.call-done = bf16[64,1024]{1,0:T(8,128)(2,1)} async-done(((bf16[1024,1024]{1,0:T(8,128)(2,1)}), bf16[64,1024]{1,0:T(8,128)(2,1)}) %reduce-scatter.5.cloned.1.call-update) | async-done | bytes 131088 | tf_op jit(solution)/shard_map/reduce_scatter | solution.py:1304
  885.7 89.0 %all-reduce.6.cloned.1.call-done = (bf16[16,2,64,448]{3,2,0,1:T(8,128)(2,1)}, bf16[2,64,1024]{2,1,0:T(8,128)(2,1)}, bf16[2,256,1024]{2,1,0:T(8,128)(2,1)}) async-done(((bf16[16,2,64,448]{3,2,0,1:T(8,128)(2,1)}, bf16[2,64,1024]{2,1,0:T(8,128)(2,1)}, bf16[2,256,1024]{2,1,0:T(8,128)(2,1)}), (bf16[16,2,64,448]{3,2,0,1:T(8,128)(2,1)}, bf16[2,64,1024]{2,1,0:T(8,128)(2,1)}, ...) | async-done | bytes 3145744 | tf_op jit(solution)/shard_map/psum | solution.py:1331
  974.7 3.1 copy.99
  977.8 5.8 all-to-all-start.1
  987.6 141.9 %all-reduce.4.cloned.1.call-done = f32[2,22544]{1,0:T(2,128)} async-done(((f32[2,22544]{1,0:T(2,128)}), f32[2,22544]{1,0:T(2,128)}) %all-reduce.4.cloned.1.call-update) | async-done | bytes 180368 | tf_op jit(solution)/shard_map/psum | solution.py:1329
  1137.8 4.6 copy.100
  1142.5 3.0 convert_element_type.91
  1150.1 3.4 copy.103
  1159.9 3.7 copy.102
  (417 shorter events, 126.6 us)
Async XLA Ops:
  7.2 204.4 %all-gather.5.cloned.1.call-start = ((), (), s32[]{:S(2)}) async-start(), calls=%async_computation.7 | async-start | bytes 2228224 | tf_op jit(solution)/shard_map/all_gather | solution.py:1251
  11.6 11.8 %copy-start.72 = (f32[2,7,1024]{2,0,1:T(2,128)S(1)}, f32[2,7,1024]{2,0,1:T(2,128)}, u32[]{:S(2)}) copy-start(f32[2,7,1024]{2,0,1:T(2,128)} %param.24) | copy-start | bytes 172036
  11.6 11.9 %copy-start.74 = (f32[2,3,1024]{2,0,1:T(2,128)S(1)}, f32[2,3,1024]{2,0,1:T(2,128)}, u32[]{:S(2)}) copy-start(f32[2,3,1024]{2,0,1:T(2,128)} %param.23) | copy-start | bytes 73732
  11.6 11.9 %copy-start.48 = (bf16[160,1024]{1,0:T(8,128)(2,1)S(1)}, bf16[160,1024]{1,0:T(8,128)(2,1)}, u32[]{:S(2)}) copy-start(bf16[160,1024]{1,0:T(8,128)(2,1)} %param.15) | copy-start | bytes 983044
  13.1 193.3 %all-to-all-start = ((bf16[16,64,512]{2,1,0:T(8,128)(2,1)}), bf16[16,64,512]{2,1,0:T(8,128)(2,1)}, u32[]{:S(2)}, u32[]{:S(2)}) async-start(bf16[16,64,512]{2,1,0:T(8,128)(2,1)} %reshape.463), calls=%async_computation | async-start | bytes 2097152 | tf_op jit(solution)/shard_map/all_to_all | solution.py:1237
  20.6 365.2 %all-gather.7.cloned.1.call-start = ((), (), s32[]{:S(2)}) async-start(), calls=%async_computation.8 | async-start | bytes 2228224 | tf_op jit(solution)/shard_map/all_gather | solution.py:1251
  21.3 822.9 %reduce-scatter.3.cloned.1.call-start = ((), (), s32[]{:S(2)}) async-start(), calls=%async_computation.4 | async-start | bytes 2228224 | tf_op jit(solution)/shard_map/reduce_scatter | solution.py:1304
  23.9 63.5 %copy-start.81 = (f32[160]{0:T(256)}, f32[160]{0:T(256)S(1)}, u32[]{:S(2)}) copy-start(f32[160]{0:T(256)S(1)} %fusion.29) | copy-start | bytes 1924
  24.9 62.5 %copy-start.92 = (f32[2,16]{1,0:T(2,128)S(1)}, f32[2,16]{1,0:T(2,128)}, u32[]{:S(2)}) copy-start(f32[2,16]{1,0:T(2,128)} %param.27) | copy-start | bytes 388
  24.9 62.5 %copy-start.93 = (s32[3]{0:T(128)S(1)}, s32[3]{0:T(128)}, u32[]{:S(2)}) copy-start(s32[3]{0:T(128)} %constant.136) | copy-start | bytes 40
  24.9 62.5 %copy-start.67 = (bf16[2,64,3072]{2,1,0:T(8,128)(2,1)S(1)}, bf16[2,64,3072]{2,1,0:T(8,128)(2,1)}, u32[]{:S(2)}) copy-start(bf16[2,64,3072]{2,1,0:T(8,128)(2,1)} %param.19) | copy-start | bytes 2359300
  120.4 27.6 %copy-start.9 = (bf16[1024,192]{1,0:T(8,128)(2,1)}, bf16[1024,192]{1,0:T(8,128)(2,1)S(1)}, u32[]{:S(2)}) copy-start(bf16[1024,192]{1,0:T(8,128)(2,1)S(1)} %get-tuple-element.179.w_ref) | copy-start | bytes 1179652
  130.8 221.3 %copy-start.34 = (s32[81]{0:T(128)}, s32[81]{0:T(128)S(1)}, u32[]{:S(2)}) copy-start(s32[81]{0:T(128)S(1)} %pad_add_fusion.table) | copy-start | bytes 976
  151.3 17.9 %copy-start.73 = (f32[2,4096]{1,0:T(2,128)S(1)}, f32[2,4096]{1,0:T(2,128)}, u32[]{:S(2)}) copy-start(f32[2,4096]{1,0:T(2,128)} %param.25) | copy-start | bytes 98308
  151.3 17.9 %copy-start.71 = (f32[2,2,4096]{2,1,0:T(2,128)S(1)}, f32[2,2,4096]{2,1,0:T(2,128)}, u32[]{:S(2)}) copy-start(f32[2,2,4096]{2,1,0:T(2,128)} %param.26) | copy-start | bytes 196612
  169.8 507.3 %copy-start.11 = (f32[256,1]{1,0:T(8,128)}, f32[256,1]{1,0:T(8,128)S(1)}, u32[]{:S(2)}) copy-start(f32[256,1]{1,0:T(8,128)S(1)} %copy.86.gain_ref) | copy-start | bytes 3076
  170.2 283.7 %copy-start.12 = (f32[256,1]{1,0:T(8,128)}, f32[256,1]{1,0:T(8,128)S(1)}, u32[]{:S(2)}) copy-start(f32[256,1]{1,0:T(8,128)S(1)} %copy.90.gain_ref) | copy-start | bytes 3076
  170.2 36.1 %copy-start.64 = (bf16[2,256,1024]{2,1,0:T(8,128)(2,1)S(1)}, bf16[2,256,1024]{2,1,0:T(8,128)(2,1)}, u32[]{:S(2)}) copy-start(bf16[2,256,1024]{2,1,0:T(8,128)(2,1)} %param.22) | copy-start | bytes 3145732
  211.6 39.2 %copy-start.7 = (bf16[256,1024]{1,0:T(8,128)(2,1)}, bf16[256,1024]{1,0:T(8,128)(2,1)S(1)}, u32[]{:S(2)}) copy-start(bf16[256,1024]{1,0:T(8,128)(2,1)S(1)} %get-tuple-element.177.w_ref) | copy-start | bytes 1572868
  211.6 214.1 %copy-start.8 = (bf16[256,1024]{1,0:T(8,128)(2,1)}, bf16[256,1024]{1,0:T(8,128)(2,1)S(1)}, u32[]{:S(2)}) copy-start(bf16[256,1024]{1,0:T(8,128)(2,1)S(1)} %get-tuple-element.176.w_ref) | copy-start | bytes 1572868
  214.5 36.2 %copy-start.75 = (f32[160]{0:T(256)}, f32[160]{0:T(256)S(1)}, u32[]{:S(2)}) copy-start(f32[160]{0:T(256)S(1)} %fusion.39) | copy-start | bytes 1924
  215.7 35.1 %copy-start.85 = (f32[160]{0:T(256)}, f32[160]{0:T(256)S(1)}, u32[]{:S(2)}) copy-start(f32[160]{0:T(256)S(1)} %multiply_reduce_fusion.13) | copy-start | bytes 1924
  215.7 35.0 %copy-start.77 = (f32[160]{0:T(256)}, f32[160]{0:T(256)S(1)}, u32[]{:S(2)}) copy-start(f32[160]{0:T(256)S(1)} %fusion.40) | copy-start | bytes 1924
  279.4 37.5 %copy-start.14 = (bf16[256,2560]{1,0:T(8,128)(2,1)}, bf16[256,2560]{1,0:T(8,128)(2,1)S(1)}, u32[]{:S(2)}) copy-start(bf16[256,2560]{1,0:T(8,128)(2,1)S(1)} %get-tuple-element.70.mid_ref) | copy-start | bytes 3932164
  282.3 34.5 %copy-start.37 = (f32[160,1024]{1,0:T(8,128)S(1)}, f32[160,1024]{1,0:T(8,128)}, u32[]{:S(2)}) copy-start(f32[160,1024]{1,0:T(8,128)} %copy-done.36) | copy-start | bytes 1966084
  317.3 34.8 %copy-start.87 = (f32[160]{0:T(256)}, f32[160]{0:T(256)S(1)}, u32[]{:S(2)}) copy-start(f32[160]{0:T(256)S(1)} %multiply_reduce_fusion.12) | copy-start | bytes 1924
  317.3 34.8 %copy-start.79 = (f32[160]{0:T(256)}, f32[160]{0:T(256)S(1)}, u32[]{:S(2)}) copy-start(f32[160]{0:T(256)S(1)} %fusion.41) | copy-start | bytes 1924
  318.8 33.3 %copy-start.10 = (bf16[1024,192]{1,0:T(8,128)(2,1)S(1)}, bf16[1024,192]{1,0:T(8,128)(2,1)}, u32[]{:S(2)}) copy-start(bf16[1024,192]{1,0:T(8,128)(2,1)} %get-tuple-element.178.w_ref) | copy-start | bytes 1179652
  388.4 37.3 %copy-start.89 = (f32[160]{0:T(256)}, f32[160]{0:T(256)S(1)}, u32[]{:S(2)}) copy-start(f32[160]{0:T(256)S(1)} %multiply_reduce_fusion.11) | copy-start | bytes 1924
  475.5 49.4 %slice-start = ((s8[5242880]{0:T(1024)(128)(4,1)}), s8[4194304]{0:T(1024)(128)(4,1)S(1)}, s32[]{:S(2)}) async-start(s8[5242880]{0:T(1024)(128)(4,1)} %bitcast.275), calls=%async_computation.10 | async-start | bytes 8388608
  475.5 49.4 %slice-start.1 = ((s8[5242880]{0:T(1024)(128)(4,1)}), s8[1048576]{0:T(1024)(128)(4,1)S(1)}, s32[]{:S(2)}) async-start(s8[5242880]{0:T(1024)(128)(4,1)} %bitcast.275), calls=%async_computation.11 | async-start | bytes 2097152
  489.7 34.9 %copy-start.43 = (f32[160,1024]{1,0:T(8,128)S(1)}, f32[160,1024]{1,0:T(8,128)}, u32[]{:S(2)}) copy-start(f32[160,1024]{1,0:T(8,128)} %copy-done.42) | copy-start | bytes 1966084
  561.7 81.9 %copy-start.50 = (f32[160,1024]{1,0:T(8,128)}, f32[160,1024]{1,0:T(8,128)S(1)}, u32[]{:S(2)}) copy-start(f32[160,1024]{1,0:T(8,128)S(1)} %get-tuple-element.165) | copy-start | bytes 1966084
  605.6 37.4 %copy-start.41 = (f32[160,1024]{1,0:T(8,128)S(1)}, f32[160,1024]{1,0:T(8,128)}, u32[]{:S(2)}) copy-start(f32[160,1024]{1,0:T(8,128)} %copy-done.39) | copy-start | bytes 1966084
  605.6 37.4 %copy-start.80 = (f32[160]{0:T(256)S(1)}, f32[160]{0:T(256)}, u32[]{:S(2)}) copy-start(f32[160]{0:T(256)} %copy-done.79) | copy-start | bytes 1924
  605.6 37.7 %copy-start.88 = (f32[160]{0:T(256)S(1)}, f32[160]{0:T(256)}, u32[]{:S(2)}) copy-start(f32[160]{0:T(256)} %copy-done.87) | copy-start | bytes 1924
  644.6 32.5 %copy-start.15 = (bf16[256,2560]{1,0:T(8,128)(2,1)S(1)}, bf16[256,2560]{1,0:T(8,128)(2,1)}, u32[]{:S(2)}) copy-start(bf16[256,2560]{1,0:T(8,128)(2,1)} %copy-done.14) | copy-start | bytes 3932164
  644.6 32.5 %copy-start.24 = (f32[2,2560]{1,0:T(2,128)S(1)}, f32[2,2560]{1,0:T(2,128)}, u32[]{:S(2)}) copy-start(f32[2,2560]{1,0:T(2,128)} %pool_rows.4.stat_ref) | copy-start | bytes 61444
  713.0 35.2 %copy-start.38 = (f32[160,1024]{1,0:T(8,128)S(1)}, f32[160,1024]{1,0:T(8,128)}, u32[]{:S(2)}) copy-start(f32[160,1024]{1,0:T(8,128)} %copy-done.36) | copy-start | bytes 1966084
  713.0 35.2 %copy-start.78 = (f32[160]{0:T(256)S(1)}, f32[160]{0:T(256)}, u32[]{:S(2)}) copy-start(f32[160]{0:T(256)} %copy-done.77) | copy-start | bytes 1924
  713.0 35.5 %copy-start.86 = (f32[160]{0:T(256)S(1)}, f32[160]{0:T(256)}, u32[]{:S(2)}) copy-start(f32[160]{0:T(256)} %copy-done.85) | copy-start | bytes 1924
  753.5 127.5 %reduce-scatter.5.cloned.1.call-start = ((), (), s32[]{:S(2)}) async-start(), calls=%async_computation.5 | async-start | bytes 2228224 | tf_op jit(solution)/shard_map/reduce_scatter | solution.py:1304
  755.6 219.1 %all-reduce.6.cloned.1.call-start = ((), (), s32[]{:S(2)}) async-start(), calls=%async_computation.9 | async-start | bytes 6815744 | tf_op jit(solution)/shard_map/psum | solution.py:1331
  797.8 37.0 %copy-start.66 = (f32[192,1024]{1,0:T(8,128)S(1)}, f32[192,1024]{1,0:T(8,128)}, u32[]{:S(2)}) copy-start(f32[192,1024]{1,0:T(8,128)} %get-tuple-element.79) | copy-start | bytes 2359300
  797.8 37.1 %copy-start.65 = (f32[192,1024]{1,0:T(8,128)S(1)}, f32[192,1024]{1,0:T(8,128)}, u32[]{:S(2)}) copy-start(f32[192,1024]{1,0:T(8,128)} %get-tuple-element.81) | copy-start | bytes 2359300
  977.8 160.0 %all-to-all-start.1 = ((bf16[16,2,64,448]{3,2,1,0:T(8,128)(2,1)}), bf16[16,2,64,448]{3,2,1,0:T(8,128)(2,1)}, u32[]{:S(2)}, u32[]{:S(2)}) async-start(bf16[16,2,64,448]{3,2,1,0:T(8,128)(2,1)} %copy.99), calls=%async_computation.1 | async-start | bytes 4194304 | tf_op jit(solution)/shard_map/all_to_all | solution.py:1333
  983.7 145.8 %all-reduce.4.cloned.1.call-start = ((), (), s32[]{:S(2)}) async-start(), calls=%async_computation.6 | async-start | bytes 362496 | tf_op jit(solution)/shard_map/psum | solution.py:1329
  985.6 149.7 %copy-start.61 = (bf16[2,256,1024]{2,1,0:T(8,128)(2,1)S(1)}, bf16[2,256,1024]{2,1,0:T(8,128)(2,1)}, u32[]{:S(2)}) copy-start(bf16[2,256,1024]{2,1,0:T(8,128)(2,1)} %get-tuple-element.149) | copy-start | bytes 3145732
  (59 other events, 119.1 us)
Sparse Core Ops, SparseCore 0:
  10.7 54.6 all-gather.4
  67.6 50.2 all-gather.6
  753.6 62.2 reduce-scatter.2
  820.5 60.3 reduce-scatter.4
  883.8 90.8 all-reduce.5
  991.2 138.2 all-reduce.3

commit v2 on v1

--- a/solution.py
+++ b/solution.py
@@ -439,7 +439,13 @@
     pl.semaphore_signal(pltpu.get_barrier_semaphore(), inc=1, device_id=where, device_id_type=MESH)
 
 
-def greet_neighbours(z, y, c):
+def other_group():
+    return {"batch": 1 - lax.axis_index("batch")}
+
+
+def greet_neighbours(z, y, c, also=None):
+    if also is not None:
+        hail(also)
     hail(device(z, y, 1 - c))
     hail(device(z, 1 - y, c))
 
@@ -451,7 +457,12 @@
     def _():
         hail(device(z + 1, y, c))
 
-    pl.semaphore_wait(pltpu.get_barrier_semaphore(), 3 + jnp.where((z > 0) & (z < LINE - 1), 1, 0))
+    greeted = 3 if also is None else 4
+    pl.semaphore_wait(pltpu.get_barrier_semaphore(), greeted + jnp.where((z > 0) & (z < LINE - 1), 1, 0))
+
+
+def lasting(microseconds):
+    return pl.CostEstimate(flops=0, bytes_accessed=int(microseconds * 3.5e6), transcendentals=0)
 
 
 def remote(src, dst, send, recv, where):
@@ -460,11 +471,184 @@
     )
 
 
-def gather_kernel(x_ref, o_ref, sr, rr, sl, rl, sy, ry, sc, rc, own_sem):
+class Swap:
+    def __init__(self, x_ref, o_ref, ss, rs, own_sem):
+        self.x_ref, self.o_ref, self.ss, self.rs, self.own_sem = x_ref, o_ref, ss, rs, own_sem
+        self.k, self.n = lax.axis_index("blk"), o_ref.shape[0]
+
+    @staticmethod
+    def result(x):
+        return jax.ShapeDtypeStruct((4 * LINE,) + x.shape[1:], x.dtype)
+
+    @staticmethod
+    def scratch():
+        dma = pltpu.SemaphoreType.DMA
+        return [dma((4 * LINE,)), dma((4 * LINE,)), dma]
+
+    def source(self, to):
+        return self.x_ref.at[lax.rem(to, self.x_ref.shape[0])]
+
+    def send(self, i):
+        to = lax.rem(self.k + i, self.n)
+        return remote(self.source(to), self.o_ref.at[self.k], self.ss.at[i], self.rs.at[i], {"blk": to})
+
+    def receive(self, i):
+        at = lax.rem(self.k - i + self.n, self.n)
+        return remote(self.o_ref.at[at], self.o_ref.at[at], self.ss.at[i], self.rs.at[i], {"blk": at})
+
+    def own(self):
+        return pltpu.make_async_copy(self.source(self.k), self.o_ref.at[self.k], self.own_sem)
+
+    def start(self):
+        def one(i, carry):
+            self.send(i).start()
+            return carry
+
+        lax.fori_loop(1, self.n, one, 0)
+        self.own().start()
+
+    def finish(self):
+        def one(i, carry):
+            self.receive(i).wait_recv()
+            self.send(i).wait_send()
+            return carry
+
+        self.own().wait()
+        lax.fori_loop(1, self.n, one, 0)
+
+
+class Trade:
+    def __init__(self, x_ref, o_ref, ss, rs, own_sem):
+        self.x_ref, self.o_ref, self.ss, self.rs, self.own_sem = x_ref, o_ref, ss, rs, own_sem
+        self.z, self.y, self.c = place()
+
+    @staticmethod
+    def result(x):
+        return jax.ShapeDtypeStruct((LINE,) + x.shape[1:], x.dtype)
+
+    @staticmethod
+    def scratch():
+        dma = pltpu.SemaphoreType.DMA
+        return [dma((LINE,)), dma((LINE,)), dma]
+
+    def source(self, to):
+        return self.x_ref.at[lax.rem(to, self.x_ref.shape[0])]
+
+    def send(self, s):
+        to = lax.rem(self.z + s, LINE)
+        return remote(self.source(to), self.o_ref.at[self.z], self.ss.at[s], self.rs.at[s], device(to, self.y, self.c))
+
+    def own(self):
+        return pltpu.make_async_copy(self.source(self.z), self.o_ref.at[self.z], self.own_sem)
+
+    def start(self):
+        for s in range(1, LINE):
+            self.send(s).start()
+        self.own().start()
+
+    def finish(self):
+        self.own().wait()
+        for s in range(1, LINE):
+            at = lax.rem(self.z - s + LINE, LINE)
+            slot = self.o_ref.at[at]
+            remote(slot, slot, self.ss.at[s], self.rs.at[s], device(at, self.y, self.c)).wait_recv()
+            self.send(s).wait_send()
+
+
+class Cross:
+    def __init__(self, x_ref, o_ref, ss, rs):
+        self.copy = remote(x_ref, o_ref, ss, rs, other_group())
+
+    @staticmethod
+    def result(x):
+        return jax.ShapeDtypeStruct(x.shape, x.dtype)
+
+    @staticmethod
+    def scratch():
+        return [pltpu.SemaphoreType.DMA] * 2
+
+    def start(self):
+        self.copy.start()
+
+    def finish(self):
+        self.copy.wait()
+
+
+class Rides:
+    def __init__(self, rides):
+        self.kinds = [kind for kind, _ in rides]
+        self.arrays = [array for _, array in rides]
+
+    def results(self):
+        return [kind.result(array) for kind, array in zip(self.kinds, self.arrays)]
+
+    def specs(self):
+        return [pl.BlockSpec(memory_space=pl.ANY)] * len(self.kinds)
+
+    def scratch(self):
+        return [entry for kind in self.kinds for entry in kind.scratch()]
+
+    def split(self, refs, inputs, outputs):
+        n = len(self.kinds)
+        ins, refs = refs[:inputs], refs[inputs:]
+        sources, refs = refs[:n], refs[n:]
+        outs, refs = refs[:outputs], refs[outputs:]
+        results, refs = refs[:n], refs[n:]
+        count = len(self.scratch())
+        own, sems = refs[: len(refs) - count], list(refs[len(refs) - count :])
+        objects = []
+        for kind, source, result in zip(self.kinds, sources, results):
+            k = len(kind.scratch())
+            objects.append(kind(source, result, *sems[:k]))
+            sems = sems[k:]
+        return ins + outs + own, objects
+
+    def far(self):
+        return any(kind in (Swap, Trade) for kind in self.kinds)
+
+    def crossing(self):
+        return Cross in self.kinds
+
+
+def start_all(rides):
+    for ride in rides:
+        ride.start()
+
+
+def finish_all(rides):
+    for ride in rides:
+        ride.finish()
+
+
+def greet_group(crossing=False, plane=False):
+    k, n = lax.axis_index("blk"), 4 * LINE
+
+    def one(i, carry):
+        hail({"blk": lax.rem(k + i, n)})
+        return carry
+
+    lax.fori_loop(1, n, one, 0)
+    more = 0
+    if plane:
+        x, z, y, c = plane_place()
+        for d in range(4):
+            hail(plane_device(1 - x, z, 1 - y if d & 2 else y, 1 - c if d & 1 else c))
+        more = 4
+    elif crossing:
+        hail(other_group())
+        more = 1
+    pl.semaphore_wait(pltpu.get_barrier_semaphore(), n - 1 + more)
+
+
+def gather_kernel(rides, *refs):
+    (x_ref, o_ref, sr, rr, sl, rl, sy, ry, sc, rc, own_sem), riders = rides.split(refs, 1, 1)
     z, y, c = place()
     rows = x_ref.shape[0]
     half = rows // HALVES
-    greet_neighbours(z, y, c)
+    if rides.far():
+        greet_group(rides.crossing())
+    else:
+        greet_neighbours(z, y, c, other_group() if rides.crossing() else None)
 
     def block(zz, yy, h):
         return o_ref.at[pl.ds(index_of(zz, yy, c) * rows + h * half, half)]
@@ -505,6 +689,7 @@
         across(z, h, True).start()
     for h in range(HALVES):
         twin(z, y, h, True).start()
+    start_all(riders)
 
     def from_line(zz, h, send, recv):
         arrival(block(zz, y, h), send, recv)
@@ -583,19 +768,23 @@
             def _():
                 left(s, h).wait_send()
 
-
-def gather_rows(x, collective_id):
+    finish_all(riders)
+
+
+def gather_rows(x, collective_id, rides=()):
     rows, columns = x.shape
     dma = pltpu.SemaphoreType.DMA
+    rides = Rides(rides)
     return pl.pallas_call(
-        gather_kernel,
-        out_shape=jax.ShapeDtypeStruct((4 * LINE * rows, columns), x.dtype),
-        in_specs=[pl.BlockSpec(memory_space=pl.ANY)],
-        out_specs=pl.BlockSpec(memory_space=pl.ANY),
-        scratch_shapes=[dma((LINE, HALVES))] * 6 + [dma((2 * LINE, HALVES))] * 2 + [dma],
+        functools.partial(gather_kernel, rides),
+        out_shape=[jax.ShapeDtypeStruct((4 * LINE * rows, columns), x.dtype)] + rides.results(),
+        in_specs=[pl.BlockSpec(memory_space=pl.ANY)] + rides.specs(),
+        out_specs=[pl.BlockSpec(memory_space=pl.ANY)] + rides.specs(),
+        scratch_shapes=[dma((LINE, HALVES))] * 6 + [dma((2 * LINE, HALVES))] * 2 + [dma] + rides.scratch(),
+        cost_estimate=lasting(30),
         compiler_params=pltpu.CompilerParams(collective_id=collective_id, has_side_effects=True),
         name="gather_rows",
-    )(x)
+    )(x, *rides.arrays)
 
 
 def order_at(z, t):
@@ -605,11 +794,16 @@
     return jnp.where(z < 2, low, high)
 
 
-def scatter_kernel(p_ref, o_ref, mine, twins, ysend, yrecv, zsend, zright, zleft, sm, sc, rc, sy, ry, sz, rzr, rzl):
+def scatter_kernel(rides, *refs):
+    refs, riders = rides.split(refs, 1, 1)
+    p_ref, o_ref, mine, twins, ysend, yrecv, zsend, zright, zleft, sm, sc, rc, sy, ry, sz, rzr, rzl = refs
     z, y, c = place()
     rows = mine.shape[1]
     half = rows // HALVES
-    greet_neighbours(z, y, c)
+    if rides.far():
+        greet_group(rides.crossing())
+    else:
+        greet_neighbours(z, y, c, other_group() if rides.crossing() else None)
 
     def part(h):
         return pl.ds(h * half, half)
@@ -637,6 +831,7 @@
             for h in range(HALVES):
                 twin(t, own_y, h).start()
                 local_copy(t, own_y, h).start()
+    start_all(riders)
     for t in range(LINE):
         for h in range(HALVES):
             twin(t, 0, h).wait_recv()
@@ -710,137 +905,118 @@
             twin(t, 1, h).wait_send()
         for t in range(LINE - 1):
             along(0, t, h, True).wait_send()
-
-
-def scatter_rows(parts, collective_id):
+    finish_all(riders)
+
+
+def scatter_rows(parts, collective_id, rides=()):
     rows, columns = parts.shape[0] // (4 * LINE), parts.shape[1]
     dma = pltpu.SemaphoreType.DMA
 
     def blocks(n):
         return pltpu.VMEM((n, rows, columns), parts.dtype)
 
+    rides = Rides(rides)
     return pl.pallas_call(
-        scatter_kernel,
-        out_shape=jax.ShapeDtypeStruct((rows, columns), jnp.float32),
-        in_specs=[pl.BlockSpec(memory_space=pl.ANY)],
-        out_specs=pl.BlockSpec(memory_space=pltpu.VMEM),
+        functools.partial(scatter_kernel, rides),
+        out_shape=[jax.ShapeDtypeStruct((rows, columns), jnp.float32)] + rides.results(),
+        in_specs=[pl.BlockSpec(memory_space=pl.ANY)] + rides.specs(),
+        out_specs=[pl.BlockSpec(memory_space=pltpu.VMEM)] + rides.specs(),
         scratch_shapes=[blocks(2 * LINE), blocks(2 * LINE), blocks(LINE), blocks(LINE), blocks(LINE - 1), blocks(LINE), blocks(LINE)]
         + [dma((2 * LINE, HALVES))] * 3
-        + [dma((LINE, HALVES))] * 5,
+        + [dma((LINE, HALVES))] * 5
+        + rides.scratch(),
+        cost_estimate=lasting(32),
         compiler_params=pltpu.CompilerParams(
             collective_id=collective_id, has_side_effects=True, vmem_limit_bytes=40 << 20
         ),
         name="scatter_rows",
-    )(parts)
-
-
-def swap_kernel(x_ref, o_ref, ss, rs, own_sem):
-    k = lax.axis_index("blk")
-    n = x_ref.shape[0]
-
-    def greet(i, carry):
-        hail({"blk": lax.rem(k + i, n)})
-        return carry
-
-    lax.fori_loop(1, n, greet, 0)
-    pl.semaphore_wait(pltpu.get_barrier_semaphore(), n - 1)
-
-    def send(i):
-        to = lax.rem(k + i, n)
-        return remote(x_ref.at[to], o_ref.at[k], ss.at[i], rs.at[i], {"blk": to})
-
-    def receive(i):
-        at = lax.rem(k - i + n, n)
-        return remote(x_ref.at[at], o_ref.at[at], ss.at[i], rs.at[i], {"blk": at})
-
-    def begin(i, carry):
-        send(i).start()
-        return carry
-
-    lax.fori_loop(1, n, begin, 0)
-    own = pltpu.make_async_copy(x_ref.at[k], o_ref.at[k], own_sem)
-    own.start()
-    own.wait()
-
-    def finish(i, carry):
-        receive(i).wait_recv()
-        send(i).wait_send()
-        return carry
-
-    lax.fori_loop(1, n, finish, 0)
-
-
-def swap_blocks(x, collective_id):
-    n = x.shape[0]
-    dma = pltpu.SemaphoreType.DMA
+    )(parts, *rides.arrays)
+
+
+def swap_kernel(rides, *refs):
+    _, riders = rides.split(refs, 0, 0)
+    greet_group(rides.crossing())
+    start_all(riders)
+    finish_all(riders)
+
+
+def swap_blocks(x, collective_id, rides=()):
+    rides = Rides([(Swap, x), *rides])
     return pl.pallas_call(
-        swap_kernel,
-        out_shape=jax.ShapeDtypeStruct(x.shape, x.dtype),
-        in_specs=[pl.BlockSpec(memory_space=pl.ANY)],
-        out_specs=pl.BlockSpec(memory_space=pl.ANY),
-        scratch_shapes=[dma((n,)), dma((n,)), dma],
+        functools.partial(swap_kernel, rides),
+        out_shape=rides.results(),
+        in_specs=rides.specs(),
+        out_specs=rides.specs(),
+        scratch_shapes=rides.scratch(),
+        cost_estimate=lasting(10),
         compiler_params=pltpu.CompilerParams(collective_id=collective_id, has_side_effects=True),
         name="swap_blocks",
-    )(x)
-
-
-def pool_kernel(count, x_ref, o_ref, sent, got, ss, rs):
+    )(*rides.arrays)
+
+
+def finale_kernel(rides, *refs):
+    (v_ref, vo_ref, sent, got, vs, vr), riders = rides.split(refs, 1, 1)
     z, y, c = place()
-    hail(device(z, y, 1 - c))
-    hail(device(z, 1 - y, c))
-    for s in range(1, LINE):
-        hail(device(lax.rem(z + s, LINE), y, c))
-    pl.semaphore_wait(pltpu.get_barrier_semaphore(), LINE + 1)
-
-    def pooled(values, share):
-        if count is None:
-            return functools.reduce(jnp.add, values)
-        means = [v[0:1] for v in values]
-        mean = functools.reduce(jnp.add, means) * (1.0 / len(values))
-        squares = functools.reduce(jnp.add, [v[1:2] for v in values])
-        apart = functools.reduce(jnp.add, [(m - mean) * (m - mean) for m in means])
-        return jnp.concatenate([mean, squares + apart * share], axis=0)
-
-    def exchange(slot, where):
-        return remote(sent.at[slot], got.at[slot], ss.at[slot], rs.at[slot], where)
-
-    value = x_ref[...]
-    share = count
-    for stage, where in enumerate((device(z, y, 1 - c), device(z, 1 - y, c))):
-        sent[stage] = value
-        copy = exchange(stage, where)
+    greet_group(True)
+    cross = remote(v_ref, got.at[0], vs.at[0], vr.at[0], other_group())
+    cross.start()
+    start_all(riders)
+
+    def wide(ref):
+        return ref.astype(jnp.float32)
+
+    cross.wait_recv()
+    value = wide(v_ref[...]) + wide(got[0])
+    for stage, where in ((1, device(z, y, 1 - c)), (2, device(z, 1 - y, c))):
+        sent[stage - 1] = value.astype(jnp.bfloat16)
+        copy = remote(sent.at[stage - 1], got.at[stage], vs.at[stage], vr.at[stage], where)
         copy.start()
-        copy.wait()
-        value = pooled([value, got[stage]], share)
-        share = None if count is None else 2 * share
-    sent[2] = value
+        copy.wait_recv()
+        value = wide(sent[stage - 1]) + wide(got[stage])
+    sent[2] = value.astype(jnp.bfloat16)
     copies = []
     for s in range(1, LINE):
         where = device(lax.rem(z + s, LINE), y, c)
-        copies.append(remote(sent.at[2], got.at[1 + s], ss.at[1 + s], rs.at[1 + s], where))
+        copies.append(remote(sent.at[2], got.at[2 + s], vs.at[2 + s], vr.at[2 + s], where))
     for copy in copies:
         copy.start()
     for copy in copies:
-        copy.wait()
-    o_ref[...] = pooled([value] + [got[1 + s] for s in range(1, LINE)], share)
-
-
-def pool_rows(x, count, collective_id):
+        copy.wait_recv()
+    total = jnp.zeros_like(value)
+    for zz in range(LINE):
+        term = wide(sent[2])
+        for s in range(1, LINE):
+            term = jnp.where(lax.rem(z - s + LINE, LINE) == zz, wide(got[2 + s]), term)
+        total += term
+    vo_ref[...] = total
+    cross.wait_send()
+    for stage in (1, 2):
+        remote(sent.at[stage - 1], got.at[stage], vs.at[stage], vr.at[stage], device(z, y, 1 - c)).wait_send()
+    for copy in copies:
+        copy.wait_send()
+    finish_all(riders)
+
+
+def finale(v, collective_id, rides):
+    rides = Rides(rides)
     dma = pltpu.SemaphoreType.DMA
+    vmem = [pl.BlockSpec(memory_space=pltpu.VMEM)]
     return pl.pallas_call(
-        functools.partial(pool_kernel, count),
-        out_shape=jax.ShapeDtypeStruct(x.shape, x.dtype),
-        in_specs=[pl.BlockSpec(memory_space=pltpu.VMEM)],
-        out_specs=pl.BlockSpec(memory_space=pltpu.VMEM),
+        functools.partial(finale_kernel, rides),
+        out_shape=[jax.ShapeDtypeStruct(v.shape, jnp.float32)] + rides.results(),
+        in_specs=vmem + rides.specs(),
+        out_specs=vmem + rides.specs(),
         scratch_shapes=[
-            pltpu.VMEM((3,) + x.shape, x.dtype),
-            pltpu.VMEM((LINE + 1,) + x.shape, x.dtype),
-            dma((LINE + 1,)),
-            dma((LINE + 1,)),
-        ],
+            pltpu.VMEM((3,) + v.shape, v.dtype),
+            pltpu.VMEM((LINE + 2,) + v.shape, v.dtype),
+            dma((LINE + 2,)),
+            dma((LINE + 2,)),
+        ]
+        + rides.scratch(),
+        cost_estimate=lasting(18),
         compiler_params=pltpu.CompilerParams(collective_id=collective_id, has_side_effects=True),
-        name="pool_rows",
-    )(x)
+        name="finale",
+    )(v, *rides.arrays)
 
 
 NN = (((1,), (0,)), ((), ()))
@@ -946,6 +1122,7 @@
             pltpu.VMEM((total, 64), jnp.bfloat16),
             pltpu.VMEM((64, total), jnp.bfloat16),
         ],
+        cost_estimate=lasting(11),
         compiler_params=pltpu.CompilerParams(vmem_limit_bytes=50 << 20),
         name="attend",
     )(table, x, w, b, scale)
@@ -953,8 +1130,8 @@
 
 def attend_back_kernel(
     table, da_ref, x_ref, w_ref, scale_ref, qvk_ref, lse_ref, out_ref,
-    part_ref, gw_ref, gb_ref, gs_ref,
-    packed, dout, delta, query, keys, values, keys_t, dkeys, dvalues, dquery_t, flat,
+    part_ref, gwt_ref, gb_ref, gs_ref,
+    gw_ref, packed, dout, delta, query, keys, values, keys_t, dkeys, dvalues, dquery_t, flat,
 ):
     total = x_ref.shape[0]
     tiles = total // TILE
@@ -1023,6 +1200,7 @@
         return carry
 
     lax.fori_loop(0, tiles, finish, 0)
+    gwt_ref[...] = jnp.transpose(gw_ref[...]).astype(jnp.bfloat16)
 
 
 def attend_back(table, da, x, w, scale, qvk, lse, out):
@@ -1035,175 +1213,564 @@
         attend_back_kernel,
         out_shape=(
             jax.ShapeDtypeStruct((total, width), jnp.bfloat16),
-            jax.ShapeDtypeStruct((192, width), jnp.float32),
+            jax.ShapeDtypeStruct((width, 192), jnp.bfloat16),
             jax.ShapeDtypeStruct((1, 192), jnp.float32),
             jax.ShapeDtypeStruct((1, 1), jnp.float32),
         ),
         in_specs=[smem, vmem, vmem, vmem, smem, vmem, vmem, vmem],
         out_specs=(vmem, vmem, vmem, vmem),
         scratch_shapes=[
-            low(total // 2, 128), low(total, 64), full(1, total), low(total, 64), low(total, 64), low(total, 64),
+            full(192, width), low(total // 2, 128), low(total, 64), full(1, total), low(total, 64), low(total, 64), low(total, 64),
             low(64, total), full(total, 64), full(total, 64), full(64, total), low(total, 192),
         ],
+        cost_estimate=lasting(19),
         compiler_params=pltpu.CompilerParams(vmem_limit_bytes=56 << 20),
         name="attend_back",
     )(table, da, x, w, scale, qvk, lse, out)
 
 
-def up_kernel(x_ref, w_ref, b_ref, act_ref, slope_ref, stat_ref):
-    def step(t, carry):
-        at = tile_at(t)
-        upper = mul(w_ref[...], x_ref[at], NT) + b_ref[...]
-        chance = 0.5 * (1.0 + lax.erf(upper * (0.5**0.5)))
-        act = upper * chance
-        act_ref[:, at] = act
-        slope_ref[:, at] = chance + upper * (jnp.exp(-0.5 * upper * upper) * 0.3989422804014327)
-        mean = jnp.mean(act, axis=0, keepdims=True)
-        apart = act - mean
-        stat_ref[0:1, at] = mean
-        stat_ref[1:2, at] = jnp.sum(apart * apart, axis=0, keepdims=True)
-        return carry
-
-    lax.fori_loop(0, x_ref.shape[0] // TILE, step, 0)
-
-
-def up(x, w, b):
-    total, hidden = x.shape[0], w.shape[0]
-    vmem = pl.BlockSpec(memory_space=pltpu.VMEM)
+PLANE = 8
+
+
+def plane_place():
+    x = lax.axis_index("batch")
+    z, y, c = place()
+    return x, z, y, c
+
+
+def plane_device(x, z, y, c):
+    return {"batch": x, "blk": index_of(z, y, c)}
+
+
+def plane_index(x, y, c):
+    return (x * 2 + y) * 2 + c
+
+
+class PlaneGather:
+    def __init__(self, all_ref, sems):
+        self.all_ref = all_ref
+        self.sx, self.rx, self.sy, self.ry, self.sc, self.rc = sems
+        self.x, self.z, self.y, self.c = plane_place()
+        self.half = all_ref.shape[0] // (2 * PLANE)
+
+    @staticmethod
+    def scratch():
+        dma = pltpu.SemaphoreType.DMA
+        return [dma((3,))] * 4 + [dma((PLANE,))] * 2
+
+    def piece(self, x, y, c, h):
+        return self.all_ref.at[pl.ds(plane_index(x, y, c) * 2 * self.half + h * self.half, self.half)]
+
+    def over_x(self, i):
+        x, y, c = self.x, self.y, self.c
+        piece = self.piece(x, y if i < 2 else 1 - y, c, (0, 1, 1)[i])
+        return remote(piece, piece, self.sx.at[i], self.rx.at[i], plane_device(1 - x, self.z, y, c))
+
+    def over_y(self, i):
+        x, y, c = self.x, self.y, self.c
+        piece = self.piece(x if i < 2 else 1 - x, y, c, (1, 0, 0)[i])
+        return remote(piece, piece, self.sy.at[i], self.ry.at[i], plane_device(x, self.z, 1 - y, c))
+
+    def from_x(self, i):
+        x, y, c = self.x, self.y, self.c
+        piece = self.piece(1 - x, y if i < 2 else 1 - y, c, (0, 1, 1)[i])
+        remote(piece, piece, self.sx.at[i], self.rx.at[i], plane_device(1 - x, self.z, y, c)).wait_recv()
+
+    def from_y(self, i):
+        x, y, c = self.x, self.y, self.c
+        piece = self.piece(x if i < 2 else 1 - x, 1 - y, c, (1, 0, 0)[i])
+        remote(piece, piece, self.sy.at[i], self.ry.at[i], plane_device(x, self.z, 1 - y, c)).wait_recv()
+
+    def twin(self, other_x, other_y, h):
+        x = 1 - self.x if other_x else self.x
+        y = 1 - self.y if other_y else self.y
+        slot = (other_x * 2 + other_y) * 2 + h
+        piece = self.piece(x, y, self.c, h)
+        return remote(piece, piece, self.sc.at[slot], self.rc.at[slot], plane_device(self.x, self.z, self.y, 1 - self.c))
+
+    def from_twin(self, other_x, other_y, h):
+        x = 1 - self.x if other_x else self.x
+        y = 1 - self.y if other_y else self.y
+        slot = (other_x * 2 + other_y) * 2 + h
+        piece = self.piece(x, y, 1 - self.c, h)
+        where = plane_device(self.x, self.z, self.y, 1 - self.c)
+        remote(piece, piece, self.sc.at[slot], self.rc.at[slot], where).wait_recv()
+
+    def start(self):
+        self.over_x(0).start()
+        self.over_y(0).start()
+        self.over_x(1).start()
+        self.over_y(1).start()
+        self.twin(0, 0, 0).start()
+        self.twin(0, 0, 1).start()
+
+    def near(self):
+        self.from_x(0)
+        self.over_y(2).start()
+        self.twin(1, 0, 0).start()
+        self.from_y(0)
+        self.over_x(2).start()
+        self.twin(0, 1, 1).start()
+        self.from_y(1)
+        self.twin(0, 1, 0).start()
+        for other_y in range(2):
+            for h in range(2):
+                self.from_twin(0, other_y, h)
+
+    def far(self):
+        self.from_x(1)
+        self.twin(1, 0, 1).start()
+        self.from_x(2)
+        self.twin(1, 1, 1).start()
+        self.from_y(2)
+        self.twin(1, 1, 0).start()
+        for other_y in range(2):
+            for h in range(2):
+                self.from_twin(1, other_y, h)
+
+    def finish(self):
+        for i in range(3):
+            self.over_x(i).wait_send()
+            self.over_y(i).wait_send()
+        for other_x in range(2):
+            for other_y in range(2):
+                for h in range(2):
+                    self.twin(other_x, other_y, h).wait_send()
+
+
+class PlaneScatter:
+    def __init__(self, part_ref, bufs, sems):
+        self.part_ref = part_ref
+        self.twins, self.xs, self.xr, self.ys, self.yr = bufs
+        self.sx, self.rx, self.sy, self.ry, self.sc, self.rc = sems
+        self.x, self.z, self.y, self.c = plane_place()
+        self.half = part_ref.shape[0] // (2 * PLANE)
+
+    @staticmethod
+    def scratch(rows, columns):
+        dma = pltpu.SemaphoreType.DMA
+        half = pltpu.VMEM((3, rows // 2, columns), jnp.bfloat16)
+        return [pltpu.VMEM((4, rows, columns), jnp.bfloat16)] + [half] * 4, [dma((3,))] * 4 + [dma((4,))] * 2
+
+    def rows(self, which, c, h=None):
+        x = self.x if which >= 2 else 1 - self.x
+        y = self.y if which % 2 else 1 - self.y
+        at = plane_index(x, y, c) * 2 * self.half
+        return pl.ds(at, 2 * self.half) if h is None else pl.ds(at + h * self.half, self.half)
+
+    def twin(self, which):
+        where = plane_device(self.x, self.z, self.y, 1 - self.c)
+        source = self.part_ref.at[self.rows(which, 1 - self.c)]
+        return remote(source, self.twins.at[which], self.sc.at[which], self.rc.at[which], where)
+
+    def over_x(self, i):
+        return remote(
+            self.xs.at[i], self.xr.at[i], self.sx.at[i], self.rx.at[i], plane_device(1 - self.x, self.z, self.y, self.c)
+        )
+
+    def over_y(self, i):
+        return remote(
+            self.ys.at[i], self.yr.at[i], self.sy.at[i], self.ry.at[i], plane_device(self.x, self.z, 1 - self.y, self.c)
+        )
+
+    def chip(self, which, h):
+        own = self.part_ref[self.rows(which, self.c, h)].astype(jnp.float32)
+        return own + self.twins[which, h * self.half : (h + 1) * self.half].astype(jnp.float32)
+
+    def first(self):
+        self.twin(0).wait_recv()
+        self.xs[0] = self.chip(0, 0).astype(jnp.bfloat16)
+        self.over_x(0).start()
+        self.ys[0] = self.chip(0, 1).astype(jnp.bfloat16)
+        self.over_y(0).start()
+        self.twin(1).wait_recv()
+        self.xs[1] = self.chip(1, 0).astype(jnp.bfloat16)
+        self.over_x(1).start()
+        self.twin(2).wait_recv()
+        self.ys[1] = self.chip(2, 1).astype(jnp.bfloat16)
+        self.over_y(1).start()
+
+    def second(self):
+        self.over_x(0).wait_recv()
+        self.ys[2] = (self.chip(2, 0) + self.xr[0].astype(jnp.float32)).astype(jnp.bfloat16)
+        self.over_y(2).start()
+        self.over_y(0).wait_recv()
+        self.xs[2] = (self.chip(1, 1) + self.yr[0].astype(jnp.float32)).astype(jnp.bfloat16)
+        self.over_x(2).start()
+
+    def finish(self, o_ref):
+        half = self.half
+        self.twin(3).wait_recv()
+        self.over_x(1).wait_recv()
+        self.over_y(1).wait_recv()
+        self.over_y(2).wait_recv()
+        o_ref[0:half] = self.chip(3, 0) + self.xr[1].astype(jnp.float32) + self.yr[2].astype(jnp.float32)
+        self.over_x(2).wait_recv()
+        o_ref[half : 2 * half] = self.chip(3, 1) + self.yr[1].astype(jnp.float32) + self.xr[2].astype(jnp.float32)
+        for which in range(4):
+            self.twin(which).wait_send()
+        for i in range(3):
+            self.over_x(i).wait_send()
+            self.over_y(i).wait_send()
+
+
+class PlanePool:
+    def __init__(self, own_ref, got_ref, send, recv):
+        self.own_ref, self.got_ref, self.send, self.recv = own_ref, got_ref, send, recv
+        self.x, self.z, self.y, self.c = plane_place()
+
+    def others(self):
+        for d in range(1, PLANE):
+            x = 1 - self.x if d & 4 else self.x
+            y = 1 - self.y if d & 2 else self.y
+            c = 1 - self.c if d & 1 else self.c
+            yield d, x, y, c
+
+    def run(self):
+        me = plane_index(self.x, self.y, self.c)
+        copies = [
+            remote(self.own_ref, self.got_ref.at[me], self.send.at[d], self.recv.at[d], plane_device(x, self.z, y, c))
+            for d, x, y, c in self.others()
+        ]
+        for copy in copies:
+            copy.start()
+        self.got_ref[me] = self.own_ref[...]
+        for d, x, y, c in self.others():
+            slot = self.got_ref.at[plane_index(x, y, c)]
+            remote(slot, slot, self.send.at[d], self.recv.at[d], plane_device(x, self.z, y, c)).wait_recv()
+        for copy in copies:
+            copy.wait_send()
+
+
+def greet_plane():
+    x, z, y, c = plane_place()
+    for d in range(1, PLANE):
+        hail(plane_device(1 - x if d & 4 else x, z, 1 - y if d & 2 else y, 1 - c if d & 1 else c))
+    pl.semaphore_wait(pltpu.get_barrier_semaphore(), PLANE - 1)
+
+
+def greet_for(rides):
+    if rides.far():
+        greet_group(plane=True)
+    else:
+        greet_plane()
+
+
+def span_at(th, width):
+    return pl.ds(pl.multiple_of(th * width, 128), width)
+
+
+def units_at(ut):
+    return pl.ds(pl.multiple_of(ut * 256, 256), 256)
+
+
+def mean_and_rate(stat, hidden_all):
+    return stat[0:1], lax.rsqrt(stat[1:2] * (1.0 / hidden_all) + EPSILON)
+
+
+def ffn_kernel(hidden_all, rides, *refs):
+    refs, riders = rides.split(refs, 6, 6)
+    x_ref, wu_ref, b_ref, gain_ref, shift_ref, wd_ref = refs[:6]
+    y_ref, xo_ref, acto_ref, slopeo_ref, stat_ref, mido_ref = refs[6:12]
+    rows_all, act, slope, mid, part, own_stat, got_stat, ps, pr, out_sem = refs[12:22]
+    refs = refs[22:]
+    gather = PlaneGather(rows_all, refs[:6])
+    scatter = PlaneScatter(part, refs[6:11], refs[11:17])
+    pool = PlanePool(own_stat, got_stat, ps, pr)
+    x, z, y, c = plane_place()
+    rows = x_ref.shape[0]
+    hidden, total = act.shape
+    width = total // 2
+    rows_all[pl.ds(plane_index(x, y, c) * rows, rows)] = x_ref[...]
+    greet_for(rides)
+    gather.start()
+    start_all(riders)
+
+    def climb(th):
+        at = span_at(th, width)
+
+        def units(ut, carry):
+            here = units_at(ut)
+            upper = mul(wu_ref[here], rows_all[pl.ds(th * width, width)], NT) + b_ref[here]
+            chance = 0.5 * (1.0 + lax.erf(upper * (0.5**0.5)))
+            act[here, at] = upper * chance
+            slope[here, at] = chance + upper * (jnp.exp(-0.5 * upper * upper) * 0.3989422804014327)
+            return carry
+
+        lax.fori_loop(0, hidden // 256, units, 0)
+        values = act[:, at]
+        mean = jnp.mean(values, axis=0, keepdims=True)
+        apart = values - mean
+        own_stat[0:1, at] = mean
+        own_stat[1:2, at] = jnp.sum(apart * apart, axis=0, keepdims=True)
+
+    gather.near()
+    climb(x)
+    gather.far()
+    climb(1 - x)
+    pool.run()
+    means = [got_stat[i, 0:1] for i in range(PLANE)]
+    mean = functools.reduce(jnp.add, means) * (1.0 / PLANE)
+    apart = functools.reduce(jnp.add, [(m - mean) * (m - mean) for m in means])
+    stat_ref[0:1] = mean
+    stat_ref[1:2] = functools.reduce(jnp.add, [got_stat[i, 1:2] for i in range(PLANE)]) + apart * float(hidden)
+    outs = [
+        pltpu.make_async_copy(source, dest, out_sem.at[i])
+        for i, (source, dest) in enumerate(((rows_all, xo_ref), (act, acto_ref), (slope, slopeo_ref), (mid, mido_ref)))
+    ]
+    for copy in outs[:3]:
+        copy.start()
+
+    def descend(th):
+        at = span_at(th, width)
+        mean, rate = mean_and_rate(stat_ref[:, at], hidden_all)
+
+        def units(ut, carry):
+            here = units_at(ut)
+            mid[here, at] = ((act[here, at] - mean) * rate * gain_ref[here] + shift_ref[here]).astype(jnp.bfloat16)
+            return carry
+
+        lax.fori_loop(0, hidden // 256, units, 0)
+        part[pl.ds(th * width, width)] = mul(mid[:, at], wd_ref[...], TN).astype(jnp.bfloat16)
+
+    descend(1 - x)
+    scatter.twin(0).start()
+    scatter.twin(1).start()
+    descend(x)
+    scatter.twin(2).start()
+    scatter.twin(3).start()
+    outs[3].start()
+    scatter.first()
+    scatter.second()
+    scatter.finish(y_ref)
+    gather.finish()
+    for copy in outs:
+        copy.wait()
+    finish_all(riders)
+
+
+def ffn(hidden_all, x, w_up, bias, gain, shift, w_down, collective_id, rides=()):
+    rides = Rides(rides)
+    rows, columns = x.shape
+    hidden, total = w_up.shape[0], rows * PLANE
+    vmem, anywhere = pl.BlockSpec(memory_space=pltpu.VMEM), pl.BlockSpec(memory_space=pl.ANY)
+    dma = pltpu.SemaphoreType.DMA
+    full = lambda *shape: pltpu.VMEM(shape, jnp.float32)
+    low = lambda *shape: pltpu.VMEM(shape, jnp.bfloat16)
+    bufs, sems = PlaneScatter.scratch(rows, columns)
     return pl.pallas_call(
-        up_kernel,
-        out_shape=(
+        functools.partial(ffn_kernel, hidden_all, rides),
+        out_shape=[
+            jax.ShapeDtypeStruct((rows, columns), jnp.float32),
+            jax.ShapeDtypeStruct((total, columns), jnp.bfloat16),
             jax.ShapeDtypeStruct((hidden, total), jnp.float32),
             jax.ShapeDtypeStruct((hidden, total), jnp.float32),
             jax.ShapeDtypeStruct((2, total), jnp.float32),
+            jax.ShapeDtypeStruct((hidden, total), jnp.bfloat16),
+        ]
+        + rides.results(),
+        in_specs=[vmem] * 6 + rides.specs(),
+        out_specs=[vmem, anywhere, anywhere, anywhere, vmem, anywhere] + rides.specs(),
+        scratch_shapes=[
+            low(total, columns), full(hidden, total), full(hidden, total), low(hidden, total), low(total, columns),
+            full(2, total), full(PLANE, 2, total), dma((PLANE,)), dma((PLANE,)), dma((4,)),
+        ]
+        + PlaneGather.scratch()
+        + bufs
+        + sems
+        + rides.scratch(),
+        cost_estimate=lasting(40),
+        compiler_params=pltpu.CompilerParams(
+            collective_id=collective_id, has_side_effects=True, vmem_limit_bytes=50 << 20
         ),
-        in_specs=[vmem] * 3,
-        out_specs=(vmem,) * 3,
-        compiler_params=pltpu.CompilerParams(vmem_limit_bytes=50 << 20),
-        name="up",
-    )(x, w, b)
-
-
-def centred(act, stat, hidden_all):
-    return (act - stat[0:1]) * lax.rsqrt(stat[1:2] * (1.0 / hidden_all) + EPSILON)
-
-
-def down_kernel(hidden_all, act_ref, stat_ref, gain_ref, shift_ref, w_ref, part_ref, mid_ref):
-    def step(t, carry):
-        at = tile_at(t)
-        vh = centred(act_ref[:, at], stat_ref[:, at], hidden_all)
-        low = (vh * gain_ref[...] + shift_ref[...]).astype(jnp.bfloat16)
-        mid_ref[:, at] = low
-        part_ref[at] = mul(low, w_ref[...], TN).astype(jnp.bfloat16)
+        name="ffn",
+    )(x, w_up, bias, gain, shift, w_down, *rides.arrays)
+
+
+def ffn_back_kernel(hidden_all, rides, *refs):
+    refs, riders = rides.split(refs, 9, 6)
+    dy_ref, wu_ref, gain_ref, wd_ref, stat_ref, xi_ref, acti_ref, slopei_ref, midi_ref = refs[:9]
+    dx_ref, gdown_ref, gup_ref, gg_ref, gs_ref, gb_ref = refs[9:15]
+    rows_all, dy_all, act, slope, mid, dmid, part, own_sums, got_sums, sums, ps, pr, in_sem = refs[15:28]
+    refs = refs[28:]
+    gather = PlaneGather(dy_all, refs[:6])
+    scatter = PlaneScatter(part, refs[6:11], refs[11:17])
+    pool = PlanePool(own_sums, got_sums, ps, pr)
+    x, z, y, c = plane_place()
+    rows = dy_ref.shape[0]
+    hidden, total = act.shape
+    width = total // 2
+    dy_all[pl.ds(plane_index(x, y, c) * rows, rows)] = dy_ref[...]
+    greet_for(rides)
+    gather.start()
+    start_all(riders)
+    ins = [
+        pltpu.make_async_copy(source, dest, in_sem.at[i])
+        for i, (source, dest) in enumerate(((acti_ref, act), (slopei_ref, slope), (midi_ref, mid), (xi_ref, rows_all)))
+    ]
+    for copy in ins:
+        copy.start()
+    gg_ref[...] = jnp.zeros_like(gg_ref)
+    gs_ref[...] = jnp.zeros_like(gs_ref)
+    gb_ref[...] = jnp.zeros_like(gb_ref)
+    own_sums[...] = jnp.zeros_like(own_sums)
+
+    def climb(th):
+        at = span_at(th, width)
+        mean, rate = mean_and_rate(stat_ref[:, at], hidden_all)
+
+        def units(ut, carry):
+            here = units_at(ut)
+            dm = mul(wd_ref[here], dy_all[pl.ds(th * width, width)], NT)
+            dmid[here, at] = dm
+            vh = (act[here, at] - mean) * rate
+            act[here, at] = vh
+            gg_ref[here] += jnp.sum(dm * vh, axis=1, keepdims=True)
+            gs_ref[here] += jnp.sum(dm, axis=1, keepdims=True)
+            scaled = dm * gain_ref[here]
+            own_sums[0:1, at] += jnp.sum(scaled, axis=0, keepdims=True)
+            own_sums[1:2, at] += jnp.sum(scaled * vh, axis=0, keepdims=True)
+            return carry
+
+        lax.fori_loop(0, hidden // 256, units, 0)
+
+    gather.near()
+    ins[0].wait()
+    climb(x)
+    gather.far()
+    climb(1 - x)
+    pool.run()
+    sums[...] = functools.reduce(jnp.add, [got_sums[i] for i in range(PLANE)]) * (1.0 / hidden_all)
+    ins[1].wait()
+
+    def descend(th):
+        at = span_at(th, width)
+        mean, rate = mean_and_rate(stat_ref[:, at], hidden_all)
+        sum0, sum1 = sums[0:1, at], sums[1:2, at]
+
+        def units(ut, carry):
+            here = units_at(ut)
+            dact = rate * (dmid[here, at] * gain_ref[here] - sum0 - act[here, at] * sum1)
+            du = (dact * slope[here, at]).astype(jnp.bfloat16)
+            du_ref[here, at] = du
+            gb_ref[here] += jnp.sum(du.astype(jnp.float32), axis=1, keepdims=True)
+            return carry
+
+        lax.fori_loop(0, hidden // 256, units, 0)
+        part[pl.ds(th * width, width)] = mul(du_ref[:, at], wu_ref[...], TN).astype(jnp.bfloat16)
+
+    du_ref = refs[17]
+    descend(1 - x)
+    scatter.twin(0).start()
+    scatter.twin(1).start()
+    descend(x)
+    scatter.twin(2).start()
+    scatter.twin(3).start()
+    scatter.first()
+    ins[2].wait()
+
+    def down_grad(ut, carry):
+        here = units_at(ut)
+        gdown_ref[here] = mul(mid[here], dy_all[...]).astype(jnp.bfloat16)
         return carry
 
-    lax.fori_loop(0, act_ref.shape[1] // TILE, step, 0)
-
-
-def down(hidden_all, act, stat, gain, shift, w):
+    lax.fori_loop(0, hidden // 256, down_grad, 0)
+    scatter.second()
+    ins[3].wait()
+
+    def up_grad(ut, carry):
+        here = units_at(ut)
+        gup_ref[:, here] = jnp.transpose(mul(du_ref[here], rows_all[...])).astype(jnp.bfloat16)
+        return carry
+
+    lax.fori_loop(0, hidden // 256, up_grad, 0)
+    scatter.finish(dx_ref)
+    gather.finish()
+    finish_all(riders)
+
+
+def ffn_back(hidden_all, dy, w_up, gain, w_down, stat, x_all, act, slope, mid, collective_id, rides=()):
+    rides = Rides(rides)
+    rows, columns = dy.shape
     hidden, total = act.shape
+    vmem, anywhere = pl.BlockSpec(memory_space=pltpu.VMEM), pl.BlockSpec(memory_space=pl.ANY)
+    dma = pltpu.SemaphoreType.DMA
+    full = lambda *shape: pltpu.VMEM(shape, jnp.float32)
+    low = lambda *shape: pltpu.VMEM(shape, jnp.bfloat16)
+    bufs, sems = PlaneScatter.scratch(rows, columns)
+    column = jax.ShapeDtypeStruct((hidden, 1), jnp.float32)
+    return pl.pallas_call(
+        functools.partial(ffn_back_kernel, hidden_all, rides),
+        out_shape=[
+            jax.ShapeDtypeStruct((rows, columns), jnp.float32),
+            jax.ShapeDtypeStruct((hidden, columns), jnp.bfloat16),
+            jax.ShapeDtypeStruct((columns, hidden), jnp.bfloat16),
+            column,
+            column,
+            column,
+        ]
+        + rides.results(),
+        in_specs=[vmem] * 5 + [anywhere] * 4 + rides.specs(),
+        out_specs=[vmem] * 6 + rides.specs(),
+        scratch_shapes=[
+            low(total, columns), low(total, columns), full(hidden, total), full(hidden, total), low(hidden, total),
+            full(hidden, total), low(total, columns), full(2, total), full(PLANE, 2, total), full(2, total),
+            dma((PLANE,)), dma((PLANE,)), dma((4,)),
+        ]
+        + PlaneGather.scratch()
+        + bufs
+        + sems
+        + [low(hidden, total)]
+        + rides.scratch(),
+        cost_estimate=lasting(45),
+        compiler_params=pltpu.CompilerParams(
+            collective_id=collective_id, has_side_effects=True, vmem_limit_bytes=58 << 20
+        ),
+        name="ffn_back",
+    )(dy, w_up, gain, w_down, stat, x_all, act, slope, mid, *rides.arrays)
+
+
+def assemble_kernel(head0, head1, near0, near1, far0, far1, qkv_ref, up_ref):
+    x = lax.axis_index("batch")
+    for layer, head_ref, halves in ((0, head0, (near0, far0)), (1, head1, (near1, far1))):
+        width = 64 * head_ref.shape[0]
+        for j in range(0, head_ref.shape[0], 2):
+            left, right = head_ref[j].astype(jnp.float32), head_ref[j + 1].astype(jnp.float32)
+            for part, source in ((0, 0), (1, 128), (2, 64)):
+                pair = jnp.concatenate([left[:, source : source + 64], right[:, source : source + 64]], axis=1)
+                qkv_ref[layer, :, part * width + j * 64 : part * width + (j + 2) * 64] = pair
+        for half, half_ref in zip((x, 1 - x), halves):
+            for q in range(half_ref.shape[0]):
+                for z in range(LINE):
+                    at = pl.ds(pl.multiple_of((z * 4 + q) * 256 + half * 128, 128), 128)
+                    up_ref[layer, :, at] = half_ref[q, :, z * 128 : (z + 1) * 128].astype(jnp.float32)
+
+
+def assemble(heads, near, far, qkv_shape, up_shape):
     vmem = pl.BlockSpec(memory_space=pltpu.VMEM)
     return pl.pallas_call(
-        functools.partial(down_kernel, hidden_all),
-        out_shape=(
-            jax.ShapeDtypeStruct((total, w.shape[1]), jnp.bfloat16),
-            jax.ShapeDtypeStruct((hidden, total), jnp.bfloat16),
-        ),
-        in_specs=[vmem] * 5,
+        assemble_kernel,
+        out_shape=(jax.ShapeDtypeStruct(qkv_shape, jnp.float32), jax.ShapeDtypeStruct(up_shape, jnp.float32)),
+        in_specs=[vmem] * 6,
         out_specs=(vmem,) * 2,
-        compiler_params=pltpu.CompilerParams(vmem_limit_bytes=50 << 20),
-        name="down",
-    )(act, stat, gain, shift, w)
-
-
-def down_back_kernel(hidden_all, dy_ref, w_ref, act_ref, stat_ref, gain_ref, mid_ref, dmid_ref, sums_ref, gw_ref, gg_ref, gs_ref):
-    gw_ref[...] = jnp.zeros_like(gw_ref)
-    gg_ref[...] = jnp.zeros_like(gg_ref)
-    gs_ref[...] = jnp.zeros_like(gs_ref)
-
-    def step(t, carry):
-        at = tile_at(t)
-        dmid = mul(w_ref[...], dy_ref[at], NT)
-        dmid_ref[:, at] = dmid
-        vh = centred(act_ref[:, at], stat_ref[:, at], hidden_all)
-        gg_ref[...] += jnp.sum(dmid * vh, axis=1, keepdims=True)
-        gs_ref[...] += jnp.sum(dmid, axis=1, keepdims=True)
-        scaled = dmid * gain_ref[...]
-        sums_ref[0:1, at] = jnp.sum(scaled, axis=0, keepdims=True)
-        sums_ref[1:2, at] = jnp.sum(scaled * vh, axis=0, keepdims=True)
-        gw_ref[...] += mul(mid_ref[:, at], dy_ref[at])
-        return carry
-
-    lax.fori_loop(0, act_ref.shape[1] // TILE, step, 0)
-
-
-def down_back(hidden_all, dy, w, act, stat, gain, mid):
-    hidden, total = act.shape
-    vmem = pl.BlockSpec(memory_space=pltpu.VMEM)
-    return pl.pallas_call(
-        functools.partial(down_back_kernel, hidden_all),
-        out_shape=(
-            jax.ShapeDtypeStruct((hidden, total), jnp.float32),
-            jax.ShapeDtypeStruct((2, total), jnp.float32),
-            jax.ShapeDtypeStruct(w.shape, jnp.float32),
-            jax.ShapeDtypeStruct((hidden, 1), jnp.float32),
-            jax.ShapeDtypeStruct((hidden, 1), jnp.float32),
-        ),
-        in_specs=[vmem] * 6,
-        out_specs=(vmem,) * 5,
-        compiler_params=pltpu.CompilerParams(vmem_limit_bytes=50 << 20),
-        name="down_back",
-    )(dy, w, act, stat, gain, mid)
-
-
-def up_back_kernel(hidden_all, dmid_ref, act_ref, slope_ref, stat_ref, sums_ref, gain_ref, x_ref, w_ref, part_ref, gw_ref, gb_ref):
-    gw_ref[...] = jnp.zeros_like(gw_ref)
-    gb_ref[...] = jnp.zeros_like(gb_ref)
-
-    def step(t, carry):
-        at = tile_at(t)
-        stat = stat_ref[:, at]
-        vh = centred(act_ref[:, at], stat, hidden_all)
-        rate = lax.rsqrt(stat[1:2] * (1.0 / hidden_all) + EPSILON)
-        sums = sums_ref[:, at] * (1.0 / hidden_all)
-        dact = rate * (dmid_ref[:, at] * gain_ref[...] - sums[0:1] - vh * sums[1:2])
-        low = (dact * slope_ref[:, at]).astype(jnp.bfloat16)
-        gb_ref[...] += jnp.sum(low.astype(jnp.float32), axis=1, keepdims=True)
-        gw_ref[...] += mul(low, x_ref[at])
-        part_ref[at] = mul(low, w_ref[...], TN).astype(jnp.bfloat16)
-        return carry
-
-    lax.fori_loop(0, act_ref.shape[1] // TILE, step, 0)
-
-
-def up_back(hidden_all, dmid, act, slope, stat, sums, gain, x, w):
-    hidden, total = act.shape
-    vmem = pl.BlockSpec(memory_space=pltpu.VMEM)
-    return pl.pallas_call(
-        functools.partial(up_back_kernel, hidden_all),
-        out_shape=(
-            jax.ShapeDtypeStruct((total, w.shape[1]), jnp.bfloat16),
-            jax.ShapeDtypeStruct(w.shape, jnp.float32),
-            jax.ShapeDtypeStruct((hidden, 1), jnp.float32),
-        ),
-        in_specs=[vmem] * 8,
-        out_specs=(vmem,) * 3,
-        compiler_params=pltpu.CompilerParams(vmem_limit_bytes=56 << 20),
-        name="up_back",
-    )(dmid, act, slope, stat, sums, gain, x, w)
+        cost_estimate=lasting(5),
+        compiler_params=pltpu.CompilerParams(vmem_limit_bytes=40 << 20),
+        name="assemble",
+    )(*heads, *near, *far)
 
 
 def chunk_table(first_rows, span_of, rows_here):
     blocks = span_of.shape[0]
-    device_of = jnp.zeros((blocks,), jnp.int32).at[span_of].set(jnp.arange(blocks, dtype=jnp.int32))
     first = first_rows[0]
     second = rows_here - first
     row = jnp.arange(blocks * rows_here // CHUNK, dtype=jnp.int32) * CHUNK
     later = row >= first * blocks
     inside = jnp.where(later, row - first * blocks, row)
     length = jnp.where(later, jnp.maximum(second, 1), first)
-    span = jnp.minimum(inside // length, blocks - 1)
-    source = device_of[span] * rows_here + jnp.where(later, first, 0) + inside - span * length
+    span = inside // length
+    of_span = (span_of[None, :] == span[:, None]).astype(jnp.int32)
+    device_of = jnp.sum(of_span * jnp.arange(blocks, dtype=jnp.int32)[None, :], axis=1)
+    source = device_of * rows_here + jnp.where(later, first, 0) + inside - span * length
     return jnp.concatenate([source // CHUNK, (first * blocks // TILE)[None]]).astype(jnp.int32)
 
 
@@ -1219,6 +1786,16 @@
     return split.transpose(1, 3, 2, 0, 4).reshape(2 * half_rows, heads * HEAD_DIM)
 
 
+def fold_halves(blocks):
+    n, rows, columns = blocks.shape
+    return blocks.reshape(n, 2, rows // 2, columns).transpose(0, 2, 1, 3).reshape(n, rows // 2, 2 * columns)
+
+
+def unfold_halves(blocks):
+    n, rows, columns = blocks.shape
+    return blocks.reshape(n, rows, 2, columns // 2).transpose(0, 2, 1, 3).reshape(n, 2 * rows, columns // 2)
+
+
 def own_share(vector, index, size):
     return lax.dynamic_slice_in_dim(vector, index * size, size, 0)
 
@@ -1227,15 +1804,22 @@
     return lax.dynamic_update_slice_in_dim(jnp.zeros((whole,), jnp.float32), vector, index * vector.shape[0], 0)
 
 
-def exchange_weights(w_qkv, w_up, blocks):
-    layers, rows, _ = w_qkv.shape
-    width = rows * blocks
-    by_head = w_qkv.reshape(layers, rows, 3, blocks, HEAD_DIM).transpose(3, 1, 0, 2, 4)
-    by_head = by_head[:, :, :, jnp.array([0, 2, 1])].reshape(blocks, rows, -1)
-    by_unit = w_up.reshape(layers, rows, blocks, -1).transpose(2, 1, 0, 3).reshape(blocks, rows, -1)
-    by_head = swap_blocks(by_head, 2).reshape(width, layers, -1)
-    by_unit = lax.all_to_all(by_unit, "blk", 0, 0, tiled=True).reshape(width, layers, -1)
-    return by_head.transpose(1, 0, 2), by_unit.transpose(1, 2, 0)
+def own_units(vector, slot):
+    return lax.dynamic_slice_in_dim(vector.reshape(LINE, PLANE, -1), slot, 1, 1).reshape(-1, 1)
+
+
+def spread_units(column, slot):
+    parts = column.reshape(LINE, 1, -1)
+    whole = jnp.zeros((LINE, PLANE, parts.shape[2]), jnp.float32)
+    return lax.dynamic_update_slice_in_dim(whole, parts, slot, 1).reshape(-1)
+
+
+def add_low(own, other):
+    return (own.astype(jnp.float32) + other.astype(jnp.float32)).astype(jnp.bfloat16)
+
+
+def sum_low(parts):
+    return jnp.sum(parts.astype(jnp.float32), axis=0).astype(jnp.bfloat16)
 
 
 def travel(
@@ -1243,22 +1827,44 @@
 ):
     blocks = lax.axis_size("blk")
     rows_here, row_width = tokens.shape
-    index = lax.axis_index("blk")
+    group, index = lax.axis_index("batch"), lax.axis_index("blk")
     hidden_all = mid_gain.shape[1]
-    hidden = hidden_all // blocks
+    unit_rows = hidden_all // (LINE * PLANE)
+    weight_rows = row_width // blocks
+    slot = lax.rem(index, 4) * 2 + group
     table = chunk_table(first_rows, span_of, rows_here)
-    head_w, unit_w = exchange_weights(w_qkv, w_up, blocks)
+    scales = [own_share(head_scale[layer], index, 1).reshape(1, 1) for layer in range(2)]
+    middle_gain = [own_units(mid_gain[layer], slot) for layer in range(2)]
+    middle_shift = [own_units(mid_bias[layer, 0], slot) for layer in range(2)]
+    middle_bias = [own_units(mid_bias[layer, 1], slot) for layer in range(2)]
+    by_head, by_unit, own_down = [], [], []
+    for layer in range(2):
+        split = w_qkv[layer].reshape(weight_rows, 3, blocks, HEAD_DIM)
+        split = jnp.stack([split[:, 0], split[:, 2], split[:, 1]], axis=1).transpose(2, 0, 1, 3)
+        by_head.append(fold_halves(split.reshape(blocks, weight_rows, 3 * HEAD_DIM)))
+        split = w_up[layer].reshape(weight_rows, LINE, 4, 2, unit_rows)
+        split = lax.dynamic_slice_in_dim(split, group, 1, 3).reshape(weight_rows, LINE, 4, unit_rows)
+        by_unit.append(split.transpose(2, 0, 1, 3).reshape(4, weight_rows, LINE * unit_rows))
+        own_down.append(lax.dynamic_slice_in_dim(w_down[layer].reshape(2, unit_rows, row_width), group, 1, 0))
+    head_w, up_w, down_w = [None] * 2, [None] * 2, [None] * 2
+
+    def set_weights(layer, head_blocks, unit_blocks, down_blocks):
+        head_w[layer] = unfold_halves(head_blocks).reshape(row_width, -1)
+        up_w[layer] = unit_blocks.reshape(row_width, -1).T
+        down_w[layer] = down_blocks.reshape(-1, row_width)
+
     out_w = [lax.all_gather(w_out[layer], "blk", axis=0, tiled=True) for layer in range(2)]
-    scales = [own_share(head_scale[layer], index, 1).reshape(1, 1) for layer in range(2)]
-    middle_gain = [own_share(mid_gain[layer], index, hidden)[:, None] for layer in range(2)]
-    middle_shift = [own_share(mid_bias[layer, 0], index, hidden)[:, None] for layer in range(2)]
-    middle_bias = [own_share(mid_bias[layer, 1], index, hidden)[:, None] for layer in range(2)]
     current = tokens.astype(jnp.float32)
     records = []
     for layer in range(2):
         gains, biases = vec_gain[layer], vec_bias[layer]
         normed, pre_pull = jax.vjp(norm_rows, current, gains[0], biases[0])
-        normed_all = gather_rows(normed.astype(jnp.bfloat16), 0)
+        normed_low = normed.astype(jnp.bfloat16)
+        if layer == 0:
+            normed_all, *got = gather_rows(normed_low, 0, [(Swap, by_head[0]), (Swap, by_unit[0]), (Trade, own_down[0])])
+            set_weights(0, *got)
+        else:
+            (normed_all,) = gather_rows(normed_low, 1)
         head_bias = jnp.concatenate(
             [
                 own_share(biases[3], index, HEAD_DIM),
@@ -1267,48 +1873,66 @@
             ]
         )[None]
         qvk, lse, head_out, packed = attend(table, normed_all, head_w[layer], head_bias, scales[layer])
-        scaled_low = unpack_rows(swap_blocks(packed.reshape(blocks, rows_here // 2, 128), 3))
+        (mixed,) = swap_blocks(packed.reshape(blocks, rows_here // 2, 128), 2)
+        scaled_low = unpack_rows(mixed)
         branch = jnp.dot(scaled_low, out_w[layer], preferred_element_type=jnp.float32) + biases[5]
         post_normed, post_pull = jax.vjp(norm_rows, branch, gains[1], biases[1])
         middle_res = current + post_normed
         ffn_normed, ffn_pull = jax.vjp(norm_rows, middle_res, gains[2], biases[2])
-        ffn_all = gather_rows(ffn_normed.astype(jnp.bfloat16), 0)
-        act, slope, stat = up(ffn_all, unit_w[layer], middle_bias[layer])
-        stat = pool_rows(stat, hidden, 4)
-        parts, mid_low = down(hidden_all, act, stat, middle_gain[layer], middle_shift[layer], w_down[layer])
-        current = middle_res + (scatter_rows(parts, 1) + biases[6])
+        rides = [(Swap, by_head[1]), (Swap, by_unit[1]), (Trade, own_down[1])] if layer == 0 else []
+        results, ffn_all, act, slope, stat, mid_low, *got = ffn(
+            hidden_all, ffn_normed.astype(jnp.bfloat16), up_w[layer], middle_bias[layer], middle_gain[layer],
+            middle_shift[layer], down_w[layer], 3 + layer, rides,
+        )
+        if layer == 0:
+            set_weights(1, *got)
+        current = middle_res + (results + biases[6])
         records.append(
             (pre_pull, post_pull, ffn_pull, normed_all, ffn_all, qvk, lse, head_out, scaled_low, act, slope, stat, mid_low)
         )
     results_low = current.astype(jnp.bfloat16)
     d_current = grad_out.astype(jnp.float32)
-    head_grads, unit_grads, out_grads, down_grads = [None] * 2, [None] * 2, [None] * 2, [None] * 2
-    small = [None] * 2
+    head_grads, out_grads = [None] * 2, [None] * 2
+    near_units, far_units, near_downs, far_downs = [None] * 2, [None] * 2, [None] * 2, [None] * 2
+    vectors, middles, scale_grads = [None] * 2, [None] * 2, [None] * 2
     for layer in (1, 0):
         pre_pull, post_pull, ffn_pull, normed_all, ffn_all, qvk, lse, head_out, scaled_low, act, slope, stat, mid_low = records[layer]
         d_low = d_current.astype(jnp.bfloat16)
-        d_all = gather_rows(d_low, 0)
-        dmid, sums, down_grads[layer], grad_mid_gain, grad_mid_shift = down_back(
-            hidden_all, d_all, w_down[layer], act, stat, middle_gain[layer], mid_low
+        rides = [] if layer == 1 else [(Swap, head_blocks), (Swap, unit_grad), (Trade, down_grad)]
+        d_ffn, down_grad, unit_grad, grad_mid_gain, grad_mid_shift, grad_up_bias, *got = ffn_back(
+            hidden_all, d_low, up_w[layer], middle_gain[layer], down_w[layer], stat, ffn_all, act, slope, mid_low,
+            5 + layer, rides,
         )
-        sums = pool_rows(sums, None, 5)
-        parts, unit_grads[layer], grad_up_bias = up_back(
-            hidden_all, dmid, act, slope, stat, sums, middle_gain[layer], ffn_all, unit_w[layer]
-        )
-        d_res_part, grad_gain_ffn, grad_shift_ffn = ffn_pull(scatter_rows(parts, 1))
+        down_grad = down_grad.reshape(LINE, unit_rows, row_width)
+        unit_grad = unit_grad.reshape(blocks, weight_rows, LINE * unit_rows)
+        if layer == 0:
+            head_grads[1] = unfold_halves(got[0])
+            near_units[1] = sum_low(got[1].reshape(LINE, 4, weight_rows, LINE * unit_rows))
+            near_downs[1] = sum_low(got[2])
+        d_res_part, grad_gain_ffn, grad_shift_ffn = ffn_pull(d_ffn)
         d_middle_res = d_current + d_res_part
         d_branch, grad_gain_post, grad_shift_post = post_pull(d_middle_res)
         d_branch_low = d_branch.astype(jnp.bfloat16)
         d_scaled = jnp.einsum("td,cd->tc", d_branch_low, out_w[layer], preferred_element_type=jnp.float32)
         out_grad = jnp.einsum("tc,td->cd", scaled_low, d_branch_low, preferred_element_type=jnp.float32)
         out_grads[layer] = lax.psum_scatter(out_grad.astype(jnp.bfloat16), "blk", scatter_dimension=0, tiled=True)
-        d_heads = swap_blocks(pack_rows(d_scaled.astype(jnp.bfloat16)), 3).reshape(-1, 128)
-        parts, head_grads[layer], head_bias, grad_scale = attend_back(
-            table, d_heads, normed_all, head_w[layer], scales[layer], qvk, lse, head_out
+        (d_heads,) = swap_blocks(pack_rows(d_scaled.astype(jnp.bfloat16)), 2)
+        parts, head_grad, head_bias, grad_scale = attend_back(
+            table, d_heads.reshape(-1, 128), normed_all, head_w[layer], scales[layer], qvk, lse, head_out
         )
-        d_in_part, grad_gain_pre, grad_shift_pre = pre_pull(scatter_rows(parts, 1))
+        if layer == 1:
+            d_in, other_head = scatter_rows(parts, 7, [(Cross, head_grad)])
+        else:
+            d_in, other_head, far_units[1], far_downs[1], unit_blocks, down_blocks = scatter_rows(
+                parts, 8,
+                [(Cross, head_grad), (Cross, near_units[1]), (Cross, near_downs[1]), (Swap, unit_grad), (Trade, down_grad)],
+            )
+            near_units[0] = sum_low(unit_blocks.reshape(LINE, 4, weight_rows, LINE * unit_rows))
+            near_downs[0] = sum_low(down_blocks)
+        head_blocks = fold_halves(add_low(head_grad, other_head).reshape(blocks, weight_rows, 3 * HEAD_DIM))
+        d_in_part, grad_gain_pre, grad_shift_pre = pre_pull(d_in)
         d_current = d_middle_res + d_in_part
-        small[layer] = jnp.concatenate(
+        vectors[layer] = jnp.stack(
             [
                 grad_gain_pre,
                 grad_gain_post,
@@ -1320,25 +1944,31 @@
                 spread(head_bias[0, HEAD_DIM : 2 * HEAD_DIM], index, row_width),
                 jnp.sum(d_branch_low, axis=0, dtype=jnp.float32),
                 jnp.sum(d_low, axis=0, dtype=jnp.float32),
-                spread(grad_mid_gain[:, 0], index, hidden_all),
-                spread(grad_mid_shift[:, 0], index, hidden_all),
-                spread(grad_up_bias[:, 0], index, hidden_all),
-                spread(grad_scale[0], index, blocks),
             ]
         )
-    small = lax.psum(jnp.stack(small), ("batch", "blk"))
-    turned = [jnp.concatenate([head_grads[layer], unit_grads[layer]], axis=0).astype(jnp.bfloat16) for layer in range(2)]
-    turned = lax.psum(jnp.stack(turned), "batch")
-    turned = turned.reshape(2, -1, blocks, row_width // blocks).transpose(2, 0, 3, 1)
-    turned = lax.all_to_all(turned, "blk", 0, 0, tiled=True).astype(jnp.float32)
-    heads_back = turned[..., : 3 * HEAD_DIM].reshape(blocks, 2, -1, 3, HEAD_DIM)[:, :, :, jnp.array([0, 2, 1])]
-    grad_qkv = heads_back.transpose(1, 2, 3, 0, 4).reshape(w_qkv.shape)
-    grad_up = turned[..., 3 * HEAD_DIM :].transpose(1, 2, 0, 3).reshape(w_up.shape)
-    grad_out_w = lax.psum(jnp.stack(out_grads), "batch").astype(jnp.float32)
-    grad_down = lax.psum(jnp.stack(down_grads).astype(jnp.bfloat16), "batch").astype(jnp.float32)
-    vec_end = 10 * row_width
-    vectors = small[:, :vec_end].reshape(2, 10, row_width)
-    middles = small[:, vec_end : vec_end + 3 * hidden_all].reshape(2, 3, hidden_all)
+        middles[layer] = jnp.stack([spread_units(g, slot) for g in (grad_mid_gain, grad_mid_shift, grad_up_bias)])
+        scale_grads[layer] = spread(grad_scale[0], index, blocks)
+    scale_row = jnp.zeros((row_width,), jnp.float32).at[: 2 * blocks].set(jnp.concatenate(scale_grads))
+    summed = jnp.concatenate([jnp.stack(vectors).reshape(-1), jnp.stack(middles).reshape(-1), scale_row])
+    summed = jnp.pad(summed, (0, -summed.shape[0] % (16 * row_width))).reshape(-1, row_width)
+    out_near = jnp.concatenate(out_grads)
+    summed, head_got, out_far, far_units[0], far_downs[0] = finale(
+        summed.astype(jnp.bfloat16), 9,
+        [(Swap, head_blocks), (Cross, out_near), (Cross, near_units[0]), (Cross, near_downs[0])],
+    )
+    head_grads[0] = unfold_halves(head_got)
+    grad_out_w = (out_near.astype(jnp.float32) + out_far.astype(jnp.float32)).reshape(w_out.shape)
+    grad_qkv, grad_up = assemble(head_grads, near_units, far_units, w_qkv.shape, w_up.shape)
+    near_down, far_down = jnp.stack(near_downs).astype(jnp.float32), jnp.stack(far_downs).astype(jnp.float32)
+    grad_down = jnp.where(
+        group == 0,
+        jnp.concatenate([near_down, far_down], axis=1),
+        jnp.concatenate([far_down, near_down], axis=1),
+    )
+    summed = summed.reshape(-1)
+    vec_end, mid_end = 20 * row_width, 20 * row_width + 6 * hidden_all
+    vectors = summed[:vec_end].reshape(2, 10, row_width)
+    middles = summed[vec_end:mid_end].reshape(2, 3, hidden_all)
     return (
         results_low,
         d_current,
@@ -1350,7 +1980,7 @@
         vectors[:, 3:],
         middles[:, 0],
         middles[:, 1:],
-        small[:, vec_end + 3 * hidden_all :],
+        summed[mid_end : mid_end + 2 * blocks].reshape(2, blocks),
     )
 
 
@@ -1358,7 +1988,7 @@
     tokens, w_qkv = args[0], args[4]
     blocks = lax.axis_size("blk")
     heads = w_qkv.shape[2] // (3 * HEAD_DIM)
-    if blocks == heads and blocks == 4 * LINE and tokens.shape[0] * blocks % TILE == 0:
+    if blocks == heads == 4 * LINE and lax.axis_size("batch") == 2 and tokens.shape[0] * blocks % TILE == 0:
         return travel(*args)
     return general(*args)
 

time: 1180 us -> 829 us (0.70)
  waiting for transfers between devices: 268 us -> 52.1 us
  Pallas kernels: 707 us -> 606 us
  local copies, waits for them, and re-layouts: 119 us -> 83.2 us
  starting transfers between devices: 13.5 us -> 0.16 us
    psum x2 -> x0, waiting for transfers between devices: 231 us -> none  [the longest x1 142 us: travel(): small = lax.psum(jnp.stack(small), ('batch', 'blk'))]
    pallas_call x29 -> x14, Pallas kernels: 625 us -> 542 us  [the longest x2 144 us: gather_rows(): pl.pallas_call(functools.partial(gather_kernel, rides), out_shape=[jax.Sh...]
    reduce_scatter x2, waiting for transfers between devices: 36.7 us -> 51.3 us  [travel(): lax.psum_scatter(out_grad.astype(jnp.bfloat16), 'blk', scatter_dimension=...]
    unnamed x228 -> x274, local copies, waits for them, and re-layouts: 39 us -> 24.9 us
    all_to_all x2 -> x0, starting transfers between devices: 13.2 us -> none  [the longest x1 7.44 us: exchange_weights(): lax.all_to_all(by_unit, 'blk', 0, 0, tiled=True).reshape(width, layers, -1)]
  transfers between devices with their start and end apart: 8 -> 4, of which waited for: 3 -> 1; matrix products, arithmetic and copies ran while one was open for 7% -> 9% of each run, Pallas kernels for 32% -> 45%
where the time goes in v2:
time: 829 us; the launch traced here: 814 us
  Pallas kernels  606 us (73%)
  local copies, waits for them, and re-layouts  83.2 us (10%)
  waiting for transfers between devices  52.1 us (6%)
  other arithmetic  45.2 us (5%)
  between operations  17.1 us (2%)
  matrix products  10.3 us (1%)
    pallas_call x2, Pallas kernels, gather_rows(): pl.pallas_call(functools.partial(gather_kernel, rides), out_shape=[jax.Sh...  144 us
    pallas_call x2, Pallas kernels, scatter_rows(): pl.pallas_call(functools.partial(scatter_kernel, rides), out_shape=[jax.S...  116 us
    pallas_call x2, Pallas kernels, ffn(): pl.pallas_call(functools.partial(ffn_kernel, hidden_all, rides), out_shap...  106 us
    pallas_call x2, Pallas kernels, ffn_back(): pl.pallas_call(functools.partial(ffn_back_kernel, hidden_all, rides), out...  99.8 us
    reduce_scatter x2, waiting for transfers between devices, travel(): lax.psum_scatter(out_grad.astype(jnp.bfloat16), 'blk', scatter_dimension=...  51.3 us
    pallas_call x4, Pallas kernels, swap_blocks(): pl.pallas_call(functools.partial(swap_kernel, rides), out_shape=rides.res...  47.9 us
    pallas_call x2, Pallas kernels, attend_back(): pl.pallas_call(attend_back_kernel, out_shape=(jax.ShapeDtypeStruct((total...  39.7 us
    pallas_call x1, Pallas kernels, finale(): pl.pallas_call(functools.partial(finale_kernel, rides), out_shape=[jax.Sh...  25.9 us
  transfers between devices with their start and end apart: 4, of which 1 were waited for; matrix products, arithmetic and copies ran while one was open for 9% of the time, Pallas kernels for 45%

profile of v2, /device:TPU:0, one launch (start us, length us, event | category | flops | bytes accessed | tf_op | source)
XLA Modules:
  0.0 814.0 jit_solution(11476552380729854255)
XLA Ops:
  7.2 1.8 fusion.77
  10.5 1.5 fusion.79
  12.0 1.4 fusion.81
  18.7 2.1 fusion.72
  20.8 1.9 fusion.75
  24.9 2.2 maximum_bitcast_fusion
  31.1 108.6 %gather_rows.2 = (bf16[2560,1024]{1,0:T(8,128)(2,1)}, bf16[16,32,384]{2,1,0:T(8,128)(2,1)}, bf16[16,64,512]{2,1,0:T(8,128)(2,1)}, bf16[4,128,1024]{2,1,0:T(8,128)(2,1)}) custom-call(bf16[160,1024]{1,0:T(8,128)(2,1)} %fusion.27.refs_0_, bf16[16,32,384]{2,1,0:T(8,128)(2,1)} %reshape.499.refs_1_, bf16[4,64,512]{2,1,0:T(8,128)(2,1)} %reshape.501.refs_2_, ...), custom_call_target="tpu_custom_call" | custom-call | bytes 105000000 | tf_op jit(solution)/shard_map/gather_rows/pallas_call | solution.py:778
  142.6 12.3 %attend.2 = (bf16[2560,192]{1,0:T(8,128)(2,1)S(1)}, f32[1,2560]{1,0:T(1,128)S(1)}, f32[64,2560]{1,0:T(8,128)S(1)}, bf16[1280,128]{1,0:T(8,128)(2,1)S(1)}) custom-call(s32[81]{0:T(128)S(1)} %pad_add_fusion.table, bf16[2560,1024]{1,0:T(8,128)(2,1)} %get-tuple-element.88.x_ref, bf16[1024,192]{1,0:T(8,128)(2,1)S(1)} %bitcast.200, f32[1,192]{1,0:T(1,128)S(1)} %bitcast.216, ...), custom_call_target="tpu_custom_call" | custom-call | bytes 38500000 | tf_op jit(solution)/shard_map/attend/pallas_call | solution.py:1110
  158.2 9.7 %swap_blocks.4 = bf16[16,80,128]{2,1,0:T(8,128)(2,1)} custom-call(bf16[16,80,128]{2,1,0:T(8,128)(2,1)} %bitcast.212), custom_call_target="tpu_custom_call" | custom-call | bytes 35000000 | tf_op jit(solution)/shard_map/swap_blocks/pallas_call | solution.py:945
  170.3 2.3 copy.95
  172.9 1.5 reshape_squeeze.42
  176.1 3.1 maximum_bitcast_fusion.1
  179.2 2.5 reshape_reshape.20
  184.9 2.2 fusion.85
  188.7 63.0 %ffn.2 = (f32[160,1024]{1,0:T(8,128)S(1)}, bf16[1280,1024]{1,0:T(8,128)(2,1)}, f32[512,1280]{1,0:T(8,128)}, f32[512,1280]{1,0:T(8,128)}, f32[2,1280]{1,0:T(2,128...) custom-call(bf16[160,1024]{1,0:T(8,128)(2,1)S(1)} %add_convert_fusio, ...), custom_call_target="tpu_custom_call" | custom-call | bytes 140000000 | tf_op jit(solution)/shard_map/ffn/pallas_call | solution.py:1561
  253.6 35.4 %gather_rows.3.x_ref = bf16[2560,1024]{1,0:T(8,128)(2,1)} custom-call(bf16[160,1024]{1,0:T(8,128)(2,1)} %add_convert_fusion.6.refs_0_), custom_call_target="tpu_custom_call" | custom-call | bytes 105000000 | tf_op jit(solution)/shard_map/gather_rows/pallas_call | solution.py:778
  289.4 12.2 %attend.3 = (bf16[2560,192]{1,0:T(8,128)(2,1)S(1)}, f32[1,2560]{1,0:T(1,128)S(1)}, f32[64,2560]{1,0:T(8,128)S(1)}, bf16[1280,128]{1,0:T(8,128)(2,1)S(1)}) custom-call(s32[81]{0:T(128)S(1)} %pad_add_fusion.table, bf16[2560,1024]{1,0:T(8,128)(2,1)} %gather_rows.3.x_ref, bf16[1024,192]{1,0:T(8,128)(2,1)S(1)} %bitcast.202, f32[1,192]{1,0:T(1,128)S(1)} %bitcast.215, ...), custom_call_target="tpu_custom_call" | custom-call | bytes 38500000 | tf_op jit(solution)/shard_map/attend/pallas_call | solution.py:1110
  304.9 12.6 %swap_blocks.5 = bf16[16,80,128]{2,1,0:T(8,128)(2,1)} custom-call(bf16[16,80,128]{2,1,0:T(8,128)(2,1)} %bitcast.213), custom_call_target="tpu_custom_call" | custom-call | bytes 35000000 | tf_op jit(solution)/shard_map/swap_blocks/pallas_call | solution.py:945
  319.5 2.3 fusion.86
  323.9 1.5 copy.109
  325.4 1.7 add_convert_fusion.5.refs_0_
  327.1 42.8 %ffn.3 = (f32[160,1024]{1,0:T(8,128)S(1)}, bf16[1280,1024]{1,0:T(8,128)(2,1)}, f32[512,1280]{1,0:T(8,128)}, f32[512,1280]{1,0:T(8,128)}, f32[2,1280]{1,0:T(2,128)S(1)}, /*index=5*/bf16[512,1280]{1,0:T(8,128)(2,1)}) custom-call(bf16[160,1024]{1,0:T(8,128)(2,1)S(1)} %add_convert_fusion.5.refs_0_, bf16[512,1024]{1,0:T(8,128)(2,1)S(1)} %bitcast.198, ...), custom_call_target="tpu_custom_call" | custom-call | bytes 140000000 | tf_op jit(solution)/shard_map/ffn/pallas_call | solution.py:1561
  370.5 40.5 %ffn_back.2 = (f32[160,1024]{1,0:T(8,128)}, bf16[512,1024]{1,0:T(8,128)(2,1)}, bf16[1024,512]{1,0:T(8,128)(2,1)}, f32[512,1]{1,0:T(8,128)}, f32[512,1]{1,0:T(8,128)}, /*index=5*/f32[512,1]{1,0:T(8,128)}) custom-call(bf16[160,1024]{1,0:T(8,128)(2,1)} %refs_0_, bf16[512,1024]{1,0:T(8,128)(2,1)} %bitcast.199, f32[512,1]{1,0:T(8,128)} %copy-done.7, ...), custom_call_target="tpu_custom_call" | custom-call | bytes 157500000 | tf_op jit(solution)/shard_map/ffn_back/pallas_call | solution.py:1702
  411.0 2.1 multiply_reduce_fusion
  413.1 2.1 fusion.68
  420.3 11.0 %swap_blocks.6 = bf16[16,80,128]{2,1,0:T(8,128)(2,1)} custom-call(bf16[16,80,128]{2,1,0:T(8,128)(2,1)} %reshape.524.refs_0_), custom_call_target="tpu_custom_call" | custom-call | bytes 35000000 | tf_op jit(solution)/shard_map/swap_blocks/pallas_call | solution.py:945
  431.3 19.8 %attend_back.2 = (bf16[2560,1024]{1,0:T(8,128)(2,1)}, bf16[1024,192]{1,0:T(8,128)(2,1)}, f32[1,192]{1,0:T(1,128)}, f32[1,1]{1,0:T(1,128)}) custom-call(s32[81]{0:T(128)} %copy-done.28, bf16[1280,128]{1,0:T(8,128)(2,1)} %bitcast.233, bf16[2560,1024]{1,0:T(8,128)(2,1)} %gather_rows.3.x_ref, bf16[1024,192]{1,0:T(8,128)(2,1)} %bitcast.203, ...), custom_call_target="tpu_custom_call" | custom-call | bytes 66500000 | tf_op jit(solution)/shard_map/attend_back/pallas_call | solution.py:1212
  451.1 2.5 copy-done.1
  454.6 41.0 %scatter_rows.2 = (f32[160,1024]{1,0:T(8,128)S(1)}, bf16[1024,192]{1,0:T(8,128)(2,1)S(1)}) custom-call(bf16[2560,1024]{1,0:T(8,128)(2,1)S(1)} %copy-done.1, bf16[1024,192]{1,0:T(8,128)(2,1)S(1)} %copy-done.11), custom_call_target="tpu_custom_call" | custom-call | bytes 112000000 | tf_op jit(solution)/shard_map/scatter_rows/pallas_call | solution.py:919
  497.1 2.1 reshape.526.refs_9_
  500.4 1.5 fusion.60
  501.9 59.4 %ffn_back.3 = (f32[160,1024]{1,0:T(8,128)}, bf16[512,1024]{1,0:T(8,128)(2,1)}, bf16[1024,512]{1,0:T(8,128)(2,1)}, f32[512,1]{1,0:T(8,128)}, f32[512,1]{1,0:T(8,1...) custom-call(bf16[160,1024]{1,0:T(8,128)(2,1)} %get-tuple-element.195, ...), custom_call_target="tpu_custom_call" | custom-call | bytes 157500000 | tf_op jit(solution)/shard_map/ffn_back/pallas_call | solution.py:1702
  561.3 2.1 multiply_reduce_fusion.3
  563.4 1.4 fusion.65
  567.1 2.1 convolution_convert_fusion.1
  572.3 14.7 %swap_blocks.7 = bf16[16,80,128]{2,1,0:T(8,128)(2,1)} custom-call(bf16[16,80,128]{2,1,0:T(8,128)(2,1)} %reshape.530.refs_0_), custom_call_target="tpu_custom_call" | custom-call | bytes 35000000 | tf_op jit(solution)/shard_map/swap_blocks/pallas_call | solution.py:945
  587.4 19.9 %attend_back.3 = (bf16[2560,1024]{1,0:T(8,128)(2,1)}, bf16[1024,192]{1,0:T(8,128)(2,1)}, f32[1,192]{1,0:T(1,128)}, f32[1,1]{1,0:T(1,128)}) custom-call(s32[81]{0:T(128)} %copy-done.28, bf16[1280,128]{1,0:T(8,128)(2,1)} %bitcast.232, bf16[2560,1024]{1,0:T(8,128)(2,1)} %get-tuple-element.88.x_ref, bf16[1024,192]{1,0:T(8,128)(2,1)} %bitcast.201, ...), custom_call_target="tpu_custom_call" | custom-call | bytes 66500000 | tf_op jit(solution)/shard_map/attend_back/pallas_call | solution.py:1212
  607.4 2.5 copy-done.2
  610.9 74.8 %scatter_rows.3 = (f32[160,1024]{1,0:T(8,128)S(1)}, bf16[1024,192]{1,0:T(8,128)(2,1)S(1)}, bf16[4,64,512]{2,1,0:T(8,128)(2,1)S(1)}, bf16[128,1024]{1,0:T(8,128)(...) custom-call(bf16[2560,1024]{1,0:T(8,128)(2,1)S(1)} %copy-done.2, ...), custom_call_target="tpu_custom_call" | custom-call | bytes 112000000 | tf_op jit(solution)/shard_map/scatter_rows/pallas_call | solution.py:919
  687.4 2.2 reduce_sum.557.refs_4_
  691.3 2.1 reshape.555.refs_1_
  696.2 2.1 convolution_convert_fusion
  709.6 2.0 maximum_convert_fusion
  713.7 51.3 %reduce-scatter.5.cloned.1.call-done = bf16[64,1024]{1,0:T(8,128)(2,1)} async-done(((bf16[1024,1024]{1,0:T(8,128)(2,1)}), bf16[64,1024]{1,0:T(8,128)(2,1)}) %reduce-scatter.5.cloned.1.call-update) | async-done | bytes 131088 | tf_op jit(solution)/shard_map/reduce_scatter | solution.py:1918
  766.6 25.9 %finale.1 = (f32[48,1024]{1,0:T(8,128)}, bf16[16,32,384]{2,1,0:T(8,128)(2,1)}, bf16[128,1024]{1,0:T(8,128)(2,1)}, bf16[4,64,512]{2,1,0:T(8,128)(2,1)}, bf16[128,1024]{1,0:T(8,128)(2,1)}) custom-call(bf16[48,1024]{1,0:T(8,128)(2,1)} %convert_element_type.115.refs_0_, bf16[16,32,384]{2,1,0:T(8,128)(2,1)} %reshape.555.refs_1_, bf16[128,1024]{1,0:T(8,128)(2,1)} %copy-done.52, ...), custom_call_target="tpu_custom_call" | custom-call | bytes 63000000 | tf_op jit(solution)/shard_map/finale/pallas_call | solution.py:1004
  792.6 2.7 slice.271
  803.4 1.5 maximum_select_fusion
  804.9 2.3 assemble.1
  (478 shorter events, 81.0 us)
Async XLA Ops:
  7.2 8.6 %copy-start.57 = (bf16[2,64,4096]{2,1,0:T(8,128)(2,1)S(1)}, bf16[2,64,4096]{2,1,0:T(8,128)(2,1)}, u32[]{:S(2)}) copy-start(bf16[2,64,4096]{2,1,0:T(8,128)(2,1)} %param.21) | copy-start | bytes 3145732
  7.2 177.7 %all-gather.5.cloned.1.call-start = ((), (), s32[]{:S(2)}) async-start(), calls=%async_computation.4 | async-start | bytes 2228224 | tf_op jit(solution)/shard_map/all_gather | solution.py:1856
  9.0 310.5 %all-gather.7.cloned.1.call-start = ((), (), s32[]{:S(2)}) async-start(), calls=%async_computation.5 | async-start | bytes 2228224 | tf_op jit(solution)/shard_map/all_gather | solution.py:1856
  9.8 703.0 %reduce-scatter.3.cloned.1.call-start = ((), (), s32[]{:S(2)}) async-start(), calls=%async_computation.2 | async-start | bytes 2228224 | tf_op jit(solution)/shard_map/reduce_scatter | solution.py:1918
  14.5 15.5 %copy-start.69 = (f32[160]{0:T(256)}, f32[160]{0:T(256)S(1)}, u32[]{:S(2)}) copy-start(f32[160]{0:T(256)S(1)} %broadcast_multiply_fusion.5) | copy-start | bytes 1924
  15.8 14.3 %copy-start.91 = (f32[160]{0:T(256)}, f32[160]{0:T(256)S(1)}, u32[]{:S(2)}) copy-start(f32[160]{0:T(256)S(1)} %fusion.46) | copy-start | bytes 1924
  30.0 111.1 %copy-start.129 = (f32[2,16]{1,0:T(2,128)S(1)}, f32[2,16]{1,0:T(2,128)}, u32[]{:S(2)}) copy-start(f32[2,16]{1,0:T(2,128)} %param.27) | copy-start | bytes 388
  30.0 111.1 %copy-start.68 = (f32[2,2,4096]{2,1,0:T(2,128)S(1)}, f32[2,2,4096]{2,1,0:T(2,128)}, u32[]{:S(2)}) copy-start(f32[2,2,4096]{2,1,0:T(2,128)} %param.26) | copy-start | bytes 196612
  30.0 111.1 %copy-start.71 = (f32[2,4096]{1,0:T(2,128)S(1)}, f32[2,4096]{1,0:T(2,128)}, u32[]{:S(2)}) copy-start(f32[2,4096]{1,0:T(2,128)} %param.25) | copy-start | bytes 98308
  30.0 111.3 %copy-start.131 = (s32[16]{0:T(128)S(1)}, s32[16]{0:T(128)}, u32[]{:S(2)}) copy-start(s32[16]{0:T(128)} %param.18) | copy-start | bytes 196
  141.1 13.8 %copy-start.3 = (bf16[16,32,2,192]{3,1,2,0:T(8,128)(2,1)}, bf16[16,32,2,192]{3,1,2,0:T(8,128)(2,1)S(1)}, u32[]{:S(2)}) copy-start(bf16[16,32,2,192]{3,1,2,0:T(8,128)(2,1)S(1)} %copy.93) | copy-start | bytes 1179652
  142.6 146.8 %copy-start.28 = (s32[81]{0:T(128)}, s32[81]{0:T(128)S(1)}, u32[]{:S(2)}) copy-start(s32[81]{0:T(128)S(1)} %pad_add_fusion.table) | copy-start | bytes 976
  169.8 15.1 %copy-start.48 = (bf16[160,1024]{1,0:T(8,128)(2,1)}, bf16[160,1024]{1,0:T(8,128)(2,1)S(1)}, u32[]{:S(2)}) copy-start(bf16[160,1024]{1,0:T(8,128)(2,1)S(1)} %reshape.505) | copy-start | bytes 983044
  170.2 18.6 %copy-start.6 = (f32[512,1]{1,0:T(8,128)}, f32[512,1]{1,0:T(8,128)S(1)}, u32[]{:S(2)}) copy-start(f32[512,1]{1,0:T(8,128)S(1)} %copy.105.refs_3_.refs_2_) | copy-start | bytes 6148
  184.7 142.3 %copy-start.7 = (f32[512,1]{1,0:T(8,128)}, f32[512,1]{1,0:T(8,128)S(1)}, u32[]{:S(2)}) copy-start(f32[512,1]{1,0:T(8,128)S(1)} %copy.114.refs_3_.refs_2_) | copy-start | bytes 6148
  188.4 63.4 %copy-start.88 = (f32[1,1,1024]{2,0,1:T(1,128)S(1)}, f32[1,1,1024]{2,0,1:T(1,128)}, u32[]{:S(2)}) copy-start(f32[1,1,1024]{2,0,1:T(1,128)} %get-tuple-element.243) | copy-start | bytes 12292
  252.4 70.3 %copy-start.29 = (f32[160,1024]{1,0:T(8,128)}, f32[160,1024]{1,0:T(8,128)S(1)}, u32[]{:S(2)}) copy-start(f32[160,1024]{1,0:T(8,128)S(1)} %get-tuple-element.215) | copy-start | bytes 1966084
  252.4 36.6 %copy-start.78 = (f32[160]{0:T(256)}, f32[160]{0:T(256)S(1)}, u32[]{:S(2)}) copy-start(f32[160]{0:T(256)S(1)} %broadcast_multiply_fusion.2) | copy-start | bytes 1924
  252.6 36.4 %copy-start.106 = (f32[160]{0:T(256)}, f32[160]{0:T(256)S(1)}, u32[]{:S(2)}) copy-start(f32[160]{0:T(256)S(1)} %multiply_reduce_fusion.12) | copy-start | bytes 1924
  252.6 36.4 %copy-start.97 = (f32[160]{0:T(256)}, f32[160]{0:T(256)S(1)}, u32[]{:S(2)}) copy-start(f32[160]{0:T(256)S(1)} %fusion.49) | copy-start | bytes 1924
  289.4 12.3 %copy-start.4 = (bf16[16,32,2,192]{3,1,2,0:T(8,128)(2,1)}, bf16[16,32,2,192]{3,1,2,0:T(8,128)(2,1)S(1)}, u32[]{:S(2)}) copy-start(bf16[16,32,2,192]{3,1,2,0:T(8,128)(2,1)S(1)} %copy.107) | copy-start | bytes 1179652
  304.9 14.6 %copy-start.86 = (f32[1,1,1024]{2,0,1:T(1,128)S(1)}, f32[1,1,1024]{2,0,1:T(1,128)}, u32[]{:S(2)}) copy-start(f32[1,1,1024]{2,0,1:T(1,128)} %get-tuple-element.239) | copy-start | bytes 12292
  325.4 44.5 %copy-start = (bf16[1024,512]{0,1:T(8,128)(2,1)}, bf16[1024,512]{0,1:T(8,128)(2,1)S(1)}, u32[]{:S(2)}) copy-start(bf16[1024,512]{0,1:T(8,128)(2,1)S(1)} %copy.109) | copy-start | bytes 3145732
  370.4 40.5 %copy-start.32 = (f32[160,1024]{1,0:T(8,128)S(1)}, f32[160,1024]{1,0:T(8,128)}, u32[]{:S(2)}) copy-start(f32[160,1024]{1,0:T(8,128)} %copy-done.31) | copy-start | bytes 1966084
  370.4 40.5 %copy-start.81 = (f32[160]{0:T(256)S(1)}, f32[160]{0:T(256)}, u32[]{:S(2)}) copy-start(f32[160]{0:T(256)} %copy-done.80) | copy-start | bytes 1924
  370.4 40.5 %copy-start.99 = (f32[160]{0:T(256)S(1)}, f32[160]{0:T(256)}, u32[]{:S(2)}) copy-start(f32[160]{0:T(256)} %fusion.51) | copy-start | bytes 1924
  370.4 42.6 %copy-start.111 = (f32[160]{0:T(256)S(1)}, f32[160]{0:T(256)}, u32[]{:S(2)}) copy-start(f32[160]{0:T(256)} %copy-done.110) | copy-start | bytes 1924
  370.5 42.6 %copy-start.84 = (f32[1,1,1024]{2,0,1:T(1,128)S(1)}, f32[1,1,1024]{2,0,1:T(1,128)}, u32[]{:S(2)}) copy-start(f32[1,1,1024]{2,0,1:T(1,128)} %get-tuple-element.237) | copy-start | bytes 12292
  501.9 59.4 %copy-start.63 = (f32[1,1,1024]{2,0,1:T(1,128)S(1)}, f32[1,1,1024]{2,0,1:T(1,128)}, u32[]{:S(2)}) copy-start(f32[1,1,1024]{2,0,1:T(1,128)} %get-tuple-element.255) | copy-start | bytes 12292
  501.9 59.4 %copy-start.77 = (f32[160]{0:T(256)S(1)}, f32[160]{0:T(256)}, u32[]{:S(2)}) copy-start(f32[160]{0:T(256)} %copy-done.76) | copy-start | bytes 1924
  501.9 59.4 %copy-start.96 = (f32[160]{0:T(256)S(1)}, f32[160]{0:T(256)}, u32[]{:S(2)}) copy-start(f32[160]{0:T(256)} %copy-done.95) | copy-start | bytes 1924
  501.9 61.5 %copy-start.105 = (f32[160]{0:T(256)S(1)}, f32[160]{0:T(256)}, u32[]{:S(2)}) copy-start(f32[160]{0:T(256)} %copy-done.104) | copy-start | bytes 1924
  569.1 195.9 %reduce-scatter.5.cloned.1.call-start = ((), (), s32[]{:S(2)}) async-start(), calls=%async_computation.3 | async-start | bytes 2228224 | tf_op jit(solution)/shard_map/reduce_scatter | solution.py:1918
  570.2 16.8 %copy-start.56 = (bf16[16,64,512]{2,1,0:T(8,128)(2,1)S(1)}, bf16[16,64,512]{2,1,0:T(8,128)(2,1)}, u32[]{:S(2)}) copy-start(bf16[16,64,512]{2,1,0:T(8,128)(2,1)} %get-tuple-element.125) | copy-start | bytes 3145732
  570.6 16.6 %copy-start.55 = (bf16[4,128,1024]{2,1,0:T(8,128)(2,1)S(1)}, bf16[4,128,1024]{2,1,0:T(8,128)(2,1)}, u32[]{:S(2)}) copy-start(bf16[4,128,1024]{2,1,0:T(8,128)(2,1)} %get-tuple-element.126) | copy-start | bytes 3145732
  587.4 19.9 %copy-start.15 = (bf16[512,1024]{1,0:T(8,128)(2,1)S(1)}, bf16[512,1024]{1,0:T(8,128)(2,1)}, u32[]{:S(2)}) copy-start(bf16[512,1024]{1,0:T(8,128)(2,1)} %get-tuple-element.128) | copy-start | bytes 3145732
  587.4 19.9 %copy-start.16 = (bf16[1024,512]{1,0:T(8,128)(2,1)S(1)}, bf16[1024,512]{1,0:T(8,128)(2,1)}, u32[]{:S(2)}) copy-start(bf16[1024,512]{1,0:T(8,128)(2,1)} %get-tuple-element.127) | copy-start | bytes 3145732
  610.9 78.7 %copy-start.10 = (bf16[1024,192]{1,0:T(8,128)(2,1)S(1)}, bf16[1024,192]{1,0:T(8,128)(2,1)}, u32[]{:S(2)}) copy-start(bf16[1024,192]{1,0:T(8,128)(2,1)} %get-tuple-element.124.refs_1_) | copy-start | bytes 1179652
  689.9 5.0 copy-start.116
  689.9 5.0 copy-start.115
  689.9 5.0 copy-start.114
  689.9 6.3 copy-start.47
  689.9 6.3 copy-start.51
  698.3 6.2 copy-start.60
  698.3 6.4 copy-start.59
  792.5 5.4 copy-start.53
  792.6 5.4 copy-start.61
  792.6 6.2 copy-start.58
  (88 other events, 206.1 us)
Sparse Core Ops, SparseCore 0:
  10.2 62.0 all-gather.4
  74.5 50.3 all-gather.6
  569.3 75.2 reduce-scatter.2
  698.5 66.4 reduce-scatter.4

commit v3 on v0

--- a/solution.py
+++ b/solution.py
@@ -1,6 +1,10 @@
+import functools
+
 import jax
 import jax.numpy as jnp
 from jax import lax
+from jax.experimental import pallas as pl
+from jax.experimental.pallas import tpu as pltpu
 from jax.sharding import PartitionSpec as P
 
 HEAD_DIM = 64
@@ -301,7 +305,7 @@
     return (d_inputs, big_grads, small_grads)
 
 
-def local(
+def general(
     tokens,
     grad_out,
     first_rows,
@@ -411,6 +415,1669 @@
     )
 
 
+MESH = pl.DeviceIdType.MESH
+LINE = 4
+HALVES = 2
+CHUNK = 32
+TILE = 512
+
+
+def place():
+    k = lax.axis_index("blk")
+    return k // 4, lax.rem(k // 2, 2), lax.rem(k, 2)
+
+
+def index_of(z, y, c):
+    return (z * 2 + y) * 2 + c
+
+
+def device(z, y, c):
+    return {"blk": index_of(z, y, c)}
+
+
+def hail(where):
+    pl.semaphore_signal(pltpu.get_barrier_semaphore(), inc=1, device_id=where, device_id_type=MESH)
+
+
+def other_group():
+    return {"batch": 1 - lax.axis_index("batch")}
+
+
+def lasting(microseconds):
+    return pl.CostEstimate(flops=0, bytes_accessed=int(microseconds * 3.5e6), transcendentals=0)
+
+
+def remote(src, dst, send, recv, where):
+    return pltpu.make_async_remote_copy(
+        src_ref=src, dst_ref=dst, send_sem=send, recv_sem=recv, device_id=where, device_id_type=MESH
+    )
+
+
+class Swap:
+    def __init__(self, x_ref, o_ref, ss, rs, own_sem, per=1):
+        self.x_ref, self.o_ref, self.ss, self.rs, self.own_sem = x_ref, o_ref, ss, rs, own_sem
+        self.k, self.n, self.per = lax.axis_index("blk"), 4 * LINE, per
+
+    @staticmethod
+    def scratch():
+        dma = pltpu.SemaphoreType.DMA
+        return [dma((4 * LINE,)), dma((4 * LINE,)), dma]
+
+    def source(self, to):
+        return self.x_ref.at[pl.ds(lax.rem(to, self.x_ref.shape[0] // self.per) * self.per, self.per)]
+
+    def place(self, at):
+        return self.o_ref.at[pl.ds(at * self.per, self.per)]
+
+    def send(self, i):
+        to = lax.rem(self.k + i, self.n)
+        return remote(self.source(to), self.place(self.k), self.ss.at[i], self.rs.at[i], {"blk": to})
+
+    def receive(self, i):
+        at = lax.rem(self.k - i + self.n, self.n)
+        return remote(self.place(at), self.place(at), self.ss.at[i], self.rs.at[i], {"blk": at})
+
+    def own(self):
+        return pltpu.make_async_copy(self.source(self.k), self.place(self.k), self.own_sem)
+
+    def start(self):
+        def one(i, carry):
+            self.send(i).start()
+            return carry
+
+        lax.fori_loop(1, self.n, one, 0)
+        self.own().start()
+
+    def finish(self):
+        def one(i, carry):
+            self.receive(i).wait_recv()
+            self.send(i).wait_send()
+            return carry
+
+        self.own().wait()
+        lax.fori_loop(1, self.n, one, 0)
+
+
+class Trade:
+    def __init__(self, x_ref, o_ref, ss, rs, own_sem):
+        self.x_ref, self.o_ref, self.ss, self.rs, self.own_sem = x_ref, o_ref, ss, rs, own_sem
+        self.z, self.y, self.c = place()
+
+    @staticmethod
+    def scratch():
+        dma = pltpu.SemaphoreType.DMA
+        return [dma((LINE,)), dma((LINE,)), dma]
+
+    def source(self, to):
+        return self.x_ref.at[lax.rem(to, self.x_ref.shape[0])]
+
+    def send(self, s):
+        to = lax.rem(self.z + s, LINE)
+        return remote(self.source(to), self.o_ref.at[self.z], self.ss.at[s], self.rs.at[s], device(to, self.y, self.c))
+
+    def own(self):
+        return pltpu.make_async_copy(self.source(self.z), self.o_ref.at[self.z], self.own_sem)
+
+    def start(self):
+        for s in range(1, LINE):
+            self.send(s).start()
+        self.own().start()
+
+    def finish(self):
+        self.own().wait()
+        for s in range(1, LINE):
+            at = lax.rem(self.z - s + LINE, LINE)
+            slot = self.o_ref.at[at]
+            remote(slot, slot, self.ss.at[s], self.rs.at[s], device(at, self.y, self.c)).wait_recv()
+            self.send(s).wait_send()
+
+
+class Cross:
+    def __init__(self, x_ref, o_ref, ss, rs):
+        self.copy = remote(x_ref, o_ref, ss, rs, other_group())
+
+    @staticmethod
+    def scratch():
+        return [pltpu.SemaphoreType.DMA] * 2
+
+    def start(self):
+        self.copy.start()
+
+    def finish(self):
+        self.copy.wait()
+
+
+def start_all(rides):
+    for ride in rides:
+        ride.start()
+
+
+def finish_all(rides):
+    for ride in rides:
+        ride.finish()
+
+
+def greet_group(crossing=False, plane=False):
+    k, n = lax.axis_index("blk"), 4 * LINE
+
+    def one(i, carry):
+        hail({"blk": lax.rem(k + i, n)})
+        return carry
+
+    lax.fori_loop(1, n, one, 0)
+    more = 0
+    if plane:
+        x, z, y, c = plane_place()
+        for d in range(4):
+            hail(plane_device(1 - x, z, 1 - y if d & 2 else y, 1 - c if d & 1 else c))
+        more = 4
+    elif crossing:
+        hail(other_group())
+        more = 1
+    pl.semaphore_wait(pltpu.get_barrier_semaphore(), n - 1 + more)
+
+
+class GroupGather:
+    def __init__(self, all_ref, sems):
+        self.all_ref = all_ref
+        self.sr, self.rr, self.sl, self.rl, self.sy, self.ry, self.sc, self.rc = sems
+        self.z, self.y, self.c = place()
+        self.half = all_ref.shape[0] // (4 * LINE * HALVES)
+
+    @staticmethod
+    def scratch():
+        dma = pltpu.SemaphoreType.DMA
+        return [dma((LINE, HALVES))] * 6 + [dma((2 * LINE, HALVES))] * 2
+
+    def block(self, z, y, h, c=None):
+        c = self.c if c is None else c
+        return self.all_ref.at[pl.ds((index_of(z, y, c) * HALVES + h) * self.half, self.half)]
+
+    def right(self, s, h):
+        block = self.block(self.z - s + 1, self.y, h)
+        return remote(block, block, self.sr.at[s, h], self.rr.at[s, h], device(self.z + 1, self.y, self.c))
+
+    def left(self, s, h):
+        block = self.block(self.z + s - 1, self.y, h)
+        return remote(block, block, self.sl.at[s, h], self.rl.at[s, h], device(self.z - 1, self.y, self.c))
+
+    def across(self, zz, h):
+        block = self.block(zz, self.y, h)
+        return remote(block, block, self.sy.at[zz, h], self.ry.at[zz, h], device(self.z, 1 - self.y, self.c))
+
+    def twin(self, zz, yy, h):
+        block = self.block(zz, yy, h)
+        slot = zz * 2 + yy
+        return remote(block, block, self.sc.at[slot, h], self.rc.at[slot, h], device(self.z, self.y, 1 - self.c))
+
+    def arrival(self, block, send, recv):
+        remote(block, block, send, recv, device(self.z, self.y, 1 - self.c)).wait_recv()
+
+    def start(self):
+        z, y = self.z, self.y
+        for h in range(HALVES):
+
+            @pl.when(z < LINE - 1)
+            def _():
+                self.right(1, h).start()
+
+            @pl.when(z > 0)
+            def _():
+                self.left(1, h).start()
+
+            self.across(z, h).start()
+        for h in range(HALVES):
+            self.twin(z, y, h).start()
+
+    def from_across(self, zz, h):
+        self.arrival(self.block(zz, 1 - self.y, h), self.sy.at[zz, h], self.ry.at[zz, h])
+        self.twin(zz, 1 - self.y, h).start()
+
+    def pass_on(self, zz, h):
+        self.across(zz, h).start()
+        self.twin(zz, self.y, h).start()
+
+    def run(self):
+        z, y = self.z, self.y
+        for s in range(1, LINE):
+            for h in range(HALVES):
+
+                @pl.when(z >= s)
+                def _():
+                    self.arrival(self.block(z - s, y, h), self.sr.at[s, h], self.rr.at[s, h])
+                    if s < LINE - 1:
+
+                        @pl.when(z < LINE - 1)
+                        def _():
+                            self.right(s + 1, h).start()
+
+                    self.pass_on(z - s, h)
+
+                @pl.when(z + s <= LINE - 1)
+                def _():
+                    self.arrival(self.block(z + s, y, h), self.sl.at[s, h], self.rl.at[s, h])
+                    if s < LINE - 1:
+
+                        @pl.when(z > 0)
+                        def _():
+                            self.left(s + 1, h).start()
+
+                    self.pass_on(z + s, h)
+
+                if s == 1:
+                    self.from_across(z, h)
+                else:
+
+                    @pl.when(z >= s - 1)
+                    def _():
+                        self.from_across(z - s + 1, h)
+
+                    @pl.when(z + s - 1 <= LINE - 1)
+                    def _():
+                        self.from_across(z + s - 1, h)
+
+        for h in range(HALVES):
+
+            @pl.when(z >= LINE - 1)
+            def _():
+                self.from_across(z - LINE + 1, h)
+
+            @pl.when(z <= 0)
+            def _():
+                self.from_across(z + LINE - 1, h)
+
+        for h in range(HALVES):
+            for zz in range(LINE):
+                for yy in range(2):
+                    slot = zz * 2 + yy
+                    self.arrival(self.block(zz, yy, h, 1 - self.c), self.sc.at[slot, h], self.rc.at[slot, h])
+
+    def finish(self):
+        z = self.z
+        for h in range(HALVES):
+            for zz in range(LINE):
+                self.across(zz, h).wait_send()
+                for yy in range(2):
+                    self.twin(zz, yy, h).wait_send()
+            for s in range(1, LINE):
+
+                @pl.when((z < LINE - 1) & (z >= s - 1))
+                def _():
+                    self.right(s, h).wait_send()
+
+                @pl.when((z > 0) & (z + s - 1 <= LINE - 1))
+                def _():
+                    self.left(s, h).wait_send()
+
+
+def order_at(z, t):
+    table = ((3, 2, 1, 0), (3, 0, 2, 1), (0, 3, 1, 2), (0, 1, 2, 3))
+    low = jnp.where(z == 0, table[0][t], table[1][t])
+    high = jnp.where(z == 2, table[2][t], table[3][t])
+    return jnp.where(z < 2, low, high)
+
+
+class GroupScatter:
+    def __init__(self, part_ref, bufs, sems):
+        self.part_ref = part_ref
+        self.twins, self.ysend, self.yrecv, self.zsend, self.zright, self.zleft = bufs
+        self.sc, self.rc, self.sy, self.ry, self.sz, self.rzr, self.rzl = sems
+        self.z, self.y, self.c = place()
+        self.half = part_ref.shape[0] // (4 * LINE * HALVES)
+
+    @staticmethod
+    def scratch(rows, columns):
+        dma = pltpu.SemaphoreType.DMA
+        bufs = [pltpu.VMEM((n, rows, columns), jnp.bfloat16) for n in (2 * LINE, LINE, LINE, LINE - 1, LINE, LINE)]
+        return bufs, [dma((2 * LINE, HALVES))] * 2 + [dma((LINE, HALVES))] * 5
+
+    def part(self, h):
+        return pl.ds(h * self.half, self.half)
+
+    def rows(self, t, own_y, c, h):
+        y = self.y if own_y else 1 - self.y
+        return pl.ds((index_of(order_at(self.z, t), y, c) * HALVES + h) * self.half, self.half)
+
+    def twin(self, t, own_y, h):
+        slot = t * 2 + own_y
+        source = self.part_ref.at[self.rows(t, own_y, 1 - self.c, h)]
+        dest = self.twins.at[slot, self.part(h)]
+        return remote(source, dest, self.sc.at[slot, h], self.rc.at[slot, h], device(self.z, self.y, 1 - self.c))
+
+    def across(self, t, h):
+        source, dest = self.ysend.at[t, self.part(h)], self.yrecv.at[t, self.part(h)]
+        return remote(source, dest, self.sy.at[t, h], self.ry.at[t, h], device(self.z, 1 - self.y, self.c))
+
+    def along(self, d, t, h, to_right):
+        buf, sem = (self.zright, self.rzr) if to_right else (self.zleft, self.rzl)
+        where = device(self.z + 1, self.y, self.c) if to_right else device(self.z - 1, self.y, self.c)
+        return remote(self.zsend.at[t, self.part(h)], buf.at[d, self.part(h)], self.sz.at[t, h], sem.at[d, h], where)
+
+    def arrived(self, d, h, to_right):
+        buf, sem = (self.zright, self.rzr) if to_right else (self.zleft, self.rzl)
+        slot = buf.at[d, self.part(h)]
+        remote(slot, slot, self.sz.at[0, h], sem.at[d, h], device(self.z, self.y, 1 - self.c)).wait_recv()
+
+    def wide(self, ref, slot, h):
+        return ref[slot, self.part(h)].astype(jnp.float32)
+
+    def chip(self, t, own_y, h):
+        return self.part_ref[self.rows(t, own_y, self.c, h)].astype(jnp.float32) + self.wide(self.twins, t * 2 + own_y, h)
+
+    def start(self):
+        for own_y in (0, 1):
+            for t in range(LINE):
+                for h in range(HALVES):
+                    self.twin(t, own_y, h).start()
+
+    def first(self):
+        for t in range(LINE):
+            for h in range(HALVES):
+                self.twin(t, 0, h).wait_recv()
+                self.ysend[t, self.part(h)] = self.chip(t, 0, h).astype(jnp.bfloat16)
+                self.across(t, h).start()
+
+    def second(self, o_ref):
+        z = self.z
+        for t in range(LINE):
+            d = order_at(z, t)
+            for h in range(HALVES):
+                self.twin(t, 1, h).wait_recv()
+                self.across(t, h).wait_recv()
+
+                def summed(t=t, h=h):
+                    return self.chip(t, 1, h) + self.wide(self.yrecv, t, h)
+
+                if t < LINE - 1:
+                    for to_right in (True, False):
+
+                        @pl.when((d > z) if to_right else (d < z))
+                        def _():
+                            first = (z == 0) if to_right else (z == LINE - 1)
+                            buf = self.zright if to_right else self.zleft
+
+                            @pl.when(first)
+                            def _():
+                                self.zsend[t, self.part(h)] = summed().astype(jnp.bfloat16)
+
+                            @pl.when(jnp.logical_not(first))
+                            def _():
+                                self.arrived(d, h, to_right)
+                                self.zsend[t, self.part(h)] = (summed() + self.wide(buf, d, h)).astype(jnp.bfloat16)
+
+                            self.along(d, t, h, to_right).start()
+                else:
+
+                    @pl.when(z > 0)
+                    def _():
+                        self.arrived(z, h, True)
+
+                    @pl.when(z < LINE - 1)
+                    def _():
+                        self.arrived(z, h, False)
+
+                    @pl.when(z == 0)
+                    def _():
+                        o_ref[self.part(h)] = summed() + self.wide(self.zleft, z, h)
+
+                    @pl.when(z == LINE - 1)
+                    def _():
+                        o_ref[self.part(h)] = summed() + self.wide(self.zright, z, h)
+
+                    @pl.when((z > 0) & (z < LINE - 1))
+                    def _():
+                        o_ref[self.part(h)] = summed() + self.wide(self.zright, z, h) + self.wide(self.zleft, z, h)
+
+    def finish(self):
+        for h in range(HALVES):
+            for t in range(LINE):
+                self.across(t, h).wait_send()
+                self.twin(t, 0, h).wait_send()
+                self.twin(t, 1, h).wait_send()
+            for t in range(LINE - 1):
+                self.along(0, t, h, True).wait_send()
+
+
+NN = (((1,), (0,)), ((), ()))
+NT = (((1,), (1,)), ((), ()))
+TN = (((0,), (0,)), ((), ()))
+
+
+def mul(a, b, dims=NN):
+    return lax.dot_general(a, b, dims, preferred_element_type=jnp.float32)
+
+
+def tile_at(t):
+    return pl.ds(pl.multiple_of(t * TILE, TILE), TILE)
+
+
+def chunk_at(index, rows=CHUNK):
+    return pl.ds(pl.multiple_of(index * rows, rows), rows)
+
+
+def diagonal(p):
+    key = lax.broadcasted_iota(jnp.int32, p.shape, 0)
+    query = lax.broadcasted_iota(jnp.int32, p.shape, 1)
+    return key <= query
+
+
+PLANE = 8
+
+
+def plane_place():
+    x = lax.axis_index("batch")
+    z, y, c = place()
+    return x, z, y, c
+
+
+def plane_device(x, z, y, c):
+    return {"batch": x, "blk": index_of(z, y, c)}
+
+
+def plane_index(x, y, c):
+    return (x * 2 + y) * 2 + c
+
+
+class PlaneGather:
+    def __init__(self, all_ref, sems):
+        self.all_ref = all_ref
+        self.sx, self.rx, self.sy, self.ry, self.sc, self.rc = sems
+        self.x, self.z, self.y, self.c = plane_place()
+        self.half = all_ref.shape[0] // (2 * PLANE)
+
+    @staticmethod
+    def scratch():
+        dma = pltpu.SemaphoreType.DMA
+        return [dma((3,))] * 4 + [dma((PLANE,))] * 2
+
+    def piece(self, x, y, c, h):
+        return self.all_ref.at[pl.ds(plane_index(x, y, c) * 2 * self.half + h * self.half, self.half)]
+
+    def over_x(self, i):
+        x, y, c = self.x, self.y, self.c
+        piece = self.piece(x, y if i < 2 else 1 - y, c, (0, 1, 1)[i])
+        return remote(piece, piece, self.sx.at[i], self.rx.at[i], plane_device(1 - x, self.z, y, c))
+
+    def over_y(self, i):
+        x, y, c = self.x, self.y, self.c
+        piece = self.piece(x if i < 2 else 1 - x, y, c, (1, 0, 0)[i])
+        return remote(piece, piece, self.sy.at[i], self.ry.at[i], plane_device(x, self.z, 1 - y, c))
+
+    def from_x(self, i):
+        x, y, c = self.x, self.y, self.c
+        piece = self.piece(1 - x, y if i < 2 else 1 - y, c, (0, 1, 1)[i])
+        remote(piece, piece, self.sx.at[i], self.rx.at[i], plane_device(1 - x, self.z, y, c)).wait_recv()
+
+    def from_y(self, i):
+        x, y, c = self.x, self.y, self.c
+        piece = self.piece(x if i < 2 else 1 - x, 1 - y, c, (1, 0, 0)[i])
+        remote(piece, piece, self.sy.at[i], self.ry.at[i], plane_device(x, self.z, 1 - y, c)).wait_recv()
+
+    def twin(self, other_x, other_y, h):
+        x = 1 - self.x if other_x else self.x
+        y = 1 - self.y if other_y else self.y
+        slot = (other_x * 2 + other_y) * 2 + h
+        piece = self.piece(x, y, self.c, h)
+        return remote(piece, piece, self.sc.at[slot], self.rc.at[slot], plane_device(self.x, self.z, self.y, 1 - self.c))
+
+    def from_twin(self, other_x, other_y, h):
+        x = 1 - self.x if other_x else self.x
+        y = 1 - self.y if other_y else self.y
+        slot = (other_x * 2 + other_y) * 2 + h
+        piece = self.piece(x, y, 1 - self.c, h)
+        where = plane_device(self.x, self.z, self.y, 1 - self.c)
+        remote(piece, piece, self.sc.at[slot], self.rc.at[slot], where).wait_recv()
+
+    def start(self):
+        self.over_x(0).start()
+        self.over_y(0).start()
+        self.over_x(1).start()
+        self.over_y(1).start()
+        self.twin(0, 0, 0).start()
+        self.twin(0, 0, 1).start()
+
+    def near(self):
+        self.from_x(0)
+        self.over_y(2).start()
+        self.twin(1, 0, 0).start()
+        self.from_y(0)
+        self.over_x(2).start()
+        self.twin(0, 1, 1).start()
+        self.from_y(1)
+        self.twin(0, 1, 0).start()
+        for other_y in range(2):
+            for h in range(2):
+                self.from_twin(0, other_y, h)
+
+    def far(self):
+        self.from_x(1)
+        self.twin(1, 0, 1).start()
+        self.from_x(2)
+        self.twin(1, 1, 1).start()
+        self.from_y(2)
+        self.twin(1, 1, 0).start()
+        for other_y in range(2):
+            for h in range(2):
+                self.from_twin(1, other_y, h)
+
+    def finish(self):
+        for i in range(3):
+            self.over_x(i).wait_send()
+            self.over_y(i).wait_send()
+        for other_x in range(2):
+            for other_y in range(2):
+                for h in range(2):
+                    self.twin(other_x, other_y, h).wait_send()
+
+
+class PlaneScatter:
+    def __init__(self, part_ref, bufs, sems):
+        self.part_ref = part_ref
+        self.twins, self.xs, self.xr, self.ys, self.yr = bufs
+        self.sx, self.rx, self.sy, self.ry, self.sc, self.rc = sems
+        self.x, self.z, self.y, self.c = plane_place()
+        self.half = part_ref.shape[0] // (2 * PLANE)
+
+    @staticmethod
+    def scratch(rows, columns):
+        dma = pltpu.SemaphoreType.DMA
+        half = pltpu.VMEM((3, rows // 2, columns), jnp.bfloat16)
+        return [pltpu.VMEM((4, rows, columns), jnp.bfloat16)] + [half] * 4, [dma((3,))] * 4 + [dma((4,))] * 2
+
+    def rows(self, which, c, h=None):
+        x = self.x if which >= 2 else 1 - self.x
+        y = self.y if which % 2 else 1 - self.y
+        at = plane_index(x, y, c) * 2 * self.half
+        return pl.ds(at, 2 * self.half) if h is None else pl.ds(at + h * self.half, self.half)
+
+    def twin(self, which):
+        where = plane_device(self.x, self.z, self.y, 1 - self.c)
+        source = self.part_ref.at[self.rows(which, 1 - self.c)]
+        return remote(source, self.twins.at[which], self.sc.at[which], self.rc.at[which], where)
+
+    def over_x(self, i):
+        return remote(
+            self.xs.at[i], self.xr.at[i], self.sx.at[i], self.rx.at[i], plane_device(1 - self.x, self.z, self.y, self.c)
+        )
+
+    def over_y(self, i):
+        return remote(
+            self.ys.at[i], self.yr.at[i], self.sy.at[i], self.ry.at[i], plane_device(self.x, self.z, 1 - self.y, self.c)
+        )
+
+    def chip(self, which, h):
+        own = self.part_ref[self.rows(which, self.c, h)].astype(jnp.float32)
+        return own + self.twins[which, h * self.half : (h + 1) * self.half].astype(jnp.float32)
+
+    def first(self):
+        self.twin(0).wait_recv()
+        self.xs[0] = self.chip(0, 0).astype(jnp.bfloat16)
+        self.over_x(0).start()
+        self.ys[0] = self.chip(0, 1).astype(jnp.bfloat16)
+        self.over_y(0).start()
+        self.twin(1).wait_recv()
+        self.xs[1] = self.chip(1, 0).astype(jnp.bfloat16)
+        self.over_x(1).start()
+        self.twin(2).wait_recv()
+        self.ys[1] = self.chip(2, 1).astype(jnp.bfloat16)
+        self.over_y(1).start()
+
+    def second(self):
+        self.over_x(0).wait_recv()
+        self.ys[2] = (self.chip(2, 0) + self.xr[0].astype(jnp.float32)).astype(jnp.bfloat16)
+        self.over_y(2).start()
+        self.over_y(0).wait_recv()
+        self.xs[2] = (self.chip(1, 1) + self.yr[0].astype(jnp.float32)).astype(jnp.bfloat16)
+        self.over_x(2).start()
+
+    def finish(self, o_ref):
+        half = self.half
+        self.twin(3).wait_recv()
+        self.over_x(1).wait_recv()
+        self.over_y(1).wait_recv()
+        self.over_y(2).wait_recv()
+        o_ref[0:half] = self.chip(3, 0) + self.xr[1].astype(jnp.float32) + self.yr[2].astype(jnp.float32)
+        self.over_x(2).wait_recv()
+        o_ref[half : 2 * half] = self.chip(3, 1) + self.yr[1].astype(jnp.float32) + self.xr[2].astype(jnp.float32)
+        for which in range(4):
+            self.twin(which).wait_send()
+        for i in range(3):
+            self.over_x(i).wait_send()
+            self.over_y(i).wait_send()
+
+
+class PlanePool:
+    def __init__(self, own_ref, got_ref, send, recv):
+        self.own_ref, self.got_ref, self.send, self.recv = own_ref, got_ref, send, recv
+        self.x, self.z, self.y, self.c = plane_place()
+
+    def others(self):
+        for d in range(1, PLANE):
+            x = 1 - self.x if d & 4 else self.x
+            y = 1 - self.y if d & 2 else self.y
+            c = 1 - self.c if d & 1 else self.c
+            yield d, x, y, c
+
+    def copies(self):
+        slot = self.got_ref.at[plane_index(self.x, self.y, self.c)]
+        for d, x, y, c in self.others():
+            yield remote(self.own_ref, slot, self.send.at[d], self.recv.at[d], plane_device(x, self.z, y, c))
+
+    def start(self):
+        for copy in self.copies():
+            copy.start()
+        self.got_ref[plane_index(self.x, self.y, self.c)] = self.own_ref[...]
+
+    def finish(self):
+        for d, x, y, c in self.others():
+            slot = self.got_ref.at[plane_index(x, y, c)]
+            remote(slot, slot, self.send.at[d], self.recv.at[d], plane_device(x, self.z, y, c)).wait_recv()
+        for copy in self.copies():
+            copy.wait_send()
+
+
+def span_at(th, width):
+    return pl.ds(pl.multiple_of(th * width, 128), width)
+
+
+def units_at(ut):
+    return pl.ds(pl.multiple_of(ut * 256, 256), 256)
+
+
+def mean_and_rate(stat, hidden_all):
+    return stat[0:1], lax.rsqrt(stat[1:2] * (1.0 / hidden_all) + EPSILON)
+
+
+class Refs:
+    def __init__(self, **named):
+        self.__dict__.update(named)
+
+
+def launch(call, kernel, inputs, outputs, scratch, collective_id, microseconds, vmem_mib):
+    def body(*refs):
+        refs = list(refs)
+        named = Refs()
+        for key in [*inputs, *outputs]:
+            setattr(named, key, refs.pop(0))
+        for key, what in scratch.items():
+            if isinstance(what, list):
+                setattr(named, key, [refs.pop(0) for _ in what])
+            else:
+                setattr(named, key, refs.pop(0))
+        kernel(named)
+
+    results = call(
+        body,
+        out_shape=[shape for shape, _ in outputs.values()],
+        in_specs=[pl.BlockSpec(memory_space=space) for _, space in inputs.values()],
+        out_specs=[pl.BlockSpec(memory_space=space) for _, space in outputs.values()],
+        scratch_shapes=[entry for what in scratch.values() for entry in (what if isinstance(what, list) else [what])],
+        cost_estimate=lasting(microseconds),
+        compiler_params=pltpu.CompilerParams(
+            collective_id=collective_id, has_side_effects=True, vmem_limit_bytes=vmem_mib << 20
+        ),
+    )(*[array for array, _ in inputs.values()])
+    return Refs(**dict(zip(outputs, results)))
+
+
+def normed(values, gain, shift):
+    centred = values - jnp.mean(values, axis=-1, keepdims=True)
+    spread = jnp.mean(centred * centred, axis=-1, keepdims=True)
+    return centred * lax.rsqrt(spread + EPSILON) * gain + shift
+
+
+def normed_back(values, gain, grads):
+    centred = values - jnp.mean(values, axis=-1, keepdims=True)
+    rate = lax.rsqrt(jnp.mean(centred * centred, axis=-1, keepdims=True) + EPSILON)
+    unit = centred * rate
+    scaled = grads * gain
+    back = rate * (
+        scaled - jnp.mean(scaled, axis=-1, keepdims=True) - unit * jnp.mean(scaled * unit, axis=-1, keepdims=True)
+    )
+    return back, jnp.sum(grads * unit, axis=0, keepdims=True), jnp.sum(grads, axis=0, keepdims=True)
+
+
+def unfold_head(blocks_ref, w_ref):
+    for j in range(blocks_ref.shape[0]):
+        for part in range(2):
+            at = slice(64 * j + 32 * part, 64 * j + 32 * part + 32)
+            w_ref[at, 0:128] = blocks_ref[j, :, 128 * part : 128 * part + 128]
+            w_ref[at, 128:192] = blocks_ref[j, :, 256 + 64 * part : 320 + 64 * part]
+
+
+def fold_head(w, head):
+    width = w.shape[1] // 3
+    at = [slice(part * width + 64 * head, part * width + 64 * head + 64) for part in range(3)]
+    halves = [w[0:32], w[32:64]]
+    pieces = [half[:, at[part]] for half in halves for part in (0, 2)] + [half[:, at[1]] for half in halves]
+    return jnp.concatenate(pieces, axis=1)
+
+
+def unit_lanes(z, slot):
+    return pl.ds(pl.multiple_of(z * PLANE * 128 + slot * 128, 128), 128)
+
+
+def unit_columns(vectors, slot, column_refs):
+    pieces = [vector[:, unit_lanes(z, slot)] for vector in vectors for z in range(LINE)]
+    pieces.append(jnp.zeros((16 - len(pieces), 128), jnp.float32))
+    turned = jnp.transpose(jnp.concatenate(pieces, axis=0))
+    for i, ref in enumerate(column_refs):
+        for z in range(LINE):
+            ref[128 * z : 128 * z + 128] = turned[:, i * LINE + z : i * LINE + z + 1]
+
+
+def of_layer(ref, layer):
+    return [ref.at[kind, pl.ds(layer, 1)] for kind in range(ref.shape[0])]
+
+
+def own_head(row, index):
+    pair = row[:, pl.ds(pl.multiple_of(index // 2 * 128, 128), 128)]
+    return jnp.where(lax.rem(index, 2) == 0, pair[:, 0:64], pair[:, 64:128])
+
+
+def chunks_of(ref, t):
+    per_tile = TILE // CHUNK
+    part = ref[pl.ds(t * per_tile, per_tile)]
+    return part.reshape(per_tile * part.shape[1], part.shape[2])
+
+
+def alive(cut, i, j):
+    return jnp.where((i >= cut) & (j < cut), NEGATIVE, 0.0)
+
+
+def natural_rows(slot, zz):
+    x, y, c = slot // 4, slot // 2 % 2, slot % 2
+    return 64 * index_of(zz, y, c) + 32 * x
+
+
+def forward_kernel(layer, hidden_all, r):
+    first = layer == 0
+    x, z, y, c = plane_place()
+    index, slot = index_of(z, y, c), plane_index(x, y, c)
+    unit_slot = (y * 2 + c) * 2 + x
+    rows, columns = r.x_in.shape
+    total = r.hb_all.shape[0]
+    tiles, chunks, per_tile = total // TILE, total // CHUNK, TILE // CHUNK
+    gather = GroupGather(r.hb_all, r.gather_sems)
+    gains, biases = of_layer(r.gains, layer), of_layer(r.biases, layer)
+    if first:
+        load_qkv = pltpu.make_async_copy(r.w_qkv, r.qkv_in, r.prep_sem.at[0])
+        load_qkv.start()
+        for l in range(2):
+            for q in range(4):
+                for zz in range(LINE):
+                    source = r.w_up.at[l, :, unit_lanes(zz, q * 2 + x)]
+                    dest = r.unit_src.at[l, q, :, pl.ds(zz * 128, 128)]
+                    pltpu.make_async_copy(source, dest, r.prep_sem.at[1 + l]).start()
+    value = r.x_in[...].astype(jnp.float32)
+    r.hb_all[pl.ds(index * rows, rows)] = normed(value, gains[0][...], biases[0][...]).astype(jnp.bfloat16)
+    head_ride = Swap(r.head_src.at[0], r.head_blocks, *r.head_sems) if first else None
+    unit_ride = Swap(r.unit_src.at[0], r.unit_blocks, *r.unit_sems) if first else None
+    down_ride = Trade(r.w_down.at[layer, pl.ds(x, 1)], r.down_blocks, *r.down_sems)
+    out_ride = Trade(r.w_out.at[layer, pl.ds(x, 1)], r.out_got, *r.out_sems)
+    next_rides = [Swap(r.head_src.at[1], r.next_head, *r.next_head_sems)] if first else []
+    next_rides += [Swap(r.unit_src.at[1], r.next_unit, *r.next_unit_sems)] if first else []
+    if first:
+        load_qkv.wait()
+        for head in range(4 * LINE):
+            r.head_src[0, head] = fold_head(r.qkv_in[0], head)
+    load_head = pltpu.make_async_copy(r.head_blocks, r.head_in, r.load_sem.at[0])
+    load_unit = pltpu.make_async_copy(r.unit_blocks, r.unit_in, r.load_sem.at[1])
+    load_down = pltpu.make_async_copy(r.down_blocks, r.down_w, r.load_sem.at[2])
+    greet_group(plane=True)
+    if first:
+        head_ride.start()
+    gather.start()
+    out_ride.start()
+    mids = [r.mid_gain_all.at[pl.ds(layer, 1)], r.mid_bias_all.at[layer, pl.ds(0, 1)], r.mid_bias_all.at[layer, pl.ds(1, 1)]]
+    unit_columns(mids, unit_slot, (r.mid_gain, r.mid_shift, r.mid_bias))
+    head_bias = [own_head(biases[row], index) for row in (3, 4)] + [jnp.zeros((1, 64), jnp.float32)]
+    head_bias = jnp.concatenate(head_bias, axis=1)
+    if first:
+        for head in range(4 * LINE):
+            r.head_src[1, head] = fold_head(r.qkv_in[1], head)
+        for l in range(2):
+            pltpu.make_async_copy(r.unit_src.at[l], r.unit_src.at[l], r.prep_sem.at[1 + l]).wait()
+    if not first:
+        load_head.start()
+        load_unit.start()
+    gather.run()
+    if first:
+        unit_ride.start()
+        head_ride.finish()
+        load_head.start()
+    else:
+        down_ride.start()
+    load_head.wait()
+    unfold_head(r.head_in, r.head_w)
+
+    def project(t, carry):
+        rows_t = (mul(r.hb_all[tile_at(t)], r.head_w[...]) + head_bias).astype(jnp.bfloat16)
+        r.flat[pl.ds(t * per_tile, per_tile)] = rows_t.reshape(per_tile, CHUNK, 192)
+        return carry
+
+    lax.fori_loop(0, tiles, project, 0)
+    out_ride.finish()
+    out_rows = r.out_all.shape[0] // PLANE
+    for zz in range(LINE):
+        r.out_all[pl.ds(slot * out_rows + zz * 32, 32)] = r.out_got[zz]
+    out_gather = PlaneGather(r.out_all, r.out_gather_sems)
+    out_gather.start()
+
+    def arrange(p, carry):
+        r.qvk[p] = r.flat[r.table[p]]
+        return carry
+
+    lax.fori_loop(0, chunks, arrange, 0)
+
+    def prepare(t, carry):
+        rows_t = chunks_of(r.qvk, t)
+        r.queries[tile_at(t)] = rows_t[:, 0:64] * 0.125
+        r.keys[tile_at(t)] = rows_t[:, 128:192]
+        turned = jnp.transpose(rows_t[:, 0:128].astype(jnp.float32))
+        r.values_t[:, tile_at(t)] = turned[64:128].astype(jnp.bfloat16)
+        return carry
+
+    lax.fori_loop(0, tiles, prepare, 0)
+    cut = r.table[2 * chunks]
+    for i in range(tiles):
+        at = slice(i * TILE, (i + 1) * TILE)
+        query = r.queries[at]
+
+        def block(j, state, masked):
+            peak, part, mixed = state
+            scores = mul(r.keys[tile_at(j)], query, NT)
+            bias = 0.0 if masked else alive(cut, i, j)
+            if masked:
+                keep = diagonal(scores)
+                scores = jnp.where(keep, scores, NEGATIVE)
+            new_peak = jnp.maximum(peak, jnp.max(scores, axis=0, keepdims=True) + bias)
+            weights = jnp.exp(scores - (new_peak - bias))
+            if masked:
+                weights = jnp.where(keep, weights, 0.0)
+            factor = jnp.exp(peak - new_peak)
+            part = part * factor + jnp.sum(weights, axis=0, keepdims=True)
+            mixed = mixed * factor + mul(r.values_t[:, tile_at(j)], weights.astype(jnp.bfloat16))
+            return (new_peak, part, mixed)
+
+        state = (
+            jnp.full((1, TILE), NEGATIVE, jnp.float32),
+            jnp.zeros((1, TILE), jnp.float32),
+            jnp.zeros((64, TILE), jnp.float32),
+        )
+        state = block(i, state, True)
+        if i > 0:
+            state = lax.fori_loop(0, i, functools.partial(block, masked=False), state)
+        peak, part, mixed = state
+        mixed = mixed / part
+        r.lse[:, at] = peak + jnp.log(part)
+        r.head_out[:, at] = mixed
+        pairs = (jnp.transpose(mixed) * r.scales[layer, index]).reshape(per_tile, 2, CHUNK // 2, 64)
+        pairs = jnp.concatenate([pairs[:, 0], pairs[:, 1]], axis=-1).astype(jnp.bfloat16)
+        r.pairs[i * per_tile : (i + 1) * per_tile] = pairs
+        if i == 2:
+            out_gather.near()
+    per_block = rows // CHUNK
+
+    def pack(p, carry):
+        r.packed[p] = r.pairs[r.table[chunks + p]]
+        return carry
+
+    lax.fori_loop(0, chunks, pack, 0)
+    mix = Swap(r.packed, r.mixed, *r.mix_sems, per=per_block)
+    mix.start()
+    out_gather.far()
+    for s in range(PLANE):
+        for zz in range(LINE):
+            at = natural_rows(s, zz)
+            r.out_w[at : at + 32] = r.out_all[s * out_rows + zz * 32 : s * out_rows + zz * 32 + 32]
+    out_gather.finish()
+    mix.finish()
+    if first:
+        down_ride.start()
+    for g in range(columns // 128):
+        left, right = (
+            r.mixed[h * per_block : (h + 1) * per_block].reshape(rows // 2, 128) for h in (2 * g, 2 * g + 1)
+        )
+        low = jnp.concatenate([left[:, 0:64], right[:, 0:64]], axis=1)
+        high = jnp.concatenate([left[:, 64:128], right[:, 64:128]], axis=1)
+        for p in range(per_block):
+            at = slice(p * (CHUNK // 2), (p + 1) * (CHUNK // 2))
+            r.ab[p * CHUNK : p * CHUNK + CHUNK // 2, 128 * g : 128 * g + 128] = low[at]
+            r.ab[p * CHUNK + CHUNK // 2 : (p + 1) * CHUNK, 128 * g : 128 * g + 128] = high[at]
+    branch = mul(r.ab[...], r.out_w[...]) + biases[5][...]
+    r.branch[...] = branch
+    middle = value + normed(branch, gains[1][...], biases[1][...])
+    r.middle[...] = middle
+
+    own = pl.ds(slot * rows, rows)
+    r.rows_all[own] = normed(middle, gains[2][...], biases[2][...]).astype(jnp.bfloat16)
+    plane_gather = PlaneGather(r.rows_all, r.plane_gather_sems)
+    plane_scatter = PlaneScatter(r.part, r.plane_bufs, r.plane_sems)
+    pool = PlanePool(r.own_stat, r.got_stat, *r.pool_sems)
+    plane_gather.start()
+    hidden = r.act.shape[0]
+    width = r.act.shape[1] // 2
+    if first:
+        plane_gather.near()
+        plane_gather.far()
+        unit_ride.finish()
+        load_unit.start()
+    load_unit.wait()
+    for j in range(r.unit_in.shape[0] // 2):
+        pair = r.unit_in[2 * j : 2 * j + 2].reshape(128, hidden)
+        r.unit_t[:, 128 * j : 128 * j + 128] = jnp.transpose(pair)
+
+    def climb(th):
+        at = span_at(th, width)
+
+        def units(ut, carry):
+            here = units_at(ut)
+            upper = mul(r.unit_t[here], r.rows_all[pl.ds(th * width, width)], NT) + r.mid_bias[here]
+            chance = 0.5 * (1.0 + lax.erf(upper * (0.5**0.5)))
+            r.act[here, at] = upper * chance
+            slope = chance + upper * (jnp.exp(-0.5 * upper * upper) * 0.3989422804014327)
+            r.slope[here, at] = slope.astype(jnp.bfloat16)
+            return carry
+
+        lax.fori_loop(0, hidden // 256, units, 0)
+        values = r.act[:, at]
+        mean = jnp.mean(values, axis=0, keepdims=True)
+        apart = values - mean
+        r.own_stat[0:1, at] = mean
+        r.own_stat[1:2, at] = jnp.sum(apart * apart, axis=0, keepdims=True)
+
+    if not first:
+        plane_gather.near()
+    climb(x)
+    if not first:
+        plane_gather.far()
+    climb(1 - x)
+    pool.start()
+    down_ride.finish()
+    load_down.start()
+    start_all(next_rides)
+    pool.finish()
+    load_down.wait()
+    means = [r.got_stat[i, 0:1] for i in range(PLANE)]
+    mean = functools.reduce(jnp.add, means) * (1.0 / PLANE)
+    apart = functools.reduce(jnp.add, [(m - mean) * (m - mean) for m in means])
+    r.stat[0:1] = mean
+    r.stat[1:2] = functools.reduce(jnp.add, [r.got_stat[i, 1:2] for i in range(PLANE)]) + apart * float(hidden)
+
+    def descend(th):
+        at = span_at(th, width)
+        mean, rate = mean_and_rate(r.stat[:, at], hidden_all)
+
+        def units(ut, carry):
+            here = units_at(ut)
+            low = (r.act[here, at] - mean) * rate * r.mid_gain[here] + r.mid_shift[here]
+            r.mid[here, at] = low.astype(jnp.bfloat16)
+            return carry
+
+        lax.fori_loop(0, hidden // 256, units, 0)
+        down_w = r.down_w[...].reshape(hidden, columns)
+        r.part[pl.ds(th * width, width)] = mul(r.mid[:, at], down_w, TN).astype(jnp.bfloat16)
+
+    descend(1 - x)
+    plane_scatter.twin(0).start()
+    plane_scatter.twin(1).start()
+    descend(x)
+    plane_scatter.twin(2).start()
+    plane_scatter.twin(3).start()
+    saved = (
+        (r.hb_all, r.hb_all_out), (r.qvk, r.qvk_out), (r.out_w, r.out_w_out), (r.rows_all, r.rows_all_out),
+        (r.unit_t, r.unit_t_out), (r.act, r.act_out), (r.slope, r.slope_out), (r.mid, r.mid_out),
+    )
+    saves = [pltpu.make_async_copy(source, dest, r.save_sem.at[i]) for i, (source, dest) in enumerate(saved)]
+    for save in saves:
+        save.start()
+    plane_scatter.first()
+    plane_scatter.second()
+    plane_scatter.finish(r.result)
+    r.y_out[...] = (r.middle[...] + (r.result[...] + biases[6][...])).astype(r.y_out.dtype)
+    gather.finish()
+    plane_gather.finish()
+    for save in saves:
+        save.wait()
+    finish_all(next_rides)
+
+
+def layer_forward_kernel(layer, table, x_in, params, blocks, y_type, collective_id):
+    rows, columns = x_in.shape
+    hidden_all = params.mid_gain.shape[1]
+    total, plane_rows, hidden = rows * 4 * LINE, rows * PLANE, hidden_all // PLANE
+    vmem, anywhere, smem = pltpu.VMEM, pl.ANY, pltpu.SMEM
+    dma = pltpu.SemaphoreType.DMA
+    low = lambda *shape: pltpu.VMEM(shape, jnp.bfloat16)
+    full = lambda *shape: pltpu.VMEM(shape, jnp.float32)
+    low_out = lambda *shape: jax.ShapeDtypeStruct(shape, jnp.bfloat16)
+    full_out = lambda *shape: jax.ShapeDtypeStruct(shape, jnp.float32)
+    swap_sems, trade_sems = Swap.scratch(), Trade.scratch()
+    inputs = dict(
+        table=(table, smem), scales=(params.head_scale, smem), x_in=(x_in, vmem), gains=(params.vec_gain, vmem),
+        biases=(params.vec_bias, vmem), mid_gain_all=(params.mid_gain, vmem), mid_bias_all=(params.mid_bias, vmem),
+        w_down=(params.w_down, anywhere), w_out=(params.w_out, anywhere),
+    )
+    head_shape, unit_shape = (4 * LINE, 32, 384), (4 * LINE, columns // (4 * LINE), hidden)
+    outputs = dict(
+        y_out=(jax.ShapeDtypeStruct((rows, columns), y_type), vmem), branch=(full_out(rows, columns), vmem),
+        middle=(full_out(rows, columns), vmem), ab=(low_out(rows, columns), vmem),
+        lse=(full_out(1, total), vmem), head_out=(full_out(64, total), vmem),
+        stat=(full_out(2, plane_rows), vmem), hb_all_out=(low_out(total, columns), anywhere),
+        qvk_out=(low_out(total // CHUNK, CHUNK, 192), anywhere), out_w_out=(low_out(columns, columns), anywhere),
+        rows_all_out=(low_out(plane_rows, columns), anywhere), unit_t_out=(low_out(hidden, columns), anywhere),
+        act_out=(full_out(hidden, plane_rows), anywhere), slope_out=(low_out(hidden, plane_rows), anywhere),
+        mid_out=(low_out(hidden, plane_rows), anywhere), down_blocks=(low_out(LINE, hidden // LINE, columns), anywhere),
+    )
+    first = layer == 0
+    if first:
+        inputs.update(w_qkv=(params.w_qkv, anywhere), w_up=(params.w_up, anywhere))
+        head_got, unit_got = (low_out(*head_shape), anywhere), (low_out(*unit_shape), anywhere)
+        outputs.update(head_blocks=head_got, unit_blocks=unit_got, next_head=head_got, next_unit=unit_got)
+    else:
+        inputs.update(head_blocks=(blocks.head, anywhere), unit_blocks=(blocks.unit, anywhere))
+    plane_bufs, plane_sems = PlaneScatter.scratch(rows, columns)
+    scratch = dict(
+        hb_all=low(total, columns), flat=low(total // CHUNK, CHUNK, 192),
+        qvk=low(total // CHUNK, CHUNK, 192), queries=low(total, 64), keys=low(total, 64),
+        values_t=low(64, total), pairs=low(total // CHUNK, CHUNK // 2, 128),
+        packed=low(total // CHUNK, CHUNK // 2, 128), mixed=low(total // CHUNK, CHUNK // 2, 128), head_in=low(4 * LINE, 32, 384), head_w=low(columns, 192),
+        unit_in=low(4 * LINE, columns // (4 * LINE), hidden), unit_t=low(hidden, columns),
+        down_w=low(LINE, hidden // LINE, columns), out_got=low(LINE, 32, columns),
+        out_all=low(columns, columns), out_w=low(columns, columns), rows_all=low(plane_rows, columns),
+        act=full(hidden, plane_rows), slope=low(hidden, plane_rows), mid=low(hidden, plane_rows),
+        part=low(plane_rows, columns), own_stat=full(2, plane_rows), got_stat=full(PLANE, 2, plane_rows),
+        result=full(rows, columns), plane_bufs=plane_bufs, plane_sems=plane_sems,
+        gather_sems=GroupGather.scratch(), plane_gather_sems=PlaneGather.scratch(),
+        out_gather_sems=PlaneGather.scratch(), pool_sems=([dma((PLANE,)), dma((PLANE,))]),
+        head_sems=swap_sems, unit_sems=swap_sems, next_head_sems=swap_sems, next_unit_sems=swap_sems,
+        mix_sems=swap_sems, down_sems=trade_sems, out_sems=trade_sems, load_sem=dma((3,)),
+        save_sem=dma((8,)),
+    )
+    scratch.update(mid_gain=full(hidden, 1), mid_shift=full(hidden, 1), mid_bias=full(hidden, 1))
+    if first:
+        scratch.update(qkv_in=low(*params.w_qkv.shape), head_src=low(2, *head_shape), prep_sem=dma((3,)))
+        scratch.update(unit_src=low(2, 4, columns // (4 * LINE), hidden))
+    kernel = functools.partial(forward_kernel, layer, hidden_all)
+    call = lambda body, **how: pl.pallas_call(body, name="layer_forward", **how)
+    return launch(call, kernel, inputs, outputs, scratch, collective_id, 95, 56)
+
+
+class AllSum:
+    def __init__(self, own_ref, sent, got, send, recv):
+        self.own_ref, self.sent, self.got, self.send, self.recv = own_ref, sent, got, send, recv
+        self.z, self.y, self.c = place()
+
+    @staticmethod
+    def scratch(shape, kind):
+        dma = pltpu.SemaphoreType.DMA
+        return [pltpu.VMEM((3, *shape), kind), pltpu.VMEM((LINE + 2, *shape), kind), dma((LINE + 2,)), dma((LINE + 2,))]
+
+    def copy(self, i):
+        z, y, c = self.z, self.y, self.c
+        where = (other_group(), device(z, y, 1 - c), device(z, 1 - y, c))[i] if i < 3 else None
+        if i >= 3:
+            where = device(lax.rem(z + i - 2, LINE), y, c)
+        source = self.own_ref if i == 0 else self.sent.at[min(i, 3) - 1]
+        return remote(source, self.got.at[i], self.send.at[i], self.recv.at[i], where)
+
+    def start(self):
+        self.copy(0).start()
+
+    def step(self, i):
+        self.copy(i - 1).wait_recv()
+        own = self.own_ref[...] if i == 1 else self.sent[i - 2]
+        self.sent[i - 1] = (own.astype(jnp.float32) + self.got[i - 1].astype(jnp.float32)).astype(self.sent.dtype)
+        for k in range(i, i + 1 if i < 3 else LINE + 2):
+            self.copy(k).start()
+
+    def finish(self, o_ref):
+        for i in range(3, LINE + 2):
+            self.copy(i).wait_recv()
+        total = None
+        for zz in range(LINE):
+            term = self.sent[2].astype(jnp.float32)
+            for s in range(1, LINE):
+                term = jnp.where(lax.rem(self.z - s + LINE, LINE) == zz, self.got[2 + s].astype(jnp.float32), term)
+            total = term if total is None else total + term
+        o_ref[...] = total
+        for i in range(LINE + 2):
+            self.copy(i).wait_send()
+
+
+OUT_BIAS, DOWN_BIAS, QUERY_BIAS, VALUE_BIAS, SCALES, MID, SMALL = 6, 7, 8, 9, 10, 12, 24
+
+
+def spread_head(piece, index, width):
+    nothing = jnp.zeros_like(piece)
+    even = lax.rem(index, 2) == 0
+    pair = jnp.concatenate([jnp.where(even, piece, nothing), jnp.where(even, nothing, piece)], axis=1)
+    lanes = lax.broadcasted_iota(jnp.int32, (1, width), 1) // 128
+    return jnp.where(lanes == index // 2, jnp.concatenate([pair] * (width // 128), axis=1), 0.0)
+
+
+def backward_kernel(layer, hidden_all, r):
+    first = layer == 1
+    x, z, y, c = plane_place()
+    index, unit_slot = index_of(z, y, c), (y * 2 + c) * 2 + x
+    rows, columns = r.dy.shape
+    total = r.hb_all_in.shape[0]
+    tiles, chunks, per_tile = total // TILE, total // CHUNK, TILE // CHUNK
+    hidden, plane_rows = r.act.shape
+    width = plane_rows // 2
+    dy_all, x_all = r.wide.at[pl.ds(0, plane_rows)], r.wide.at[pl.ds(plane_rows, plane_rows)]
+    plane_gather = PlaneGather(dy_all, r.plane_gather_sems)
+    plane_scatter = PlaneScatter(r.part, r.plane_bufs, r.plane_sems)
+    out_part = r.part.at[pl.ds(0, LINE * PLANE * 32)]
+    out_scatter = PlaneScatter(out_part, r.out_bufs, r.out_sems)
+    scatter = GroupScatter(r.wide, r.group_bufs, r.group_sems)
+    pool = PlanePool(r.own_sums, r.got_sums, *r.pool_sems)
+    unit_ride = Swap(r.gup, r.unit_got, *r.unit_sems)
+    out_ride = Trade(r.out_own, r.out_got, *r.out_ride_sems)
+    head_ride = Swap(r.head_fold, r.head_got, *r.head_sems)
+    head_cross = Cross(r.head_own, r.head_other, *r.head_cross_sems)
+    down_ride = Trade(r.gdown, r.gdown_got, *r.gdown_sems)
+    near_rides = [
+        Cross(r.unit_near, r.unit_far, *r.unit_cross_sems), Cross(r.down_near, r.down_far, *r.down_cross_sems),
+        Cross(r.out_near, r.out_far, *r.out_cross_sems),
+    ]
+    if not first:
+        bulk = AllSum(r.bulk, *r.bulk_sum)
+        rest = AllSum(r.rest, *r.rest_sum)
+    gains = of_layer(r.gains, layer)
+    r.small[...] = jnp.zeros_like(r.small)
+    dy = r.dy[...].astype(jnp.float32)
+    dy_low = dy.astype(jnp.bfloat16)
+    r.small[DOWN_BIAS : DOWN_BIAS + 1] = jnp.sum(dy_low.astype(jnp.float32), axis=0, keepdims=True)
+    dy_all[pl.ds(plane_index(x, y, c) * rows, rows)] = dy_low
+    loads = [
+        pltpu.make_async_copy(source, dest, r.load_sem.at[i])
+        for i, (source, dest) in enumerate(
+            (
+                (r.down_blocks, r.down_w), (r.act_in, r.act), (r.slope_in, r.slope), (r.unit_t_in, r.unit_t),
+                (r.mid_in, r.mid), (r.rows_all_in, x_all), (r.out_w_in, r.out_w), (r.qvk_in, r.qvk),
+            )
+        )
+    ]
+    for load in loads[:6]:
+        load.start()
+    greet_group(plane=True)
+    plane_gather.start()
+    for load in loads[6:]:
+        load.start()
+
+    def tile_load(t):
+        return pltpu.make_async_copy(r.hb_all_in.at[pl.ds(t * TILE, TILE)], r.hb_tiles.at[t % 2], r.tile_sem.at[t % 2])
+
+    tile_load(0).start()
+    tile_load(1).start()
+    unit_columns([r.mid_gain_all.at[pl.ds(layer, 1)]], unit_slot, [r.mid_gain])
+    r.gg[...] = jnp.zeros_like(r.gg)
+    r.gs[...] = jnp.zeros_like(r.gs)
+    r.gb[...] = jnp.zeros_like(r.gb)
+    r.own_sums[...] = jnp.zeros_like(r.own_sums)
+
+    def climb(th):
+        at = span_at(th, width)
+        mean, rate = mean_and_rate(r.stat[:, at], hidden_all)
+
+        def units(ut, carry):
+            here = units_at(ut)
+            down_w = r.down_w[pl.ds(ut * 2, 2)].reshape(256, columns)
+            dm = mul(down_w, dy_all[pl.ds(th * width, width)], NT)
+            r.dmid[here, at] = dm
+            vh = (r.act[here, at] - mean) * rate
+            r.act[here, at] = vh
+            r.gg[here] += jnp.sum(dm * vh, axis=1, keepdims=True)
+            r.gs[here] += jnp.sum(dm, axis=1, keepdims=True)
+            scaled = dm * r.mid_gain[here]
+            r.own_sums[0:1, at] += jnp.sum(scaled, axis=0, keepdims=True)
+            r.own_sums[1:2, at] += jnp.sum(scaled * vh, axis=0, keepdims=True)
+            return carry
+
+        lax.fori_loop(0, hidden // 256, units, 0)
+
+    plane_gather.near()
+    loads[0].wait()
+    loads[1].wait()
+    climb(x)
+    plane_gather.far()
+    climb(1 - x)
+    pool.start()
+    loads[4].wait()
+    for ut in range(hidden // 256):
+        grad = mul(r.mid[ut * 256 : (ut + 1) * 256], dy_all[...]).astype(jnp.bfloat16)
+        r.gdown[2 * ut : 2 * ut + 2] = grad.reshape(2, 128, columns)
+    down_ride.start()
+    pool.finish()
+    r.sums[...] = functools.reduce(jnp.add, [r.got_sums[i] for i in range(PLANE)]) * (1.0 / hidden_all)
+    loads[2].wait()
+    loads[3].wait()
+
+    def descend(th):
+        at = span_at(th, width)
+        _, rate = mean_and_rate(r.stat[:, at], hidden_all)
+        sum0, sum1 = r.sums[0:1, at], r.sums[1:2, at]
+
+        def units(ut, carry):
+            here = units_at(ut)
+            dact = rate * (r.dmid[here, at] * r.mid_gain[here] - sum0 - r.act[here, at] * sum1)
+            du = (dact * r.slope[here, at].astype(jnp.float32)).astype(jnp.bfloat16)
+            r.du[here, at] = du
+            r.gb[here] += jnp.sum(du.astype(jnp.float32), axis=1, keepdims=True)
+            return carry
+
+        lax.fori_loop(0, hidden // 256, units, 0)
+        r.part[pl.ds(th * width, width)] = mul(r.du[:, at], r.unit_t[...], TN).astype(jnp.bfloat16)
+
+    descend(1 - x)
+    plane_scatter.twin(0).start()
+    plane_scatter.twin(1).start()
+    descend(x)
+    plane_scatter.twin(2).start()
+    plane_scatter.twin(3).start()
+    plane_scatter.first()
+    loads[5].wait()
+    plane_scatter.second()
+    for ut in range(hidden // 256):
+        grad = jnp.transpose(mul(r.du[ut * 256 : (ut + 1) * 256], x_all[...])).astype(jnp.bfloat16)
+        r.gup[:, :, ut * 256 : (ut + 1) * 256] = grad.reshape(r.gup.shape[0], -1, 256)
+    plane_scatter.finish(r.dffn)
+    plane_gather.finish()
+
+    back, r.small[2:3], r.small[5:6] = normed_back(r.middle[...], gains[2][...], r.dffn[...])
+    r.dmiddle[...] = dy + back
+    back, r.small[1:2], r.small[4:5] = normed_back(r.branch[...], gains[1][...], r.dmiddle[...])
+    dz = back.astype(jnp.bfloat16)
+    r.small[OUT_BIAS : OUT_BIAS + 1] = jnp.sum(dz.astype(jnp.float32), axis=0, keepdims=True)
+    loads[6].wait()
+    da = mul(dz, r.out_w[...], NT).astype(jnp.bfloat16)
+    per_block = rows // CHUNK
+    halves = da.reshape(per_block, 2, CHUNK // 2, columns)
+    low, high = halves[:, 0].reshape(rows // 2, columns), halves[:, 1].reshape(rows // 2, columns)
+    for h in range(columns // 64):
+        at = slice(64 * h, 64 * h + 64)
+        pairs = jnp.concatenate([low[:, at], high[:, at]], axis=1)
+        r.packed[h * per_block : (h + 1) * per_block] = pairs.reshape(per_block, CHUNK // 2, 128)
+    mix = Swap(r.packed, r.mixed, *r.mix_sems, per=per_block)
+    mix.start()
+    out_rows = LINE * 32
+    for zz in range(LINE):
+        grad = mul(r.ab[:, 256 * zz : 256 * zz + 256], dz, TN).astype(jnp.bfloat16)
+        for s in range(PLANE):
+            at = natural_rows(s, 0)
+            out_part[s * out_rows + zz * 32 : s * out_rows + zz * 32 + 32] = grad[at : at + 32]
+    for which in range(4):
+        out_scatter.twin(which).start()
+    turned = [ref[128 * zz : 128 * zz + 128] for ref in (r.gg, r.gs, r.gb) for zz in range(LINE)]
+    turned = jnp.transpose(jnp.concatenate(turned + [jnp.zeros((128, 4), jnp.float32)], axis=1))
+    for i in range(3 * LINE):
+        r.small[MID + i : MID + i + 1, unit_lanes(0, unit_slot)] = turned[i : i + 1]
+    if not first:
+        r.bulk[0:SMALL] = r.small_in[...].astype(jnp.bfloat16)
+        r.bulk[SMALL : 2 * SMALL] = r.small[...].astype(jnp.bfloat16)
+        bulk.start()
+    loads[7].wait()
+    load_head = pltpu.make_async_copy(r.head_blocks, r.head_fold, r.load_sem.at[6])
+    load_head.start()
+    scale = r.scales[layer, index]
+
+    def prepare(t, carry):
+        at = tile_at(t)
+        rows_t = chunks_of(r.qvk, t)
+        r.query[at] = rows_t[:, 0:64] * 0.125
+        r.values[at] = rows_t[:, 64:128]
+        key = rows_t[:, 128:192]
+        r.keys[at] = key
+        r.keys_t[:, at] = jnp.transpose(key.astype(jnp.float32)).astype(jnp.bfloat16)
+        r.dkeys[at] = jnp.zeros((TILE, 64), jnp.float32)
+        r.dvalues[at] = jnp.zeros((TILE, 64), jnp.float32)
+        return carry
+
+    lax.fori_loop(0, tiles, prepare, 0)
+    load_head.wait()
+    unfold_head(r.head_fold, r.head_w)
+    out_scatter.first()
+    mix.finish()
+    unit_ride.start()
+
+    def arrange(p, carry):
+        r.pairs[p] = r.mixed[r.table[p]]
+        return carry
+
+    lax.fori_loop(0, chunks, arrange, 0)
+
+    def unpack(t, carry):
+        at = tile_at(t)
+        pairs = r.pairs[pl.ds(t * per_tile, per_tile)].astype(jnp.float32)
+        pairs = jnp.concatenate([pairs[:, :, 0:64], pairs[:, :, 64:128]], axis=1).reshape(TILE, 64)
+        low = (pairs * scale).astype(jnp.bfloat16)
+        r.dout[at] = low
+        r.delta[:, at] = jnp.sum(jnp.transpose(low.astype(jnp.float32)) * r.head_out[:, at], axis=0, keepdims=True)
+        return carry
+
+    lax.fori_loop(0, tiles, unpack, 0)
+    lanes = lax.broadcasted_iota(jnp.int32, (1, columns), 1)
+    scale_grad = jnp.sum(r.delta[...], axis=1, keepdims=True) / scale
+    r.small[SCALES : SCALES + 1] = jnp.where(lanes == layer * 4 * LINE + index, scale_grad, 0.0)
+    cut = r.table[2 * chunks]
+    for i in range(tiles):
+        at = slice(i * TILE, (i + 1) * TILE)
+        query, dout, lse, delta = r.query[at], r.dout[at], r.lse[:, at], r.delta[:, at]
+
+        def block(j, total_dq, masked):
+            there = tile_at(j)
+            scores = mul(r.keys[there], query, NT)
+            weights = jnp.exp(scores - (lse if masked else lse - alive(cut, i, j)))
+            if masked:
+                weights = jnp.where(diagonal(scores), weights, 0.0)
+            dweights = mul(r.values[there], dout, NT)
+            dscores = (weights * (dweights - delta)).astype(jnp.bfloat16)
+            r.dvalues[there] += mul(weights.astype(jnp.bfloat16), dout)
+            r.dkeys[there] += mul(dscores, query)
+            return total_dq + mul(r.keys_t[:, there], dscores)
+
+        total_dq = block(i, jnp.zeros((64, TILE), jnp.float32), True)
+        if i > 0:
+            total_dq = lax.fori_loop(0, i, functools.partial(block, masked=False), total_dq)
+        r.dquery_t[:, at] = total_dq * 0.125
+        if i == 1:
+            out_scatter.second()
+            if not first:
+                bulk.step(1)
+        if i == 2:
+            out_scatter.finish(r.out_sum)
+            r.out_own[...] = r.out_sum[...].reshape(r.out_own.shape).astype(jnp.bfloat16)
+            out_ride.start()
+            if not first:
+                bulk.step(2)
+
+    head_bias = jnp.zeros((1, 192), jnp.float32)
+    for i in range(tiles):
+        at = slice(i * TILE, (i + 1) * TILE)
+        joined = jnp.concatenate([jnp.transpose(r.dquery_t[:, at]), r.dvalues[at], r.dkeys[at]], axis=1).astype(jnp.bfloat16)
+        head_bias += jnp.sum(joined.astype(jnp.float32), axis=0, keepdims=True)
+        r.qvk[i * per_tile : (i + 1) * per_tile] = joined.reshape(per_tile, CHUNK, 192)
+
+    r.small[QUERY_BIAS : QUERY_BIAS + 1] = spread_head(head_bias[:, 0:64], index, columns)
+    r.small[VALUE_BIAS : VALUE_BIAS + 1] = spread_head(head_bias[:, 64:128], index, columns)
+
+    def restore(p, carry):
+        r.flat[p] = r.qvk[r.table[chunks + p]]
+        return carry
+
+    lax.fori_loop(0, chunks, restore, 0)
+
+    def project(t, carry):
+        r.wide[tile_at(t)] = mul(chunks_of(r.flat, t), r.head_w[...], NT).astype(jnp.bfloat16)
+        return carry
+
+    lax.fori_loop(0, tiles, project, 0)
+    scatter.start()
+    for t in range(tiles):
+        tile_load(t).wait()
+        grad = mul(chunks_of(r.flat, t), r.hb_tiles[t % 2], TN)
+        r.gw[...] = grad if t == 0 else r.gw[...] + grad
+        if t + 2 < tiles:
+            tile_load(t + 2).start()
+    r.head_own[...] = jnp.transpose(r.gw[...]).astype(jnp.bfloat16)
+    head_cross.start()
+    scatter.first()
+    if not first:
+        bulk.step(3)
+    down_ride.finish()
+    out_ride.finish()
+    unit_ride.finish()
+    reloads = [
+        pltpu.make_async_copy(source, dest, r.load_sem.at[i])
+        for i, (source, dest) in enumerate(((r.unit_got, r.gup), (r.gdown_got, r.gdown), (r.out_got, r.out_own)))
+    ]
+    for load in reloads:
+        load.start()
+    head_cross.finish()
+    for j in range(r.head_fold.shape[0]):
+        for part in range(2):
+            at = slice(64 * j + 32 * part, 64 * j + 32 * part + 32)
+            both = (r.head_own[at].astype(jnp.float32) + r.head_other[at].astype(jnp.float32)).astype(jnp.bfloat16)
+            r.head_fold[j, :, 128 * part : 128 * part + 128] = both[:, 0:128]
+            r.head_fold[j, :, 256 + 64 * part : 320 + 64 * part] = both[:, 128:192]
+    head_ride.start()
+    for load in reloads:
+        load.wait()
+    for q in range(4):
+        parts = [r.gup[zz * 4 + q].astype(jnp.float32) for zz in range(LINE)]
+        r.unit_near[q] = functools.reduce(jnp.add, parts).astype(jnp.bfloat16)
+    for near, own in ((r.down_near, r.gdown), (r.out_near, r.out_own)):
+        near[...] = functools.reduce(jnp.add, [own[zz].astype(jnp.float32) for zz in range(LINE)]).astype(jnp.bfloat16)
+    start_all(near_rides)
+    scatter.second(r.dffn)
+    back, gain_grad, shift_grad = normed_back(r.x_in[...].astype(jnp.float32), gains[0][...], r.dffn[...])
+    r.dx[...] = r.dmiddle[...] + back
+    r.small[0:1] = gain_grad
+    r.small[3:4] = shift_grad
+    if not first:
+        r.rest[0:1] = gain_grad
+        r.rest[1:2] = shift_grad
+        r.rest[2:5] = r.small[QUERY_BIAS : SCALES + 1]
+        r.rest[5:8] = jnp.zeros((3, columns), jnp.float32)
+        rest.start()
+        bulk.finish(r.bulk_out)
+        rest.step(1)
+        rest.step(2)
+        rest.step(3)
+        rest.finish(r.rest_out)
+    scatter.finish()
+    head_ride.finish()
+    finish_all(near_rides)
+
+
+def layer_backward_kernel(layer, table, dy, params, record, small, collective_id):
+    rows, columns = dy.shape
+    hidden_all = params.mid_gain.shape[1]
+    total, plane_rows, hidden = rows * 4 * LINE, rows * PLANE, hidden_all // PLANE
+    vmem, anywhere, smem = pltpu.VMEM, pl.ANY, pltpu.SMEM
+    dma = pltpu.SemaphoreType.DMA
+    low = lambda *shape: pltpu.VMEM(shape, jnp.bfloat16)
+    full = lambda *shape: pltpu.VMEM(shape, jnp.float32)
+    low_out = lambda *shape: jax.ShapeDtypeStruct(shape, jnp.bfloat16)
+    full_out = lambda *shape: jax.ShapeDtypeStruct(shape, jnp.float32)
+    swap_sems, trade_sems, cross_sems = Swap.scratch(), Trade.scratch(), Cross.scratch()
+    unit_shape = (4 * LINE, columns // (4 * LINE), hidden)
+    unit_near, down_near, out_near = (4, *unit_shape[1:]), (hidden // LINE, columns), (32, columns)
+    down_shape = (LINE, hidden // LINE, columns)
+    inputs = dict(
+        table=(table, smem), scales=(params.head_scale, smem), dy=(dy, vmem), gains=(params.vec_gain, vmem),
+        mid_gain_all=(params.mid_gain, vmem), x_in=(record.x_in, vmem), branch=(record.branch, vmem),
+        middle=(record.middle, vmem), ab=(record.ab, vmem), lse=(record.lse, vmem),
+        head_out=(record.head_out, vmem), stat=(record.stat, vmem), hb_all_in=(record.hb_all_out, anywhere),
+        qvk_in=(record.qvk_out, anywhere), out_w_in=(record.out_w_out, anywhere),
+        rows_all_in=(record.rows_all_out, anywhere), unit_t_in=(record.unit_t_out, anywhere),
+        act_in=(record.act_out, anywhere), slope_in=(record.slope_out, anywhere),
+        mid_in=(record.mid_out, anywhere), down_blocks=(record.down_blocks, anywhere),
+        head_blocks=(record.head_blocks, anywhere),
+    )
+    outputs = dict(
+        dx=(full_out(rows, columns), vmem), unit_got=(low_out(*unit_shape), anywhere),
+        gdown_got=(low_out(*down_shape), anywhere), out_got=(low_out(LINE, *out_near), anywhere),
+        head_got=(low_out(4 * LINE, 32, 384), anywhere), unit_near=(low_out(*unit_near), vmem),
+        down_near=(low_out(*down_near), vmem), out_near=(low_out(*out_near), vmem),
+        unit_far=(low_out(*unit_near), anywhere), down_far=(low_out(*down_near), anywhere),
+        out_far=(low_out(*out_near), anywhere),
+    )
+    first = layer == 1
+    if first:
+        outputs.update(small=(full_out(SMALL, columns), vmem))
+    else:
+        inputs.update(small_in=(small, vmem))
+        outputs.update(bulk_out=(full_out(2 * SMALL, columns), vmem), rest_out=(full_out(8, columns), vmem))
+    plane_bufs, plane_sems = PlaneScatter.scratch(rows, columns)
+    out_bufs, out_sems = PlaneScatter.scratch(LINE * 32, columns)
+    group_bufs, group_sems = GroupScatter.scratch(rows, columns)
+    scratch = dict(
+        wide=low(total, columns), down_w=low(*down_shape), act=full(hidden, plane_rows),
+        slope=low(hidden, plane_rows), unit_t=low(hidden, columns), mid=low(hidden, plane_rows),
+        out_w=low(columns, columns), qvk=low(total // CHUNK, CHUNK, 192), hb_tiles=low(2, TILE, columns),
+        dmid=full(hidden, plane_rows), du=low(hidden, plane_rows), part=low(plane_rows, columns),
+        own_sums=full(2, plane_rows), got_sums=full(PLANE, 2, plane_rows), sums=full(2, plane_rows),
+        gup=low(*unit_shape), gdown=low(*down_shape), dffn=full(rows, columns),
+        dmiddle=full(rows, columns), packed=low(total // CHUNK, CHUNK // 2, 128),
+        mixed=low(total // CHUNK, CHUNK // 2, 128),
+        out_sum=full(LINE * 32, columns), out_own=low(LINE, 32, columns),
+        pairs=low(total // CHUNK, CHUNK // 2, 128), dout=low(total, 64), delta=full(1, total), query=low(total, 64),
+        keys=low(total, 64), values=low(total, 64), keys_t=low(64, total), dkeys=full(total, 64),
+        dvalues=full(total, 64), dquery_t=full(64, total), flat=low(total // CHUNK, CHUNK, 192),
+        head_w=low(columns, 192), gw=full(192, columns), head_own=low(columns, 192),
+        head_other=low(columns, 192), head_fold=low(4 * LINE, 32, 384),
+        plane_bufs=plane_bufs, plane_sems=plane_sems, out_bufs=out_bufs, out_sems=out_sems,
+        group_bufs=group_bufs, group_sems=group_sems, plane_gather_sems=PlaneGather.scratch(),
+        pool_sems=([dma((PLANE,)), dma((PLANE,))]), unit_sems=swap_sems, gdown_sems=trade_sems, head_sems=swap_sems,
+        mix_sems=swap_sems, out_ride_sems=trade_sems, head_cross_sems=cross_sems, load_sem=dma((10,)),
+        tile_sem=dma((2,)),
+    )
+    scratch.update(unit_cross_sems=cross_sems, down_cross_sems=cross_sems, out_cross_sems=cross_sems)
+    scratch.update(mid_gain=full(hidden, 1), gg=full(hidden, 1), gs=full(hidden, 1), gb=full(hidden, 1))
+    if not first:
+        scratch.update(small=full(SMALL, columns), bulk=low(2 * SMALL, columns), rest=full(8, columns))
+        scratch.update(bulk_sum=AllSum.scratch((2 * SMALL, columns), jnp.bfloat16))
+        scratch.update(rest_sum=AllSum.scratch((8, columns), jnp.float32))
+    kernel = functools.partial(backward_kernel, layer, hidden_all)
+    call = lambda body, **how: pl.pallas_call(body, name="layer_backward", **how)
+    return launch(call, kernel, inputs, outputs, scratch, collective_id, 105, 63)
+
+
+def assemble_kernel(r):
+    x = lax.axis_index("batch")
+    for layer, got in enumerate((r.layer0, r.layer1)):
+        head_ref, unit_near, unit_far, down_near, down_far, out_near, out_far = got
+        width = 64 * head_ref.shape[0]
+        for j in range(0, head_ref.shape[0], 2):
+            left, right = head_ref[j].astype(jnp.float32), head_ref[j + 1].astype(jnp.float32)
+            for part in range(2):
+                for at, source in ((0, 128 * part), (width, 256 + 64 * part), (2 * width, 64 + 128 * part)):
+                    pair = jnp.concatenate([left[:, source : source + 64], right[:, source : source + 64]], axis=1)
+                    r.qkv[layer, 32 * part : 32 * part + 32, at + j * 64 : at + (j + 2) * 64] = pair
+        for half, unit_ref, down_ref, out_ref in ((x, unit_near, down_near, out_near), (1 - x, unit_far, down_far, out_far)):
+            for q in range(unit_ref.shape[0]):
+                for z in range(LINE):
+                    piece = unit_ref[q, :, z * 128 : (z + 1) * 128].astype(jnp.float32)
+                    r.up[layer, :, unit_lanes(z, q * 2 + half)] = piece
+            for ref, dest in ((down_ref, r.down), (out_ref, r.out)):
+                rows = ref.shape[0]
+                dest[layer, pl.ds(pl.multiple_of(half * rows, rows), rows)] = ref[...].astype(jnp.float32)
+        bulk = r.bulk[SMALL * (1 - layer) : SMALL * (2 - layer)]
+        rest = r.rest[...] if layer == 0 else bulk[0:1] * 0.0
+        gain, shift = (rest[0:1], rest[1:2]) if layer == 0 else (bulk[0:1], bulk[3:4])
+        heads = rest[2:4] if layer == 0 else bulk[QUERY_BIAS : VALUE_BIAS + 1]
+        gain_rows = jnp.concatenate([gain, bulk[1:3]], axis=0)
+        bias_rows = jnp.concatenate([shift, bulk[4:6], heads, bulk[OUT_BIAS : DOWN_BIAS + 1]], axis=0)
+        for ref, rows in ((r.vec_gain, gain_rows), (r.vec_bias, bias_rows)):
+            for i in range(ref.shape[0]):
+                ref[i, layer : layer + 1] = rows[i : i + 1]
+        for z in range(LINE):
+            at = slice(z * PLANE * 128, (z + 1) * PLANE * 128)
+            r.mid_gain[layer : layer + 1, at] = bulk[MID + z : MID + z + 1]
+            for i in range(2):
+                row = MID + (i + 1) * LINE + z
+                r.mid_bias[layer, i : i + 1, at] = bulk[row : row + 1]
+        row = rest[4:5] if layer == 0 else bulk[SCALES : SCALES + 1]
+        heads_here = r.head_scale.shape[1]
+        r.head_scale[layer : layer + 1] = row[:, layer * heads_here : (layer + 1) * heads_here]
+
+
+def assemble(results, dx, back, shapes):
+    vmem, anywhere = pl.BlockSpec(memory_space=pltpu.VMEM), pl.BlockSpec(memory_space=pl.ANY)
+    arrays = [results, dx]
+    for got in back:
+        arrays += [got.head_got, got.unit_near, got.unit_far, got.down_near, got.down_far, got.out_near, got.out_far]
+
+    arrays += [back[0].bulk_out, back[0].rest_out]
+    n = len(arrays)
+
+    def body(*refs):
+        ins, outs, held, sem = refs[:n], refs[n : n + 11], refs[n + 11 : -1], refs[-1]
+        loads = [pltpu.make_async_copy(ins[i], held[i], sem.at[i]) for i in range(n)]
+        passes = [pltpu.make_async_copy(held[i], outs[i], sem.at[i]) for i in range(2)]
+        for load in loads:
+            load.start()
+        for load in loads:
+            load.wait()
+        for copy in passes:
+            copy.start()
+        qkv, out, up, down, vec_gain, vec_bias, mid_gain, mid_bias, head_scale = outs[2:]
+        refs = held[2:]
+        assemble_kernel(
+            Refs(
+                layer0=refs[0:7], layer1=refs[7:14], bulk=refs[14], rest=refs[15], qkv=qkv, out=out, up=up, down=down,
+                vec_gain=vec_gain, vec_bias=vec_bias, mid_gain=mid_gain, mid_bias=mid_bias, head_scale=head_scale,
+            )
+        )
+        for copy in passes:
+            copy.wait()
+
+    return pl.pallas_call(
+        body,
+        out_shape=[jax.ShapeDtypeStruct(array.shape, array.dtype) for array in (results, dx)]
+        + [jax.ShapeDtypeStruct(shape, jnp.float32) for shape in shapes],
+        in_specs=[anywhere] * n,
+        out_specs=[anywhere] * 2 + [vmem] * len(shapes),
+        scratch_shapes=[pltpu.VMEM(array.shape, array.dtype) for array in arrays] + [pltpu.SemaphoreType.DMA((n,))],
+        cost_estimate=lasting(5),
+        compiler_params=pltpu.CompilerParams(vmem_limit_bytes=62 << 20),
+        name="assemble",
+    )(*arrays)
+
+
+def chunk_table(first_rows, span_of, rows_here):
+    blocks = span_of.shape[0]
+    first = first_rows[0]
+    second = rows_here - first
+    row = jnp.arange(blocks * rows_here // CHUNK, dtype=jnp.int32) * CHUNK
+    later = row >= first * blocks
+    inside = jnp.where(later, row - first * blocks, row)
+    length = jnp.where(later, jnp.maximum(second, 1), first)
+    span = inside // length
+    of_span = (span_of[None, :] == span[:, None]).astype(jnp.int32)
+    device_of = jnp.sum(of_span * jnp.arange(blocks, dtype=jnp.int32)[None, :], axis=1)
+    source = device_of * rows_here + jnp.where(later, first, 0) + inside - span * length
+    within = row % rows_here
+    behind = within >= first
+    place = jnp.repeat(span_of, rows_here // CHUNK) * jnp.where(behind, second, first) + within
+    place = place + jnp.where(behind, first * (blocks - 1), 0)
+    return jnp.concatenate([source // CHUNK, place // CHUNK, (first * blocks // TILE)[None]]).astype(jnp.int32)
+
+
+def travel(
+    tokens, grad_out, first_rows, span_of, w_qkv, w_out, w_up, w_down, vec_gain, vec_bias, mid_gain, mid_bias, head_scale
+):
+    rows_here, row_width = tokens.shape
+    table = chunk_table(first_rows, span_of, rows_here)
+    params = Refs(
+        w_qkv=w_qkv, w_up=w_up, w_out=w_out.reshape(2, 2, -1, row_width), w_down=w_down.reshape(2, 2, -1, row_width),
+        vec_gain=vec_gain.transpose(1, 0, 2), vec_bias=vec_bias.transpose(1, 0, 2), mid_gain=mid_gain, mid_bias=mid_bias,
+        head_scale=head_scale,
+    )
+    first = layer_forward_kernel(0, table, tokens, params, None, jnp.float32, 0)
+    first.x_in = tokens
+    blocks = Refs(head=first.next_head, unit=first.next_unit)
+    second = layer_forward_kernel(1, table, first.y_out, params, blocks, jnp.bfloat16, 1)
+    second.x_in, second.head_blocks = first.y_out, blocks.head
+    back_second = layer_backward_kernel(1, table, grad_out, params, second, None, 2)
+    back_first = layer_backward_kernel(0, table, back_second.dx, params, first, back_second.small, 3)
+    kinds = (w_qkv, w_out, w_up, w_down, params.vec_gain, params.vec_bias, mid_gain, mid_bias, head_scale)
+    results = assemble(second.y_out, back_first.dx, [back_first, back_second], [array.shape for array in kinds])
+    return (*results[:6], results[6].transpose(1, 0, 2), results[7].transpose(1, 0, 2), *results[8:])
+
+
+def local(*args):
+    tokens, w_qkv = args[0], args[4]
+    blocks = lax.axis_size("blk")
+    heads = w_qkv.shape[2] // (3 * HEAD_DIM)
+    if blocks == heads == 4 * LINE and lax.axis_size("batch") == 2 and tokens.shape[0] * blocks % TILE == 0:
+        return travel(*args)
+    return general(*args)
+
+
 def solution(mesh):
     placed = (
         P(("batch", "blk"), None),

time: 3370 us -> 537 us (0.16)
  waiting for transfers between devices: 1930 us -> 0 us
  other arithmetic: 595 us -> 1.66 us
  Pallas kernels: 0 us -> 524 us
  matrix products: 313 us -> 0 us
  local copies, waits for them, and re-layouts: 311 us -> 0.81 us
  loops' own time: 104 us -> 0 us
  starting transfers between devices: 83.4 us -> 0 us
    reduce_scatter x8 -> x0, waiting for transfers between devices: 737 us -> none  [the longest x2 214 us: local(): lax.psum_scatter(big_grads[3].astype(jnp.bfloat16), 'blk', scatter_dimens...]
    ppermute x128 -> x0, waiting for transfers between devices: 677 us -> none  [shifted(): lax.ppermute(x, axis, [(i, (i + by) % devices) for i in range(devices)])]
    pallas_call x0 -> x5, Pallas kernels: none -> 524 us  [the longest x4 518 us: launch(): call(body, out_shape=[shape for shape, _ in outputs.values()], in_specs=[...]
    all_gather x12 -> x0, waiting for transfers between devices: 373 us -> none  [the longest x2 119 us: local(): lax.all_gather(w_qkv[layer_index], 'blk', axis=0, tiled=True)]
    dot_general x160 -> x0, matrix products: 313 us -> none  [the longest x24 57.7 us: grad_block(): jnp.einsum('qhd,khd->hqk', dout_heads, value_heads, preferred_element_typ...]
    convert_element_type x137 -> x0, other arithmetic: 224 us -> none  [the longest x32 67.8 us: turn(): shifted(dvalues.astype(jnp.bfloat16), 'blk', 1).astype(dvalues.dtype)]
    psum x3 -> x0, waiting for transfers between devices: 137 us -> none  [the longest x1 83.5 us: local(): lax.psum(stacked_big[0].astype(jnp.bfloat16), 'batch').astype(jnp.float32)]
    another operation x44 -> x0, loops' own time: 104 us -> none  [the longest x32 55.3 us: turn(): lax.cond(source_span <= my_span, turn_compute, unchanged, (dquery, dkeys,...]
  transfers between devices with their start and end apart: 151 -> 0, of which waited for: 144 -> 0; matrix products, arithmetic and copies ran while one was open for 17% -> 0% of each run, Pallas kernels for 0% -> 0%
where the time goes in v3:
time: 537 us; the launch traced here: 528 us
  Pallas kernels  524 us (98%)
    pallas_call x4, Pallas kernels, launch(): call(body, out_shape=[shape for shape, _ in outputs.values()], in_specs=[...  518 us

profile of v3, /device:TPU:0, one launch (start us, length us, event | category | flops | bytes accessed | tf_op | source)
XLA Modules:
  0.0 528.3 jit_solution(13283583342493353968)
XLA Ops:
  1.3 0.1 and_select_fusion.3
  1.4 0.7 select_reduce_fusion
  2.2 0.7 broadcast_in_dim.31
  2.9 0.1 reshape.49
  3.0 0.1 and_select_fusion
  3.1 0.6 pad_add_fusion.refs_0_
  3.8 138.6 %layer_forward.2 = (f32[160,1024]{1,0:T(8,128)}, f32[160,1024]{1,0:T(8,128)}, f32[160,1024]{1,0:T(8,128)}, bf16[160,1024]{1,0:T(8,128)(2,1)}, f32[1,2560]{1,0:T(...) custom-call(s32[161]{0:T(256)} %pad_add_fusion.refs_0_, ...), custom_call_target="tpu_custom_call" | custom-call | bytes 332500000 | tf_op jit(solution)/shard_map/layer_forward/pallas_call | solution.py:1109
  142.4 113.9 %layer_forward.3 = (bf16[160,1024]{1,0:T(8,128)(2,1)}, f32[160,1024]{1,0:T(8,128)}, f32[160,1024]{1,0:T(8,128)}, bf16[160,1024]{1,0:T(8,128)(2,1)}, f32[1,2560]{...) custom-call(s32[161]{0:T(256)} %pad_add_fusion.refs_0_, ...), custom_call_target="tpu_custom_call" | custom-call | bytes 332500000 | tf_op jit(solution)/shard_map/layer_forward/pallas_call | solution.py:1109
  256.2 127.3 %layer_backward.2 = (f32[160,1024]{1,0:T(8,128)}, bf16[16,64,512]{2,1,0:T(8,128)(2,1)}, bf16[4,128,1024]{2,1,0:T(8,128)(2,1)}, bf16[4,32,1024]{2,1,0:T(8,128)(2,...) custom-call(s32[161]{0:T(256)} %pad_add_fusion.refs_0_, ...), custom_call_target="tpu_custom_call" | custom-call | bytes 367500000 | tf_op jit(solution)/shard_map/layer_backward/pallas_call | solution.py:1109
  383.6 138.2 %layer_backward.3 = (f32[160,1024]{1,0:T(8,128)}, bf16[16,64,512]{2,1,0:T(8,128)(2,1)}, bf16[4,128,1024]{2,1,0:T(8,128)(2,1)}, bf16[4,32,1024]{2,1,0:T(8,128)(2,...) custom-call(s32[161]{0:T(256)} %pad_add_fusion.refs_0_, ...), custom_call_target="tpu_custom_call" | custom-call | bytes 367500000 | tf_op jit(solution)/shard_map/layer_backward/pallas_call | solution.py:1109
  521.8 6.0 %assemble.1 = (bf16[160,1024]{1,0:T(8,128)(2,1)}, f32[160,1024]{1,0:T(8,128)}, f32[2,64,3072]{2,1,0:T(8,128)}, f32[2,64,1024]{2,1,0:T(8,128)}, f32[2,64,4096]{2,...) custom-call(bf16[160,1024]{1,0:T(8,128)(2,1)} %get-tuple-element.79., ...), custom_call_target="tpu_custom_call" | custom-call | bytes 17500000 | tf_op jit(solution)/shard_map/assemble/pallas_call | solution.py:2018

commit v4 on v3

--- a/solution.py
+++ b/solution.py
@@ -532,6 +532,111 @@
             self.send(s).wait_send()
 
 
+class Share:
+    def __init__(self, x_ref, o_ref, sr, rr, sl, rl, own_sem):
+        self.x_ref, self.o_ref, self.own_sem = x_ref, o_ref, own_sem
+        self.sr, self.rr, self.sl, self.rl = sr, rr, sl, rl
+        self.z, self.y, self.c = place()
+
+    @staticmethod
+    def scratch():
+        dma = pltpu.SemaphoreType.DMA
+        return [dma((LINE,))] * 4 + [dma]
+
+    def right(self, s):
+        slot = self.o_ref.at[self.z - s]
+        source = self.x_ref.at[0] if s == 0 else slot
+        return remote(source, slot, self.sr.at[s], self.rr.at[s + 1], device(self.z + 1, self.y, self.c))
+
+    def left(self, s):
+        slot = self.o_ref.at[self.z + s]
+        source = self.x_ref.at[0] if s == 0 else slot
+        return remote(source, slot, self.sl.at[s], self.rl.at[s + 1], device(self.z - 1, self.y, self.c))
+
+    def own(self):
+        return pltpu.make_async_copy(self.x_ref.at[0], self.o_ref.at[self.z], self.own_sem)
+
+    def start(self):
+        self.own().start()
+
+        @pl.when(self.z < LINE - 1)
+        def _():
+            self.right(0).start()
+
+        @pl.when(self.z > 0)
+        def _():
+            self.left(0).start()
+
+    def step(self, s):
+        @pl.when(self.z >= s)
+        def _():
+            slot = self.o_ref.at[self.z - s]
+            remote(slot, slot, self.sr.at[s], self.rr.at[s], device(self.z, self.y, 1 - self.c)).wait_recv()
+            if s < LINE - 1:
+
+                @pl.when(self.z < LINE - 1)
+                def _():
+                    self.right(s).start()
+
+        @pl.when(self.z + s <= LINE - 1)
+        def _():
+            slot = self.o_ref.at[self.z + s]
+            remote(slot, slot, self.sl.at[s], self.rl.at[s], device(self.z, self.y, 1 - self.c)).wait_recv()
+            if s < LINE - 1:
+
+                @pl.when(self.z > 0)
+                def _():
+                    self.left(s).start()
+
+    def finish(self):
+        self.step(LINE - 1)
+        self.own().wait()
+        for s in range(LINE - 1):
+
+            @pl.when((self.z < LINE - 1) & (self.z >= s))
+            def _():
+                self.right(s).wait_send()
+
+            @pl.when((self.z > 0) & (self.z + s <= LINE - 1))
+            def _():
+                self.left(s).wait_send()
+
+
+class Quad:
+    def __init__(self, x_ref, o_ref, send, recv, own_sem):
+        self.x_ref, self.o_ref, self.send, self.recv, self.own_sem = x_ref, o_ref, send, recv, own_sem
+        self.z, self.y, self.c = place()
+
+    @staticmethod
+    def scratch():
+        dma = pltpu.SemaphoreType.DMA
+        return [dma((4,)), dma((4,)), dma]
+
+    def to(self, d):
+        y = 1 - self.y if d & 2 else self.y
+        c = 1 - self.c if d & 1 else self.c
+        dest = self.o_ref.at[self.y * 2 + self.c]
+        return remote(self.x_ref.at[y * 2 + c], dest, self.send.at[d], self.recv.at[d], device(self.z, y, c))
+
+    def own(self):
+        q = self.y * 2 + self.c
+        return pltpu.make_async_copy(self.x_ref.at[q], self.o_ref.at[q], self.own_sem)
+
+    def start(self):
+        for d in range(1, 4):
+            self.to(d).start()
+        self.own().start()
+
+    def finish(self):
+        self.own().wait()
+        for d in range(1, 4):
+            y = 1 - self.y if d & 2 else self.y
+            c = 1 - self.c if d & 1 else self.c
+            slot = self.o_ref.at[y * 2 + c]
+            remote(slot, slot, self.send.at[d], self.recv.at[d], device(self.z, y, c)).wait_recv()
+            self.to(d).wait_send()
+
+
 class Cross:
     def __init__(self, x_ref, o_ref, ss, rs):
         self.copy = remote(x_ref, o_ref, ss, rs, other_group())
@@ -557,7 +662,7 @@
         ride.finish()
 
 
-def greet_group(crossing=False, plane=False):
+def hail_all():
     k, n = lax.axis_index("blk"), 4 * LINE
 
     def one(i, carry):
@@ -565,29 +670,26 @@
         return carry
 
     lax.fori_loop(1, n, one, 0)
-    more = 0
-    if plane:
-        x, z, y, c = plane_place()
-        for d in range(4):
-            hail(plane_device(1 - x, z, 1 - y if d & 2 else y, 1 - c if d & 1 else c))
-        more = 4
-    elif crossing:
-        hail(other_group())
-        more = 1
-    pl.semaphore_wait(pltpu.get_barrier_semaphore(), n - 1 + more)
+    x, z, y, c = plane_place()
+    for d in range(4):
+        hail(plane_device(1 - x, z, 1 - y if d & 2 else y, 1 - c if d & 1 else c))
+
+
+def hailed_by_all():
+    pl.semaphore_wait(pltpu.get_barrier_semaphore(), 4 * LINE - 1 + 4)
 
 
 class GroupGather:
     def __init__(self, all_ref, sems):
         self.all_ref = all_ref
-        self.sr, self.rr, self.sl, self.rl, self.sy, self.ry, self.sc, self.rc = sems
+        self.sr, self.rr, self.sl, self.rl, self.sy, self.ry, self.sc, self.rc, self.se, self.re = sems
         self.z, self.y, self.c = place()
         self.half = all_ref.shape[0] // (4 * LINE * HALVES)
 
     @staticmethod
     def scratch():
         dma = pltpu.SemaphoreType.DMA
-        return [dma((LINE, HALVES))] * 6 + [dma((2 * LINE, HALVES))] * 2
+        return [dma((LINE, HALVES))] * 6 + [dma((2 * LINE, HALVES))] * 2 + [dma((2,))] * 2
 
     def block(self, z, y, h, c=None):
         c = self.c if c is None else c
@@ -604,6 +706,11 @@
     def across(self, zz, h):
         block = self.block(zz, self.y, h)
         return remote(block, block, self.sy.at[zz, h], self.ry.at[zz, h], device(self.z, 1 - self.y, self.c))
+
+    def detour(self, to_right):
+        block = self.block(self.z, 1 - self.y, HALVES - 1)
+        where = device(self.z + 1, self.y, self.c) if to_right else device(self.z - 1, self.y, self.c)
+        return remote(block, block, self.se.at[to_right], self.re.at[to_right], where)
 
     def twin(self, zz, yy, h):
         block = self.block(zz, yy, h)
@@ -629,12 +736,26 @@
         for h in range(HALVES):
             self.twin(z, y, h).start()
 
-    def from_across(self, zz, h):
-        self.arrival(self.block(zz, 1 - self.y, h), self.sy.at[zz, h], self.ry.at[zz, h])
+    def from_across(self, zz, h, distance, to_right=0):
+        if distance == 1 and h == HALVES - 1:
+            self.arrival(self.block(zz, 1 - self.y, h), self.se.at[to_right], self.re.at[to_right])
+        else:
+            self.arrival(self.block(zz, 1 - self.y, h), self.sy.at[zz, h], self.ry.at[zz, h])
+        if distance == 0 and h == HALVES - 1:
+
+            @pl.when(self.z < LINE - 1)
+            def _():
+                self.detour(1).start()
+
+            @pl.when(self.z > 0)
+            def _():
+                self.detour(0).start()
+
         self.twin(zz, 1 - self.y, h).start()
 
-    def pass_on(self, zz, h):
-        self.across(zz, h).start()
+    def pass_on(self, zz, h, distance):
+        if distance > 1 or h < HALVES - 1:
+            self.across(zz, h).start()
         self.twin(zz, self.y, h).start()
 
     def run(self):
@@ -651,7 +772,7 @@
                         def _():
                             self.right(s + 1, h).start()
 
-                    self.pass_on(z - s, h)
+                    self.pass_on(z - s, h, s)
 
                 @pl.when(z + s <= LINE - 1)
                 def _():
@@ -662,29 +783,29 @@
                         def _():
                             self.left(s + 1, h).start()
 
-                    self.pass_on(z + s, h)
+                    self.pass_on(z + s, h, s)
 
                 if s == 1:
-                    self.from_across(z, h)
+                    self.from_across(z, h, 0)
                 else:
 
                     @pl.when(z >= s - 1)
                     def _():
-                        self.from_across(z - s + 1, h)
+                        self.from_across(z - s + 1, h, s - 1, 1)
 
                     @pl.when(z + s - 1 <= LINE - 1)
                     def _():
-                        self.from_across(z + s - 1, h)
+                        self.from_across(z + s - 1, h, s - 1, 0)
 
         for h in range(HALVES):
 
             @pl.when(z >= LINE - 1)
             def _():
-                self.from_across(z - LINE + 1, h)
+                self.from_across(z - LINE + 1, h, LINE - 1)
 
             @pl.when(z <= 0)
             def _():
-                self.from_across(z + LINE - 1, h)
+                self.from_across(z + LINE - 1, h, LINE - 1)
 
         for h in range(HALVES):
             for zz in range(LINE):
@@ -694,9 +815,25 @@
 
     def finish(self):
         z = self.z
+
+        @pl.when(z < LINE - 1)
+        def _():
+            self.detour(1).wait_send()
+
+        @pl.when(z > 0)
+        def _():
+            self.detour(0).wait_send()
+
         for h in range(HALVES):
             for zz in range(LINE):
-                self.across(zz, h).wait_send()
+                if h < HALVES - 1:
+                    self.across(zz, h).wait_send()
+                else:
+
+                    @pl.when((zz != z - 1) & (zz != z + 1))
+                    def _():
+                        self.across(zz, h).wait_send()
+
                 for yy in range(2):
                     self.twin(zz, yy, h).wait_send()
             for s in range(1, LINE):
@@ -720,16 +857,17 @@
 class GroupScatter:
     def __init__(self, part_ref, bufs, sems):
         self.part_ref = part_ref
-        self.twins, self.ysend, self.yrecv, self.zsend, self.zright, self.zleft = bufs
-        self.sc, self.rc, self.sy, self.ry, self.sz, self.rzr, self.rzl = sems
+        self.twins, self.ysend, self.yrecv, self.zsend, self.zrecv, self.esend, self.erecv = bufs
+        self.sc, self.rc, self.sy, self.ry, self.sz, self.rzr, self.rzl, self.se, self.re = sems
         self.z, self.y, self.c = place()
         self.half = part_ref.shape[0] // (4 * LINE * HALVES)
 
     @staticmethod
     def scratch(rows, columns):
         dma = pltpu.SemaphoreType.DMA
-        bufs = [pltpu.VMEM((n, rows, columns), jnp.bfloat16) for n in (2 * LINE, LINE, LINE, LINE - 1, LINE, LINE)]
-        return bufs, [dma((2 * LINE, HALVES))] * 2 + [dma((LINE, HALVES))] * 5
+        bufs = [pltpu.VMEM((n, rows, columns), jnp.bfloat16) for n in (2 * LINE, LINE, LINE, LINE - 1, LINE + 1)]
+        bufs += [pltpu.VMEM((2, rows // HALVES, columns), jnp.bfloat16)] * 2
+        return bufs, [dma((2 * LINE, HALVES))] * 2 + [dma((LINE, HALVES))] * 5 + [dma((2,))] * 2
 
     def part(self, h):
         return pl.ds(h * self.half, self.half)
@@ -749,13 +887,18 @@
         return remote(source, dest, self.sy.at[t, h], self.ry.at[t, h], device(self.z, 1 - self.y, self.c))
 
     def along(self, d, t, h, to_right):
-        buf, sem = (self.zright, self.rzr) if to_right else (self.zleft, self.rzl)
+        sem = self.rzr if to_right else self.rzl
         where = device(self.z + 1, self.y, self.c) if to_right else device(self.z - 1, self.y, self.c)
-        return remote(self.zsend.at[t, self.part(h)], buf.at[d, self.part(h)], self.sz.at[t, h], sem.at[d, h], where)
+        slot = d if to_right else self.from_right(d, self.z - 1)
+        return remote(self.zsend.at[t, self.part(h)], self.zrecv.at[slot, self.part(h)], self.sz.at[t, h], sem.at[d, h], where)
+
+    @staticmethod
+    def from_right(d, z):
+        return jnp.where(d == z, LINE, d)
 
     def arrived(self, d, h, to_right):
-        buf, sem = (self.zright, self.rzr) if to_right else (self.zleft, self.rzl)
-        slot = buf.at[d, self.part(h)]
+        sem = self.rzr if to_right else self.rzl
+        slot = self.zrecv.at[d if to_right else self.from_right(d, self.z), self.part(h)]
         remote(slot, slot, self.sz.at[0, h], sem.at[d, h], device(self.z, self.y, 1 - self.c)).wait_recv()
 
     def wide(self, ref, slot, h):
@@ -764,18 +907,64 @@
     def chip(self, t, own_y, h):
         return self.part_ref[self.rows(t, own_y, self.c, h)].astype(jnp.float32) + self.wide(self.twins, t * 2 + own_y, h)
 
-    def start(self):
-        for own_y in (0, 1):
-            for t in range(LINE):
-                for h in range(HALVES):
-                    self.twin(t, own_y, h).start()
+    def owner(self, t, own_y, c):
+        return index_of(order_at(self.z, t), self.y if own_y else 1 - self.y, c)
+
+    def start(self, t, own_y):
+        for h in range(HALVES):
+            self.twin(t, own_y, h).start()
+
+    def detour(self, to_right):
+        where = device(self.z + 1, self.y, self.c) if to_right else device(self.z - 1, self.y, self.c)
+        source, dest = self.esend.at[to_right], self.erecv.at[to_right]
+        return remote(source, dest, self.se.at[to_right], self.re.at[to_right], where)
+
+    def detoured(self, t, h):
+        d = order_at(self.z, t)
+        return (d == self.z + 1, d == self.z - 1) if h == HALVES - 1 and t < LINE - 1 else (False, False)
 
     def first(self):
+        z = self.z
         for t in range(LINE):
             for h in range(HALVES):
                 self.twin(t, 0, h).wait_recv()
-                self.ysend[t, self.part(h)] = self.chip(t, 0, h).astype(jnp.bfloat16)
-                self.across(t, h).start()
+                if h < HALVES - 1:
+                    self.ysend[t, self.part(h)] = self.chip(t, 0, h).astype(jnp.bfloat16)
+                    self.across(t, h).start()
+                elif t < LINE - 1:
+                    right, left = self.detoured(t, h)
+                    for to_right, here in ((1, right), (0, left)):
+
+                        @pl.when(here)
+                        def _():
+                            self.esend[to_right] = self.chip(t, 0, h).astype(jnp.bfloat16)
+                            self.detour(to_right).start()
+
+                    @pl.when(jnp.logical_not(right | left))
+                    def _():
+                        self.ysend[t, self.part(h)] = self.chip(t, 0, h).astype(jnp.bfloat16)
+                        self.across(t, h).start()
+                else:
+
+                    def added(to_right):
+                        slot = self.erecv.at[to_right]
+                        where = device(z, self.y, 1 - self.c)
+                        remote(slot, slot, self.se.at[to_right], self.re.at[to_right], where).wait_recv()
+                        return self.erecv[to_right].astype(jnp.float32)
+
+                    @pl.when(z == 0)
+                    def _():
+                        self.ysend[t, self.part(h)] = (self.chip(t, 0, h) + added(0)).astype(jnp.bfloat16)
+
+                    @pl.when(z == LINE - 1)
+                    def _():
+                        self.ysend[t, self.part(h)] = (self.chip(t, 0, h) + added(1)).astype(jnp.bfloat16)
+
+                    @pl.when((z > 0) & (z < LINE - 1))
+                    def _():
+                        self.ysend[t, self.part(h)] = (self.chip(t, 0, h) + added(0) + added(1)).astype(jnp.bfloat16)
+
+                    self.across(t, h).start()
 
     def second(self, o_ref):
         z = self.z
@@ -783,7 +972,18 @@
             d = order_at(z, t)
             for h in range(HALVES):
                 self.twin(t, 1, h).wait_recv()
-                self.across(t, h).wait_recv()
+                if h == HALVES - 1 and t < LINE - 1:
+                    right, left = self.detoured(t, h)
+
+                    @pl.when(right | left)
+                    def _():
+                        self.yrecv[t, self.part(h)] = jnp.zeros((self.half, self.yrecv.shape[2]), jnp.bfloat16)
+
+                    @pl.when(jnp.logical_not(right | left))
+                    def _():
+                        self.across(t, h).wait_recv()
+                else:
+                    self.across(t, h).wait_recv()
 
                 def summed(t=t, h=h):
                     return self.chip(t, 1, h) + self.wide(self.yrecv, t, h)
@@ -794,7 +994,6 @@
                         @pl.when((d > z) if to_right else (d < z))
                         def _():
                             first = (z == 0) if to_right else (z == LINE - 1)
-                            buf = self.zright if to_right else self.zleft
 
                             @pl.when(first)
                             def _():
@@ -803,7 +1002,7 @@
                             @pl.when(jnp.logical_not(first))
                             def _():
                                 self.arrived(d, h, to_right)
-                                self.zsend[t, self.part(h)] = (summed() + self.wide(buf, d, h)).astype(jnp.bfloat16)
+                                self.zsend[t, self.part(h)] = (summed() + self.wide(self.zrecv, d, h)).astype(jnp.bfloat16)
 
                             self.along(d, t, h, to_right).start()
                 else:
@@ -818,20 +1017,33 @@
 
                     @pl.when(z == 0)
                     def _():
-                        o_ref[self.part(h)] = summed() + self.wide(self.zleft, z, h)
+                        o_ref[self.part(h)] = summed() + self.wide(self.zrecv, LINE, h)
 
                     @pl.when(z == LINE - 1)
                     def _():
-                        o_ref[self.part(h)] = summed() + self.wide(self.zright, z, h)
+                        o_ref[self.part(h)] = summed() + self.wide(self.zrecv, z, h)
 
                     @pl.when((z > 0) & (z < LINE - 1))
                     def _():
-                        o_ref[self.part(h)] = summed() + self.wide(self.zright, z, h) + self.wide(self.zleft, z, h)
+                        o_ref[self.part(h)] = summed() + self.wide(self.zrecv, z, h) + self.wide(self.zrecv, LINE, h)
 
     def finish(self):
+        for to_right, here in ((1, self.z < LINE - 1), (0, self.z > 0)):
+
+            @pl.when(here)
+            def _():
+                self.detour(to_right).wait_send()
+
         for h in range(HALVES):
             for t in range(LINE):
-                self.across(t, h).wait_send()
+                if h == HALVES - 1 and t < LINE - 1:
+                    right, left = self.detoured(t, h)
+
+                    @pl.when(jnp.logical_not(right | left))
+                    def _():
+                        self.across(t, h).wait_send()
+                else:
+                    self.across(t, h).wait_send()
                 self.twin(t, 0, h).wait_send()
                 self.twin(t, 1, h).wait_send()
             for t in range(LINE - 1):
@@ -1009,7 +1221,7 @@
         own = self.part_ref[self.rows(which, self.c, h)].astype(jnp.float32)
         return own + self.twins[which, h * self.half : (h + 1) * self.half].astype(jnp.float32)
 
-    def first(self):
+    def over_first(self):
         self.twin(0).wait_recv()
         self.xs[0] = self.chip(0, 0).astype(jnp.bfloat16)
         self.over_x(0).start()
@@ -1018,6 +1230,8 @@
         self.twin(1).wait_recv()
         self.xs[1] = self.chip(1, 0).astype(jnp.bfloat16)
         self.over_x(1).start()
+
+    def first(self):
         self.twin(2).wait_recv()
         self.ys[1] = self.chip(2, 1).astype(jnp.bfloat16)
         self.over_y(1).start()
@@ -1060,13 +1274,14 @@
 
     def copies(self):
         slot = self.got_ref.at[plane_index(self.x, self.y, self.c)]
+        own = self.own_ref.at[0] if len(self.own_ref.shape) == len(self.got_ref.shape) else self.own_ref
         for d, x, y, c in self.others():
-            yield remote(self.own_ref, slot, self.send.at[d], self.recv.at[d], plane_device(x, self.z, y, c))
+            yield remote(own, slot, self.send.at[d], self.recv.at[d], plane_device(x, self.z, y, c))
 
     def start(self):
         for copy in self.copies():
             copy.start()
-        self.got_ref[plane_index(self.x, self.y, self.c)] = self.own_ref[...]
+        self.got_ref[plane_index(self.x, self.y, self.c)] = self.own_ref[...].reshape(self.got_ref.shape[1:])
 
     def finish(self):
         for d, x, y, c in self.others():
@@ -1199,6 +1414,7 @@
     total = r.hb_all.shape[0]
     tiles, chunks, per_tile = total // TILE, total // CHUNK, TILE // CHUNK
     gather = GroupGather(r.hb_all, r.gather_sems)
+    hail_all()
     gains, biases = of_layer(r.gains, layer), of_layer(r.biases, layer)
     if first:
         load_qkv = pltpu.make_async_copy(r.w_qkv, r.qkv_in, r.prep_sem.at[0])
@@ -1212,11 +1428,13 @@
     value = r.x_in[...].astype(jnp.float32)
     r.hb_all[pl.ds(index * rows, rows)] = normed(value, gains[0][...], biases[0][...]).astype(jnp.bfloat16)
     head_ride = Swap(r.head_src.at[0], r.head_blocks, *r.head_sems) if first else None
-    unit_ride = Swap(r.unit_src.at[0], r.unit_blocks, *r.unit_sems) if first else None
-    down_ride = Trade(r.w_down.at[layer, pl.ds(x, 1)], r.down_blocks, *r.down_sems)
+    down_ride = Share(r.w_down.at[layer, pl.ds(x, 1)], r.down_blocks, *r.down_sems)
     out_ride = Trade(r.w_out.at[layer, pl.ds(x, 1)], r.out_got, *r.out_sems)
-    next_rides = [Swap(r.head_src.at[1], r.next_head, *r.next_head_sems)] if first else []
-    next_rides += [Swap(r.unit_src.at[1], r.next_unit, *r.next_unit_sems)] if first else []
+    if first:
+        quads = [Quad(r.unit_src.at[l], r.unit_quad.at[l], *r.quad_sems[3 * l : 3 * l + 3]) for l in range(2)]
+        unit_ride = Share(r.unit_quad.at[pl.ds(0, 1)], r.unit_blocks, *r.unit_sems)
+        next_unit_ride = Share(r.unit_quad.at[pl.ds(1, 1)], r.next_unit, *r.next_unit_sems)
+        next_head_ride = Swap(r.head_src.at[1], r.next_head, *r.next_head_sems)
     if first:
         load_qkv.wait()
         for head in range(4 * LINE):
@@ -1224,7 +1442,7 @@
     load_head = pltpu.make_async_copy(r.head_blocks, r.head_in, r.load_sem.at[0])
     load_unit = pltpu.make_async_copy(r.unit_blocks, r.unit_in, r.load_sem.at[1])
     load_down = pltpu.make_async_copy(r.down_blocks, r.down_w, r.load_sem.at[2])
-    greet_group(plane=True)
+    hailed_by_all()
     if first:
         head_ride.start()
     gather.start()
@@ -1233,37 +1451,39 @@
     unit_columns(mids, unit_slot, (r.mid_gain, r.mid_shift, r.mid_bias))
     head_bias = [own_head(biases[row], index) for row in (3, 4)] + [jnp.zeros((1, 64), jnp.float32)]
     head_bias = jnp.concatenate(head_bias, axis=1)
+    if not first:
+        load_head.start()
+        r.dy_all[pl.ds(slot * rows, rows)] = r.dy[...]
+        load_unit.start()
     if first:
-        for head in range(4 * LINE):
-            r.head_src[1, head] = fold_head(r.qkv_in[1], head)
         for l in range(2):
             pltpu.make_async_copy(r.unit_src.at[l], r.unit_src.at[l], r.prep_sem.at[1 + l]).wait()
-    if not first:
-        load_head.start()
-        load_unit.start()
+        quads[0].start()
     gather.run()
     if first:
+        quads[0].finish()
         unit_ride.start()
-        head_ride.finish()
-        load_head.start()
-    else:
-        down_ride.start()
-    load_head.wait()
-    unfold_head(r.head_in, r.head_w)
-
-    def project(t, carry):
-        rows_t = (mul(r.hb_all[tile_at(t)], r.head_w[...]) + head_bias).astype(jnp.bfloat16)
-        r.flat[pl.ds(t * per_tile, per_tile)] = rows_t.reshape(per_tile, CHUNK, 192)
-        return carry
-
-    lax.fori_loop(0, tiles, project, 0)
     out_ride.finish()
     out_rows = r.out_all.shape[0] // PLANE
     for zz in range(LINE):
         r.out_all[pl.ds(slot * out_rows + zz * 32, 32)] = r.out_got[zz]
     out_gather = PlaneGather(r.out_all, r.out_gather_sems)
     out_gather.start()
-
+    dy_gather = None if first else PlaneGather(r.dy_all, r.dy_gather_sems)
+    if first:
+        head_ride.finish()
+        load_head.start()
+    else:
+        dy_gather.start()
+    load_head.wait()
+    unfold_head(r.head_in, r.head_w)
+
+    def project(t, carry):
+        rows_t = (mul(r.hb_all[tile_at(t)], r.head_w[...]) + head_bias).astype(jnp.bfloat16)
+        r.flat[pl.ds(t * per_tile, per_tile)] = rows_t.reshape(per_tile, CHUNK, 192)
+        return carry
+
+    lax.fori_loop(0, tiles, project, 0)
     def arrange(p, carry):
         r.qvk[p] = r.flat[r.table[p]]
         return carry
@@ -1315,8 +1535,14 @@
         pairs = (jnp.transpose(mixed) * r.scales[layer, index]).reshape(per_tile, 2, CHUNK // 2, 64)
         pairs = jnp.concatenate([pairs[:, 0], pairs[:, 1]], axis=-1).astype(jnp.bfloat16)
         r.pairs[i * per_tile : (i + 1) * per_tile] = pairs
-        if i == 2:
+        if i == 2 and first:
+            unit_ride.step(1)
+        if i == 3:
             out_gather.near()
+    if first:
+        unit_ride.step(2)
+    else:
+        dy_gather.near()
     per_block = rows // CHUNK
 
     def pack(p, carry):
@@ -1327,14 +1553,37 @@
     mix = Swap(r.packed, r.mixed, *r.mix_sems, per=per_block)
     mix.start()
     out_gather.far()
+    if not first:
+        dy_gather.far()
     for s in range(PLANE):
         for zz in range(LINE):
             at = natural_rows(s, zz)
             r.out_w[at : at + 32] = r.out_all[s * out_rows + zz * 32 : s * out_rows + zz * 32 + 32]
     out_gather.finish()
+
+    def turn_units():
+        for j in range(2 * LINE):
+            pair = r.unit_in[j // 2, j % 2 * 2 : j % 2 * 2 + 2].reshape(128, r.unit_in.shape[3])
+            r.unit_t[:, 128 * j : 128 * j + 128] = jnp.transpose(pair)
+
+    if first:
+        for head in range(4 * LINE):
+            r.head_src[1, head] = fold_head(r.qkv_in[1], head)
+    else:
+        load_unit.wait()
+        turn_units()
+    saves = [
+        pltpu.make_async_copy(source, dest, r.save_sem.at[i])
+        for i, (source, dest) in enumerate(
+            (
+                (r.hb_all, r.hb_all_out), (r.qvk, r.qvk_out), (r.out_w, r.out_w_out), (r.rows_all, r.rows_all_out),
+                (r.unit_t, r.unit_t_out), (r.act, r.act_out), (r.slope, r.slope_out), (r.mid, r.mid_out),
+            )
+        )
+    ]
+    start_all(saves[:3])
     mix.finish()
-    if first:
-        down_ride.start()
+    down_ride.start()
     for g in range(columns // 128):
         left, right = (
             r.mixed[h * per_block : (h + 1) * per_block].reshape(rows // 2, 128) for h in (2 * g, 2 * g + 1)
@@ -1359,14 +1608,13 @@
     hidden = r.act.shape[0]
     width = r.act.shape[1] // 2
     if first:
-        plane_gather.near()
-        plane_gather.far()
         unit_ride.finish()
         load_unit.start()
-    load_unit.wait()
-    for j in range(r.unit_in.shape[0] // 2):
-        pair = r.unit_in[2 * j : 2 * j + 2].reshape(128, hidden)
-        r.unit_t[:, 128 * j : 128 * j + 128] = jnp.transpose(pair)
+        quads[1].start()
+    down_ride.step(1)
+    if first:
+        load_unit.wait()
+        turn_units()
 
     def climb(th):
         at = span_at(th, width)
@@ -1387,16 +1635,19 @@
         r.own_stat[0:1, at] = mean
         r.own_stat[1:2, at] = jnp.sum(apart * apart, axis=0, keepdims=True)
 
-    if not first:
-        plane_gather.near()
+    plane_gather.near()
+    down_ride.step(2)
     climb(x)
-    if not first:
-        plane_gather.far()
+    plane_gather.far()
     climb(1 - x)
     pool.start()
     down_ride.finish()
     load_down.start()
-    start_all(next_rides)
+    if first:
+        quads[1].finish()
+        next_unit_ride.start()
+        next_head_ride.start()
+    start_all(saves[3:7])
     pool.finish()
     load_down.wait()
     means = [r.got_stat[i, 0:1] for i in range(PLANE)]
@@ -1422,28 +1673,32 @@
     descend(1 - x)
     plane_scatter.twin(0).start()
     plane_scatter.twin(1).start()
+    plane_scatter.over_first()
     descend(x)
     plane_scatter.twin(2).start()
     plane_scatter.twin(3).start()
-    saved = (
-        (r.hb_all, r.hb_all_out), (r.qvk, r.qvk_out), (r.out_w, r.out_w_out), (r.rows_all, r.rows_all_out),
-        (r.unit_t, r.unit_t_out), (r.act, r.act_out), (r.slope, r.slope_out), (r.mid, r.mid_out),
-    )
-    saves = [pltpu.make_async_copy(source, dest, r.save_sem.at[i]) for i, (source, dest) in enumerate(saved)]
-    for save in saves:
-        save.start()
+    if not first:
+        dy_gather.finish()
+        saves.append(pltpu.make_async_copy(r.dy_all, r.dy_all_out, r.save_sem.at[8]))
+    start_all(saves[7:])
     plane_scatter.first()
+    if first:
+        next_unit_ride.step(1)
     plane_scatter.second()
+    if first:
+        next_unit_ride.step(2)
     plane_scatter.finish(r.result)
     r.y_out[...] = (r.middle[...] + (r.result[...] + biases[6][...])).astype(r.y_out.dtype)
     gather.finish()
     plane_gather.finish()
     for save in saves:
         save.wait()
-    finish_all(next_rides)
-
-
-def layer_forward_kernel(layer, table, x_in, params, blocks, y_type, collective_id):
+    if first:
+        next_unit_ride.finish()
+        next_head_ride.finish()
+
+
+def layer_forward_kernel(layer, table, x_in, params, blocks, dy, y_type, collective_id):
     rows, columns = x_in.shape
     hidden_all = params.mid_gain.shape[1]
     total, plane_rows, hidden = rows * 4 * LINE, rows * PLANE, hidden_all // PLANE
@@ -1453,13 +1708,13 @@
     full = lambda *shape: pltpu.VMEM(shape, jnp.float32)
     low_out = lambda *shape: jax.ShapeDtypeStruct(shape, jnp.bfloat16)
     full_out = lambda *shape: jax.ShapeDtypeStruct(shape, jnp.float32)
-    swap_sems, trade_sems = Swap.scratch(), Trade.scratch()
+    swap_sems, trade_sems, share_sems = Swap.scratch(), Trade.scratch(), Share.scratch()
     inputs = dict(
         table=(table, smem), scales=(params.head_scale, smem), x_in=(x_in, vmem), gains=(params.vec_gain, vmem),
         biases=(params.vec_bias, vmem), mid_gain_all=(params.mid_gain, vmem), mid_bias_all=(params.mid_bias, vmem),
         w_down=(params.w_down, anywhere), w_out=(params.w_out, anywhere),
     )
-    head_shape, unit_shape = (4 * LINE, 32, 384), (4 * LINE, columns // (4 * LINE), hidden)
+    head_shape, unit_shape = (4 * LINE, 32, 384), (LINE, 4, columns // (4 * LINE), hidden)
     outputs = dict(
         y_out=(jax.ShapeDtypeStruct((rows, columns), y_type), vmem), branch=(full_out(rows, columns), vmem),
         middle=(full_out(rows, columns), vmem), ab=(low_out(rows, columns), vmem),
@@ -1476,14 +1731,15 @@
         head_got, unit_got = (low_out(*head_shape), anywhere), (low_out(*unit_shape), anywhere)
         outputs.update(head_blocks=head_got, unit_blocks=unit_got, next_head=head_got, next_unit=unit_got)
     else:
-        inputs.update(head_blocks=(blocks.head, anywhere), unit_blocks=(blocks.unit, anywhere))
+        inputs.update(head_blocks=(blocks.head, anywhere), unit_blocks=(blocks.unit, anywhere), dy=(dy, vmem))
+        outputs.update(dy_all_out=(low_out(plane_rows, columns), anywhere))
     plane_bufs, plane_sems = PlaneScatter.scratch(rows, columns)
     scratch = dict(
         hb_all=low(total, columns), flat=low(total // CHUNK, CHUNK, 192),
         qvk=low(total // CHUNK, CHUNK, 192), queries=low(total, 64), keys=low(total, 64),
         values_t=low(64, total), pairs=low(total // CHUNK, CHUNK // 2, 128),
         packed=low(total // CHUNK, CHUNK // 2, 128), mixed=low(total // CHUNK, CHUNK // 2, 128), head_in=low(4 * LINE, 32, 384), head_w=low(columns, 192),
-        unit_in=low(4 * LINE, columns // (4 * LINE), hidden), unit_t=low(hidden, columns),
+        unit_in=low(*unit_shape), unit_t=low(hidden, columns),
         down_w=low(LINE, hidden // LINE, columns), out_got=low(LINE, 32, columns),
         out_all=low(columns, columns), out_w=low(columns, columns), rows_all=low(plane_rows, columns),
         act=full(hidden, plane_rows), slope=low(hidden, plane_rows), mid=low(hidden, plane_rows),
@@ -1491,14 +1747,16 @@
         result=full(rows, columns), plane_bufs=plane_bufs, plane_sems=plane_sems,
         gather_sems=GroupGather.scratch(), plane_gather_sems=PlaneGather.scratch(),
         out_gather_sems=PlaneGather.scratch(), pool_sems=([dma((PLANE,)), dma((PLANE,))]),
-        head_sems=swap_sems, unit_sems=swap_sems, next_head_sems=swap_sems, next_unit_sems=swap_sems,
-        mix_sems=swap_sems, down_sems=trade_sems, out_sems=trade_sems, load_sem=dma((3,)),
-        save_sem=dma((8,)),
+        head_sems=swap_sems, unit_sems=share_sems, next_head_sems=swap_sems, next_unit_sems=share_sems,
+        mix_sems=swap_sems, down_sems=share_sems, out_sems=trade_sems, load_sem=dma((3,)),
+        save_sem=dma((9,)),
     )
     scratch.update(mid_gain=full(hidden, 1), mid_shift=full(hidden, 1), mid_bias=full(hidden, 1))
     if first:
         scratch.update(qkv_in=low(*params.w_qkv.shape), head_src=low(2, *head_shape), prep_sem=dma((3,)))
-        scratch.update(unit_src=low(2, 4, columns // (4 * LINE), hidden))
+        scratch.update(unit_src=low(2, *unit_shape[1:]), unit_quad=low(2, *unit_shape[1:]), quad_sems=Quad.scratch() * 2)
+    else:
+        scratch.update(dy_all=low(plane_rows, columns), dy_gather_sems=PlaneGather.scratch())
     kernel = functools.partial(forward_kernel, layer, hidden_all)
     call = lambda body, **how: pl.pallas_call(body, name="layer_forward", **how)
     return launch(call, kernel, inputs, outputs, scratch, collective_id, 95, 56)
@@ -1544,6 +1802,28 @@
         o_ref[...] = total
         for i in range(LINE + 2):
             self.copy(i).wait_send()
+
+
+class QuickSum:
+    def __init__(self, own_ref, plane_got, line_got, sems):
+        self.own_ref, self.line_got = own_ref, line_got
+        self.pool = PlanePool(own_ref, plane_got, *sems[0:2])
+        self.trade = Trade(own_ref, line_got, *sems[2:5])
+        self.plane_got = plane_got
+
+    @staticmethod
+    def scratch(shape):
+        dma = pltpu.SemaphoreType.DMA
+        got = [pltpu.VMEM((n, *shape), jnp.float32) for n in (PLANE, LINE)]
+        return got, [dma((PLANE,))] * 2 + Trade.scratch()
+
+    def run(self, o_ref):
+        self.pool.start()
+        self.pool.finish()
+        self.own_ref[0] = functools.reduce(jnp.add, [self.plane_got[i] for i in range(PLANE)])
+        self.trade.start()
+        self.trade.finish()
+        o_ref[...] = functools.reduce(jnp.add, [self.line_got[zz] for zz in range(LINE)])
 
 
 OUT_BIAS, DOWN_BIAS, QUERY_BIAS, VALUE_BIAS, SCALES, MID, SMALL = 6, 7, 8, 9, 10, 12, 24
@@ -1584,13 +1864,15 @@
     ]
     if not first:
         bulk = AllSum(r.bulk, *r.bulk_sum)
-        rest = AllSum(r.rest, *r.rest_sum)
+        rest = QuickSum(r.rest, *r.rest_got, r.rest_sems)
+    hail_all()
     gains = of_layer(r.gains, layer)
     r.small[...] = jnp.zeros_like(r.small)
     dy = r.dy[...].astype(jnp.float32)
     dy_low = dy.astype(jnp.bfloat16)
     r.small[DOWN_BIAS : DOWN_BIAS + 1] = jnp.sum(dy_low.astype(jnp.float32), axis=0, keepdims=True)
-    dy_all[pl.ds(plane_index(x, y, c) * rows, rows)] = dy_low
+    if not first:
+        dy_all[pl.ds(plane_index(x, y, c) * rows, rows)] = dy_low
     loads = [
         pltpu.make_async_copy(source, dest, r.load_sem.at[i])
         for i, (source, dest) in enumerate(
@@ -1600,10 +1882,14 @@
             )
         )
     ]
+    load_dy = pltpu.make_async_copy(r.dy_all_in, dy_all, r.load_sem.at[8]) if first else None
+    if first:
+        load_dy.start()
     for load in loads[:6]:
         load.start()
-    greet_group(plane=True)
-    plane_gather.start()
+    hailed_by_all()
+    if not first:
+        plane_gather.start()
     for load in loads[6:]:
         load.start()
 
@@ -1638,11 +1924,15 @@
 
         lax.fori_loop(0, hidden // 256, units, 0)
 
-    plane_gather.near()
+    if first:
+        load_dy.wait()
+    else:
+        plane_gather.near()
     loads[0].wait()
     loads[1].wait()
     climb(x)
-    plane_gather.far()
+    if not first:
+        plane_gather.far()
     climb(1 - x)
     pool.start()
     loads[4].wait()
@@ -1674,6 +1964,7 @@
     descend(1 - x)
     plane_scatter.twin(0).start()
     plane_scatter.twin(1).start()
+    plane_scatter.over_first()
     descend(x)
     plane_scatter.twin(2).start()
     plane_scatter.twin(3).start()
@@ -1684,7 +1975,8 @@
         grad = jnp.transpose(mul(r.du[ut * 256 : (ut + 1) * 256], x_all[...])).astype(jnp.bfloat16)
         r.gup[:, :, ut * 256 : (ut + 1) * 256] = grad.reshape(r.gup.shape[0], -1, 256)
     plane_scatter.finish(r.dffn)
-    plane_gather.finish()
+    if not first:
+        plane_gather.finish()
 
     back, r.small[2:3], r.small[5:6] = normed_back(r.middle[...], gains[2][...], r.dffn[...])
     r.dmiddle[...] = dy + back
@@ -1738,19 +2030,20 @@
     lax.fori_loop(0, tiles, prepare, 0)
     load_head.wait()
     unfold_head(r.head_fold, r.head_w)
+    out_scatter.over_first()
     out_scatter.first()
     mix.finish()
     unit_ride.start()
 
     def arrange(p, carry):
-        r.pairs[p] = r.mixed[r.table[p]]
+        r.packed[p] = r.mixed[r.table[p]]
         return carry
 
     lax.fori_loop(0, chunks, arrange, 0)
 
     def unpack(t, carry):
         at = tile_at(t)
-        pairs = r.pairs[pl.ds(t * per_tile, per_tile)].astype(jnp.float32)
+        pairs = r.packed[pl.ds(t * per_tile, per_tile)].astype(jnp.float32)
         pairs = jnp.concatenate([pairs[:, :, 0:64], pairs[:, :, 64:128]], axis=1).reshape(TILE, 64)
         low = (pairs * scale).astype(jnp.bfloat16)
         r.dout[at] = low
@@ -1782,16 +2075,16 @@
         if i > 0:
             total_dq = lax.fori_loop(0, i, functools.partial(block, masked=False), total_dq)
         r.dquery_t[:, at] = total_dq * 0.125
-        if i == 1:
+        if i == 2:
             out_scatter.second()
             if not first:
                 bulk.step(1)
-        if i == 2:
-            out_scatter.finish(r.out_sum)
-            r.out_own[...] = r.out_sum[...].reshape(r.out_own.shape).astype(jnp.bfloat16)
-            out_ride.start()
-            if not first:
-                bulk.step(2)
+    out_sum = r.dffn.at[pl.ds(0, out_rows)]
+    out_scatter.finish(out_sum)
+    r.out_own[...] = out_sum[...].reshape(r.out_own.shape).astype(jnp.bfloat16)
+    out_ride.start()
+    if not first:
+        bulk.step(2)
 
     head_bias = jnp.zeros((1, 192), jnp.float32)
     for i in range(tiles):
@@ -1809,12 +2102,16 @@
 
     lax.fori_loop(0, chunks, restore, 0)
 
-    def project(t, carry):
-        r.wide[tile_at(t)] = mul(chunks_of(r.flat, t), r.head_w[...], NT).astype(jnp.bfloat16)
-        return carry
-
-    lax.fori_loop(0, tiles, project, 0)
-    scatter.start()
+    def project(owner):
+        rows_of = r.flat[pl.ds(owner * per_block, per_block)].reshape(rows, 192)
+        r.wide[pl.ds(owner * rows, rows)] = mul(rows_of, r.head_w[...], NT).astype(jnp.bfloat16)
+
+    for own_y in (0, 1):
+        for t in range(LINE):
+            for other_core in (1, 0):
+                project(scatter.owner(t, own_y, 1 - c if other_core else c))
+                if other_core:
+                    scatter.start(t, own_y)
     for t in range(tiles):
         tile_load(t).wait()
         grad = mul(chunks_of(r.flat, t), r.hb_tiles[t % 2], TN)
@@ -1857,16 +2154,12 @@
     r.small[0:1] = gain_grad
     r.small[3:4] = shift_grad
     if not first:
-        r.rest[0:1] = gain_grad
-        r.rest[1:2] = shift_grad
-        r.rest[2:5] = r.small[QUERY_BIAS : SCALES + 1]
-        r.rest[5:8] = jnp.zeros((3, columns), jnp.float32)
-        rest.start()
+        r.rest[0, 0:1] = gain_grad
+        r.rest[0, 1:2] = shift_grad
+        r.rest[0, 2:5] = r.small[QUERY_BIAS : SCALES + 1]
+        r.rest[0, 5:8] = jnp.zeros((3, columns), jnp.float32)
         bulk.finish(r.bulk_out)
-        rest.step(1)
-        rest.step(2)
-        rest.step(3)
-        rest.finish(r.rest_out)
+        rest.run(r.rest_out)
     scatter.finish()
     head_ride.finish()
     finish_all(near_rides)
@@ -1907,6 +2200,7 @@
     )
     first = layer == 1
     if first:
+        inputs.update(dy_all_in=(record.dy_all_out, anywhere))
         outputs.update(small=(full_out(SMALL, columns), vmem))
     else:
         inputs.update(small_in=(small, vmem))
@@ -1923,8 +2217,8 @@
         gup=low(*unit_shape), gdown=low(*down_shape), dffn=full(rows, columns),
         dmiddle=full(rows, columns), packed=low(total // CHUNK, CHUNK // 2, 128),
         mixed=low(total // CHUNK, CHUNK // 2, 128),
-        out_sum=full(LINE * 32, columns), out_own=low(LINE, 32, columns),
-        pairs=low(total // CHUNK, CHUNK // 2, 128), dout=low(total, 64), delta=full(1, total), query=low(total, 64),
+        out_own=low(LINE, 32, columns),
+        dout=low(total, 64), delta=full(1, total), query=low(total, 64),
         keys=low(total, 64), values=low(total, 64), keys_t=low(64, total), dkeys=full(total, 64),
         dvalues=full(total, 64), dquery_t=full(64, total), flat=low(total // CHUNK, CHUNK, 192),
         head_w=low(columns, 192), gw=full(192, columns), head_own=low(columns, 192),
@@ -1938,9 +2232,10 @@
     scratch.update(unit_cross_sems=cross_sems, down_cross_sems=cross_sems, out_cross_sems=cross_sems)
     scratch.update(mid_gain=full(hidden, 1), gg=full(hidden, 1), gs=full(hidden, 1), gb=full(hidden, 1))
     if not first:
-        scratch.update(small=full(SMALL, columns), bulk=low(2 * SMALL, columns), rest=full(8, columns))
+        scratch.update(small=full(SMALL, columns), bulk=low(2 * SMALL, columns), rest=full(1, 8, columns))
         scratch.update(bulk_sum=AllSum.scratch((2 * SMALL, columns), jnp.bfloat16))
-        scratch.update(rest_sum=AllSum.scratch((8, columns), jnp.float32))
+        rest_got, rest_sems = QuickSum.scratch((8, columns))
+        scratch.update(rest_got=rest_got, rest_sems=rest_sems)
     kernel = functools.partial(backward_kernel, layer, hidden_all)
     call = lambda body, **how: pl.pallas_call(body, name="layer_backward", **how)
     return launch(call, kernel, inputs, outputs, scratch, collective_id, 105, 63)
@@ -2057,11 +2352,11 @@
         vec_gain=vec_gain.transpose(1, 0, 2), vec_bias=vec_bias.transpose(1, 0, 2), mid_gain=mid_gain, mid_bias=mid_bias,
         head_scale=head_scale,
     )
-    first = layer_forward_kernel(0, table, tokens, params, None, jnp.float32, 0)
+    first = layer_forward_kernel(0, table, tokens, params, None, None, jnp.float32, 0)
     first.x_in = tokens
     blocks = Refs(head=first.next_head, unit=first.next_unit)
-    second = layer_forward_kernel(1, table, first.y_out, params, blocks, jnp.bfloat16, 1)
-    second.x_in, second.head_blocks = first.y_out, blocks.head
+    second = layer_forward_kernel(1, table, first.y_out, params, blocks, grad_out, jnp.bfloat16, 1)
+    second.x_in, second.head_blocks = first.y_out, first.next_head
     back_second = layer_backward_kernel(1, table, grad_out, params, second, None, 2)
     back_first = layer_backward_kernel(0, table, back_second.dx, params, first, back_second.small, 3)
     kinds = (w_qkv, w_out, w_up, w_down, params.vec_gain, params.vec_bias, mid_gain, mid_bias, head_scale)

time: 537 us -> 508 us (0.946)
  Pallas kernels: 524 us -> 495 us
    pallas_call x4, Pallas kernels: 518 us -> 489 us  [launch(): call(body, out_shape=[shape for shape, _ in outputs.values()], in_specs=[...]
where the time goes in v4:
time: 508 us; the launch traced here: 499 us
  Pallas kernels  495 us (97%)
    pallas_call x4, Pallas kernels, launch(): call(body, out_shape=[shape for shape, _ in outputs.values()], in_specs=[...  489 us

profile of v4, /device:TPU:0, one launch (start us, length us, event | category | flops | bytes accessed | tf_op | source)
XLA Modules:
  0.0 498.7 jit_solution(1155961182643748100)
XLA Ops:
  1.3 0.1 and_select_fusion.3
  1.4 0.7 select_reduce_fusion
  2.2 0.7 broadcast_in_dim.31
  2.9 0.1 reshape.49
  3.0 0.1 and_select_fusion
  3.1 0.6 pad_add_fusion.refs_0_
  3.8 133.4 %layer_forward.2 = (f32[160,1024]{1,0:T(8,128)}, f32[160,1024]{1,0:T(8,128)}, f32[160,1024]{1,0:T(8,128)}, bf16[160,1024]{1,0:T(8,128)(2,1)}, f32[1,2560]{1,0:T(...) custom-call(s32[161]{0:T(256)} %pad_add_fusion.refs_0_, ...), custom_call_target="tpu_custom_call" | custom-call | bytes 332500000 | tf_op jit(solution)/shard_map/layer_forward/pallas_call | solution.py:1324
  137.2 109.5 %layer_forward.3 = (bf16[160,1024]{1,0:T(8,128)(2,1)}, f32[160,1024]{1,0:T(8,128)}, f32[160,1024]{1,0:T(8,128)}, bf16[160,1024]{1,0:T(8,128)(2,1)}, f32[1,2560]{...) custom-call(s32[161]{0:T(256)} %pad_add_fusion.refs_0_, ...), custom_call_target="tpu_custom_call" | custom-call | bytes 332500000 | tf_op jit(solution)/shard_map/layer_forward/pallas_call | solution.py:1324
  246.7 108.3 %layer_backward.2 = (f32[160,1024]{1,0:T(8,128)}, bf16[16,64,512]{2,1,0:T(8,128)(2,1)}, bf16[4,128,1024]{2,1,0:T(8,128)(2,1)}, bf16[4,32,1024]{2,1,0:T(8,128)(2,...) custom-call(s32[161]{0:T(256)} %pad_add_fusion.refs_0_, ...), custom_call_target="tpu_custom_call" | custom-call | bytes 367500000 | tf_op jit(solution)/shard_map/layer_backward/pallas_call | solution.py:1324
  355.0 137.4 %layer_backward.3 = (f32[160,1024]{1,0:T(8,128)}, bf16[16,64,512]{2,1,0:T(8,128)(2,1)}, bf16[4,128,1024]{2,1,0:T(8,128)(2,1)}, bf16[4,32,1024]{2,1,0:T(8,128)(2,...) custom-call(s32[161]{0:T(256)} %pad_add_fusion.refs_0_, ...), custom_call_target="tpu_custom_call" | custom-call | bytes 367500000 | tf_op jit(solution)/shard_map/layer_backward/pallas_call | solution.py:1324
  492.4 6.0 %assemble.1 = (bf16[160,1024]{1,0:T(8,128)(2,1)}, f32[160,1024]{1,0:T(8,128)}, f32[2,64,3072]{2,1,0:T(8,128)}, f32[2,64,1024]{2,1,0:T(8,128)}, f32[2,64,4096]{2,...) custom-call(bf16[160,1024]{1,0:T(8,128)(2,1)} %get-tuple-element.80., ...), custom_call_target="tpu_custom_call" | custom-call | bytes 17500000 | tf_op jit(solution)/shard_map/assemble/pallas_call | solution.py:2313

commit v5 on v4

--- a/solution.py
+++ b/solution.py
@@ -966,9 +966,11 @@
 
                     self.across(t, h).start()
 
-    def second(self, o_ref):
+    def second(self, o_ref, between=()):
         z = self.z
         for t in range(LINE):
+            if 0 < t <= len(between):
+                between[t - 1]()
             d = order_at(z, t)
             for h in range(HALVES):
                 self.twin(t, 1, h).wait_recv()
@@ -1639,16 +1641,21 @@
     down_ride.step(2)
     climb(x)
     plane_gather.far()
-    climb(1 - x)
-    pool.start()
-    down_ride.finish()
-    load_down.start()
     if first:
+        down_ride.finish()
+        load_down.start()
         quads[1].finish()
         next_unit_ride.start()
         next_head_ride.start()
+    climb(1 - x)
+    pool.start()
+    if not first:
+        down_ride.finish()
+        load_down.start()
     start_all(saves[3:7])
     pool.finish()
+    if first:
+        next_unit_ride.step(1)
     load_down.wait()
     means = [r.got_stat[i, 0:1] for i in range(PLANE)]
     mean = functools.reduce(jnp.add, means) * (1.0 / PLANE)
@@ -1683,10 +1690,8 @@
     start_all(saves[7:])
     plane_scatter.first()
     if first:
-        next_unit_ride.step(1)
+        next_unit_ride.step(2)
     plane_scatter.second()
-    if first:
-        next_unit_ride.step(2)
     plane_scatter.finish(r.result)
     r.y_out[...] = (r.middle[...] + (r.result[...] + biases[6][...])).astype(r.y_out.dtype)
     gather.finish()
@@ -1762,46 +1767,59 @@
     return launch(call, kernel, inputs, outputs, scratch, collective_id, 95, 56)
 
 
-class AllSum:
-    def __init__(self, own_ref, sent, got, send, recv):
-        self.own_ref, self.sent, self.got, self.send, self.recv = own_ref, sent, got, send, recv
-        self.z, self.y, self.c = place()
+class TreeSum:
+    def __init__(self, own_ref, total_ref, got, part, line, sems):
+        self.own_ref, self.total_ref, self.got, self.part, self.line = own_ref, total_ref, got, part, line
+        self.to_send, self.to_recv, self.back_send, self.back_recv = sems[0:4]
+        self.trade = Trade(part, line, *sems[4:7])
+        self.pool = PlanePool(None, got, None, None)
+        self.me = plane_index(self.pool.x, self.pool.y, self.pool.c)
 
     @staticmethod
-    def scratch(shape, kind):
+    def scratch(rows, columns):
         dma = pltpu.SemaphoreType.DMA
-        return [pltpu.VMEM((3, *shape), kind), pltpu.VMEM((LINE + 2, *shape), kind), dma((LINE + 2,)), dma((LINE + 2,))]
-
-    def copy(self, i):
-        z, y, c = self.z, self.y, self.c
-        where = (other_group(), device(z, y, 1 - c), device(z, 1 - y, c))[i] if i < 3 else None
-        if i >= 3:
-            where = device(lax.rem(z + i - 2, LINE), y, c)
-        source = self.own_ref if i == 0 else self.sent.at[min(i, 3) - 1]
-        return remote(source, self.got.at[i], self.send.at[i], self.recv.at[i], where)
+        bufs = [pltpu.VMEM((n, rows // PLANE, columns), jnp.float32) for n in (PLANE, 1, LINE)]
+        return bufs, [dma((PLANE,))] * 4 + Trade.scratch()
+
+    def slice(self, m):
+        rows = self.part.shape[1]
+        return pl.ds(pl.multiple_of(m * rows, 8), rows)
+
+    def to(self, d, x, y, c):
+        source = self.own_ref.at[self.slice(plane_index(x, y, c))]
+        where = plane_device(x, self.pool.z, y, c)
+        return remote(source, self.got.at[self.me], self.to_send.at[d], self.to_recv.at[d], where)
+
+    def back(self, d, x, y, c):
+        mine = self.total_ref.at[self.me]
+        return remote(mine, mine, self.back_send.at[d], self.back_recv.at[d], plane_device(x, self.pool.z, y, c))
+
+    def arrived(self, ref, recv):
+        for d, x, y, c in self.pool.others():
+            slot = ref.at[plane_index(x, y, c)]
+            remote(slot, slot, recv.at[d], recv.at[d], plane_device(x, self.pool.z, y, c)).wait_recv()
 
     def start(self):
-        self.copy(0).start()
-
-    def step(self, i):
-        self.copy(i - 1).wait_recv()
-        own = self.own_ref[...] if i == 1 else self.sent[i - 2]
-        self.sent[i - 1] = (own.astype(jnp.float32) + self.got[i - 1].astype(jnp.float32)).astype(self.sent.dtype)
-        for k in range(i, i + 1 if i < 3 else LINE + 2):
-            self.copy(k).start()
-
-    def finish(self, o_ref):
-        for i in range(3, LINE + 2):
-            self.copy(i).wait_recv()
-        total = None
-        for zz in range(LINE):
-            term = self.sent[2].astype(jnp.float32)
-            for s in range(1, LINE):
-                term = jnp.where(lax.rem(self.z - s + LINE, LINE) == zz, self.got[2 + s].astype(jnp.float32), term)
-            total = term if total is None else total + term
-        o_ref[...] = total
-        for i in range(LINE + 2):
-            self.copy(i).wait_send()
+        for other in self.pool.others():
+            self.to(*other).start()
+
+    def along_line(self):
+        self.arrived(self.got, self.to_recv)
+        self.got[self.me] = self.own_ref[self.slice(self.me)]
+        self.part[0] = functools.reduce(jnp.add, [self.got[m] for m in range(PLANE)])
+        self.trade.start()
+
+    def give_back(self):
+        self.trade.finish()
+        self.total_ref[self.me] = functools.reduce(jnp.add, [self.line[zz] for zz in range(LINE)])
+        for other in self.pool.others():
+            self.back(*other).start()
+
+    def finish(self):
+        self.arrived(self.total_ref, self.back_recv)
+        for other in self.pool.others():
+            self.to(*other).wait_send()
+            self.back(*other).wait_send()
 
 
 class QuickSum:
@@ -1855,15 +1873,16 @@
     pool = PlanePool(r.own_sums, r.got_sums, *r.pool_sems)
     unit_ride = Swap(r.gup, r.unit_got, *r.unit_sems)
     out_ride = Trade(r.out_own, r.out_got, *r.out_ride_sems)
-    head_ride = Swap(r.head_fold, r.head_got, *r.head_sems)
-    head_cross = Cross(r.head_own, r.head_other, *r.head_cross_sems)
+    head_cross = Cross(r.head_fold, r.head_other, *r.head_cross_sems)
     down_ride = Trade(r.gdown, r.gdown_got, *r.gdown_sems)
     near_rides = [
         Cross(r.unit_near, r.unit_far, *r.unit_cross_sems), Cross(r.down_near, r.down_far, *r.down_cross_sems),
         Cross(r.out_near, r.out_far, *r.out_cross_sems),
     ]
     if not first:
-        bulk = AllSum(r.bulk, *r.bulk_sum)
+        late_head_ride = Swap(r.late_head, r.late_head_got, *r.late_head_sems)
+        head_ride = Swap(r.head_fold, r.head_got, *r.head_sems)
+        bulk = TreeSum(r.bulk, r.bulk_out, *r.bulk_bufs, r.bulk_sems)
         rest = QuickSum(r.rest, *r.rest_got, r.rest_sems)
     hail_all()
     gains = of_layer(r.gains, layer)
@@ -1933,6 +1952,7 @@
     climb(x)
     if not first:
         plane_gather.far()
+        late_head_ride.start()
     climb(1 - x)
     pool.start()
     loads[4].wait()
@@ -2006,10 +2026,6 @@
     turned = jnp.transpose(jnp.concatenate(turned + [jnp.zeros((128, 4), jnp.float32)], axis=1))
     for i in range(3 * LINE):
         r.small[MID + i : MID + i + 1, unit_lanes(0, unit_slot)] = turned[i : i + 1]
-    if not first:
-        r.bulk[0:SMALL] = r.small_in[...].astype(jnp.bfloat16)
-        r.bulk[SMALL : 2 * SMALL] = r.small[...].astype(jnp.bfloat16)
-        bulk.start()
     loads[7].wait()
     load_head = pltpu.make_async_copy(r.head_blocks, r.head_fold, r.load_sem.at[6])
     load_head.start()
@@ -2077,14 +2093,10 @@
         r.dquery_t[:, at] = total_dq * 0.125
         if i == 2:
             out_scatter.second()
-            if not first:
-                bulk.step(1)
     out_sum = r.dffn.at[pl.ds(0, out_rows)]
     out_scatter.finish(out_sum)
     r.out_own[...] = out_sum[...].reshape(r.out_own.shape).astype(jnp.bfloat16)
     out_ride.start()
-    if not first:
-        bulk.step(2)
 
     head_bias = jnp.zeros((1, 192), jnp.float32)
     for i in range(tiles):
@@ -2095,6 +2107,12 @@
 
     r.small[QUERY_BIAS : QUERY_BIAS + 1] = spread_head(head_bias[:, 0:64], index, columns)
     r.small[VALUE_BIAS : VALUE_BIAS + 1] = spread_head(head_bias[:, 64:128], index, columns)
+
+    if not first:
+        r.bulk[0:SMALL] = r.small_in[...]
+        r.bulk[SMALL : 2 * SMALL] = r.small[...]
+        r.bulk[2 * SMALL :] = jnp.zeros((r.bulk.shape[0] - 2 * SMALL, columns), jnp.float32)
+        bulk.start()
 
     def restore(p, carry):
         r.flat[p] = r.qvk[r.table[chunks + p]]
@@ -2118,11 +2136,16 @@
         r.gw[...] = grad if t == 0 else r.gw[...] + grad
         if t + 2 < tiles:
             tile_load(t + 2).start()
-    r.head_own[...] = jnp.transpose(r.gw[...]).astype(jnp.bfloat16)
+    turned = jnp.transpose(r.gw[...]).astype(jnp.bfloat16)
+    for j in range(r.head_fold.shape[0]):
+        for part in range(2):
+            piece = turned[64 * j + 32 * part : 64 * j + 32 * part + 32]
+            r.head_fold[j, :, 128 * part : 128 * part + 128] = piece[:, 0:128]
+            r.head_fold[j, :, 256 + 64 * part : 320 + 64 * part] = piece[:, 128:192]
     head_cross.start()
     scatter.first()
     if not first:
-        bulk.step(3)
+        bulk.along_line()
     down_ride.finish()
     out_ride.finish()
     unit_ride.finish()
@@ -2133,13 +2156,12 @@
     for load in reloads:
         load.start()
     head_cross.finish()
-    for j in range(r.head_fold.shape[0]):
-        for part in range(2):
-            at = slice(64 * j + 32 * part, 64 * j + 32 * part + 32)
-            both = (r.head_own[at].astype(jnp.float32) + r.head_other[at].astype(jnp.float32)).astype(jnp.bfloat16)
-            r.head_fold[j, :, 128 * part : 128 * part + 128] = both[:, 0:128]
-            r.head_fold[j, :, 256 + 64 * part : 320 + 64 * part] = both[:, 128:192]
-    head_ride.start()
+    both = (r.head_fold[...].astype(jnp.float32) + r.head_other[...].astype(jnp.float32)).astype(jnp.bfloat16)
+    if first:
+        r.head_sum[...] = both
+    else:
+        r.head_fold[...] = both
+        head_ride.start()
     for load in reloads:
         load.wait()
     for q in range(4):
@@ -2156,16 +2178,17 @@
     if not first:
         r.rest[0, 0:1] = gain_grad
         r.rest[0, 1:2] = shift_grad
-        r.rest[0, 2:5] = r.small[QUERY_BIAS : SCALES + 1]
-        r.rest[0, 5:8] = jnp.zeros((3, columns), jnp.float32)
-        bulk.finish(r.bulk_out)
+        bulk.give_back()
         rest.run(r.rest_out)
+        bulk.finish()
     scatter.finish()
-    head_ride.finish()
+    if not first:
+        head_ride.finish()
+        late_head_ride.finish()
     finish_all(near_rides)
 
 
-def layer_backward_kernel(layer, table, dy, params, record, small, collective_id):
+def layer_backward_kernel(layer, table, dy, params, record, later, collective_id):
     rows, columns = dy.shape
     hidden_all = params.mid_gain.shape[1]
     total, plane_rows, hidden = rows * 4 * LINE, rows * PLANE, hidden_all // PLANE
@@ -2193,7 +2216,7 @@
     outputs = dict(
         dx=(full_out(rows, columns), vmem), unit_got=(low_out(*unit_shape), anywhere),
         gdown_got=(low_out(*down_shape), anywhere), out_got=(low_out(LINE, *out_near), anywhere),
-        head_got=(low_out(4 * LINE, 32, 384), anywhere), unit_near=(low_out(*unit_near), vmem),
+        unit_near=(low_out(*unit_near), vmem),
         down_near=(low_out(*down_near), vmem), out_near=(low_out(*out_near), vmem),
         unit_far=(low_out(*unit_near), anywhere), down_far=(low_out(*down_near), anywhere),
         out_far=(low_out(*out_near), anywhere),
@@ -2201,10 +2224,11 @@
     first = layer == 1
     if first:
         inputs.update(dy_all_in=(record.dy_all_out, anywhere))
-        outputs.update(small=(full_out(SMALL, columns), vmem))
+        outputs.update(small=(full_out(SMALL, columns), vmem), head_sum=(low_out(4 * LINE, 32, 384), vmem))
     else:
-        inputs.update(small_in=(small, vmem))
-        outputs.update(bulk_out=(full_out(2 * SMALL, columns), vmem), rest_out=(full_out(8, columns), vmem))
+        inputs.update(small_in=(later.small, vmem), late_head=(later.head_sum, anywhere))
+        outputs.update(head_got=(low_out(4 * LINE, 32, 384), anywhere), late_head_got=(low_out(4 * LINE, 32, 384), anywhere))
+        outputs.update(bulk_out=(full_out(PLANE, 8, columns), vmem), rest_out=(full_out(2, columns), vmem))
     plane_bufs, plane_sems = PlaneScatter.scratch(rows, columns)
     out_bufs, out_sems = PlaneScatter.scratch(LINE * 32, columns)
     group_bufs, group_sems = GroupScatter.scratch(rows, columns)
@@ -2221,8 +2245,8 @@
         dout=low(total, 64), delta=full(1, total), query=low(total, 64),
         keys=low(total, 64), values=low(total, 64), keys_t=low(64, total), dkeys=full(total, 64),
         dvalues=full(total, 64), dquery_t=full(64, total), flat=low(total // CHUNK, CHUNK, 192),
-        head_w=low(columns, 192), gw=full(192, columns), head_own=low(columns, 192),
-        head_other=low(columns, 192), head_fold=low(4 * LINE, 32, 384),
+        head_w=low(columns, 192), gw=full(192, columns),
+        head_other=low(4 * LINE, 32, 384), head_fold=low(4 * LINE, 32, 384),
         plane_bufs=plane_bufs, plane_sems=plane_sems, out_bufs=out_bufs, out_sems=out_sems,
         group_bufs=group_bufs, group_sems=group_sems, plane_gather_sems=PlaneGather.scratch(),
         pool_sems=([dma((PLANE,)), dma((PLANE,))]), unit_sems=swap_sems, gdown_sems=trade_sems, head_sems=swap_sems,
@@ -2232,9 +2256,10 @@
     scratch.update(unit_cross_sems=cross_sems, down_cross_sems=cross_sems, out_cross_sems=cross_sems)
     scratch.update(mid_gain=full(hidden, 1), gg=full(hidden, 1), gs=full(hidden, 1), gb=full(hidden, 1))
     if not first:
-        scratch.update(small=full(SMALL, columns), bulk=low(2 * SMALL, columns), rest=full(1, 8, columns))
-        scratch.update(bulk_sum=AllSum.scratch((2 * SMALL, columns), jnp.bfloat16))
-        rest_got, rest_sems = QuickSum.scratch((8, columns))
+        scratch.update(late_head_sems=swap_sems, small=full(SMALL, columns), bulk=full(8 * PLANE, columns), rest=full(1, 2, columns))
+        bulk_bufs, bulk_sems = TreeSum.scratch(8 * PLANE, columns)
+        scratch.update(bulk_bufs=bulk_bufs, bulk_sems=bulk_sems)
+        rest_got, rest_sems = QuickSum.scratch((2, columns))
         scratch.update(rest_got=rest_got, rest_sems=rest_sems)
     kernel = functools.partial(backward_kernel, layer, hidden_all)
     call = lambda body, **how: pl.pallas_call(body, name="layer_backward", **how)
@@ -2260,10 +2285,10 @@
             for ref, dest in ((down_ref, r.down), (out_ref, r.out)):
                 rows = ref.shape[0]
                 dest[layer, pl.ds(pl.multiple_of(half * rows, rows), rows)] = ref[...].astype(jnp.float32)
-        bulk = r.bulk[SMALL * (1 - layer) : SMALL * (2 - layer)]
-        rest = r.rest[...] if layer == 0 else bulk[0:1] * 0.0
-        gain, shift = (rest[0:1], rest[1:2]) if layer == 0 else (bulk[0:1], bulk[3:4])
-        heads = rest[2:4] if layer == 0 else bulk[QUERY_BIAS : VALUE_BIAS + 1]
+        per = r.bulk.shape[1]
+        bulk = r.bulk[SMALL // per * (1 - layer) : SMALL // per * (2 - layer)].reshape(SMALL, -1)
+        gain, shift = (r.rest[0:1], r.rest[1:2]) if layer == 0 else (bulk[0:1], bulk[3:4])
+        heads = bulk[QUERY_BIAS : VALUE_BIAS + 1]
         gain_rows = jnp.concatenate([gain, bulk[1:3]], axis=0)
         bias_rows = jnp.concatenate([shift, bulk[4:6], heads, bulk[OUT_BIAS : DOWN_BIAS + 1]], axis=0)
         for ref, rows in ((r.vec_gain, gain_rows), (r.vec_bias, bias_rows)):
@@ -2275,7 +2300,7 @@
             for i in range(2):
                 row = MID + (i + 1) * LINE + z
                 r.mid_bias[layer, i : i + 1, at] = bulk[row : row + 1]
-        row = rest[4:5] if layer == 0 else bulk[SCALES : SCALES + 1]
+        row = bulk[SCALES : SCALES + 1]
         heads_here = r.head_scale.shape[1]
         r.head_scale[layer : layer + 1] = row[:, layer * heads_here : (layer + 1) * heads_here]
 
@@ -2283,8 +2308,8 @@
 def assemble(results, dx, back, shapes):
     vmem, anywhere = pl.BlockSpec(memory_space=pltpu.VMEM), pl.BlockSpec(memory_space=pl.ANY)
     arrays = [results, dx]
-    for got in back:
-        arrays += [got.head_got, got.unit_near, got.unit_far, got.down_near, got.down_far, got.out_near, got.out_far]
+    for got, head in zip(back, (back[0].head_got, back[0].late_head_got)):
+        arrays += [head, got.unit_near, got.unit_far, got.down_near, got.down_far, got.out_near, got.out_far]
 
     arrays += [back[0].bulk_out, back[0].rest_out]
     n = len(arrays)
@@ -2358,7 +2383,7 @@
     second = layer_forward_kernel(1, table, first.y_out, params, blocks, grad_out, jnp.bfloat16, 1)
     second.x_in, second.head_blocks = first.y_out, first.next_head
     back_second = layer_backward_kernel(1, table, grad_out, params, second, None, 2)
-    back_first = layer_backward_kernel(0, table, back_second.dx, params, first, back_second.small, 3)
+    back_first = layer_backward_kernel(0, table, back_second.dx, params, first, back_second, 3)
     kinds = (w_qkv, w_out, w_up, w_down, params.vec_gain, params.vec_bias, mid_gain, mid_bias, head_scale)
     results = assemble(second.y_out, back_first.dx, [back_first, back_second], [array.shape for array in kinds])
     return (*results[:6], results[6].transpose(1, 0, 2), results[7].transpose(1, 0, 2), *results[8:])

time: 508 us -> 501 us (0.986)
  Pallas kernels: 495 us -> 488 us
    pallas_call x4, Pallas kernels: 489 us -> 482 us  [launch(): call(body, out_shape=[shape for shape, _ in outputs.values()], in_specs=[...]
where the time goes in v5:
time: 501 us; the launch traced here: 492 us
  Pallas kernels  488 us (97%)
    pallas_call x4, Pallas kernels, launch(): call(body, out_shape=[shape for shape, _ in outputs.values()], in_specs=[...  482 us

profile of v5, /device:TPU:0, one launch (start us, length us, event | category | flops | bytes accessed | tf_op | source)
XLA Modules:
  0.0 491.8 jit_solution(15354542210193118307)
XLA Ops:
  1.3 0.1 and_select_fusion.3
  1.4 0.7 select_reduce_fusion
  2.2 0.7 broadcast_in_dim.31
  2.9 0.1 reshape.49
  3.0 0.1 and_select_fusion
  3.1 0.6 pad_add_fusion.refs_0_
  3.8 130.2 %layer_forward.2 = (f32[160,1024]{1,0:T(8,128)}, f32[160,1024]{1,0:T(8,128)}, f32[160,1024]{1,0:T(8,128)}, bf16[160,1024]{1,0:T(8,128)(2,1)}, f32[1,2560]{1,0:T(...) custom-call(s32[161]{0:T(256)} %pad_add_fusion.refs_0_, ...), custom_call_target="tpu_custom_call" | custom-call | bytes 332500000 | tf_op jit(solution)/shard_map/layer_forward/pallas_call | solution.py:1326
  134.0 111.7 %layer_forward.3 = (bf16[160,1024]{1,0:T(8,128)(2,1)}, f32[160,1024]{1,0:T(8,128)}, f32[160,1024]{1,0:T(8,128)}, bf16[160,1024]{1,0:T(8,128)(2,1)}, f32[1,2560]{...) custom-call(s32[161]{0:T(256)} %pad_add_fusion.refs_0_, ...), custom_call_target="tpu_custom_call" | custom-call | bytes 332500000 | tf_op jit(solution)/shard_map/layer_forward/pallas_call | solution.py:1326
  245.7 99.0 %layer_backward.2 = (f32[160,1024]{1,0:T(8,128)}, bf16[16,64,512]{2,1,0:T(8,128)(2,1)}, bf16[4,128,1024]{2,1,0:T(8,128)(2,1)}, bf16[4,32,1024]{2,1,0:T(8,128)(2,...) custom-call(s32[161]{0:T(256)} %pad_add_fusion.refs_0_, ...), custom_call_target="tpu_custom_call" | custom-call | bytes 367500000 | tf_op jit(solution)/shard_map/layer_backward/pallas_call | solution.py:1326
  344.6 140.8 %layer_backward.3 = (f32[160,1024]{1,0:T(8,128)}, bf16[16,64,512]{2,1,0:T(8,128)(2,1)}, bf16[4,128,1024]{2,1,0:T(8,128)(2,1)}, bf16[4,32,1024]{2,1,0:T(8,128)(2,...) custom-call(s32[161]{0:T(256)} %pad_add_fusion.refs_0_, ...), custom_call_target="tpu_custom_call" | custom-call | bytes 367500000 | tf_op jit(solution)/shard_map/layer_backward/pallas_call | solution.py:1326
  485.5 6.1 %assemble.1 = (bf16[160,1024]{1,0:T(8,128)(2,1)}, f32[160,1024]{1,0:T(8,128)}, f32[2,64,3072]{2,1,0:T(8,128)}, f32[2,64,1024]{2,1,0:T(8,128)}, f32[2,64,4096]{2,...) custom-call(bf16[160,1024]{1,0:T(8,128)(2,1)} %get-tuple-element.81., ...), custom_call_target="tpu_custom_call" | custom-call | bytes 17500000 | tf_op jit(solution)/shard_map/assemble/pallas_call | solution.py:2338

commit v6 on v5

--- a/solution.py
+++ b/solution.py
@@ -1909,6 +1909,7 @@
     hailed_by_all()
     if not first:
         plane_gather.start()
+        late_head_ride.start()
     for load in loads[6:]:
         load.start()
 
@@ -1952,7 +1953,6 @@
     climb(x)
     if not first:
         plane_gather.far()
-        late_head_ride.start()
     climb(1 - x)
     pool.start()
     loads[4].wait()

time: 501 us -> 499 us (level)
  no operation moved by 1% of the time
where the time goes in v6:
time: 499 us; the launch traced here: 490 us
  Pallas kernels  486 us (97%)
    pallas_call x4, Pallas kernels, launch(): call(body, out_shape=[shape for shape, _ in outputs.values()], in_specs=[...  480 us

profile of v6, /device:TPU:0, one launch (start us, length us, event | category | flops | bytes accessed | tf_op | source)
XLA Modules:
  0.0 489.8 jit_solution(9222640992481702049)
XLA Ops:
  1.3 0.1 and_select_fusion.3
  1.4 0.7 select_reduce_fusion
  2.2 0.7 broadcast_in_dim.31
  2.9 0.1 reshape.49
  3.0 0.1 and_select_fusion
  3.1 0.6 pad_add_fusion.refs_0_
  3.8 130.2 %layer_forward.2 = (f32[160,1024]{1,0:T(8,128)}, f32[160,1024]{1,0:T(8,128)}, f32[160,1024]{1,0:T(8,128)}, bf16[160,1024]{1,0:T(8,128)(2,1)}, f32[1,2560]{1,0:T(...) custom-call(s32[161]{0:T(256)} %pad_add_fusion.refs_0_, ...), custom_call_target="tpu_custom_call" | custom-call | bytes 332500000 | tf_op jit(solution)/shard_map/layer_forward/pallas_call | solution.py:1326
  134.0 111.7 %layer_forward.3 = (bf16[160,1024]{1,0:T(8,128)(2,1)}, f32[160,1024]{1,0:T(8,128)}, f32[160,1024]{1,0:T(8,128)}, bf16[160,1024]{1,0:T(8,128)(2,1)}, f32[1,2560]{...) custom-call(s32[161]{0:T(256)} %pad_add_fusion.refs_0_, ...), custom_call_target="tpu_custom_call" | custom-call | bytes 332500000 | tf_op jit(solution)/shard_map/layer_forward/pallas_call | solution.py:1326
  245.7 99.0 %layer_backward.2 = (f32[160,1024]{1,0:T(8,128)}, bf16[16,64,512]{2,1,0:T(8,128)(2,1)}, bf16[4,128,1024]{2,1,0:T(8,128)(2,1)}, bf16[4,32,1024]{2,1,0:T(8,128)(2,...) custom-call(s32[161]{0:T(256)} %pad_add_fusion.refs_0_, ...), custom_call_target="tpu_custom_call" | custom-call | bytes 367500000 | tf_op jit(solution)/shard_map/layer_backward/pallas_call | solution.py:1326
  344.6 138.8 %layer_backward.3 = (f32[160,1024]{1,0:T(8,128)}, bf16[16,64,512]{2,1,0:T(8,128)(2,1)}, bf16[4,128,1024]{2,1,0:T(8,128)(2,1)}, bf16[4,32,1024]{2,1,0:T(8,128)(2,...) custom-call(s32[161]{0:T(256)} %pad_add_fusion.refs_0_, ...), custom_call_target="tpu_custom_call" | custom-call | bytes 367500000 | tf_op jit(solution)/shard_map/layer_backward/pallas_call | solution.py:1326
  483.5 6.1 %assemble.1 = (bf16[160,1024]{1,0:T(8,128)(2,1)}, f32[160,1024]{1,0:T(8,128)}, f32[2,64,3072]{2,1,0:T(8,128)}, f32[2,64,1024]{2,1,0:T(8,128)}, f32[2,64,4096]{2,...) custom-call(bf16[160,1024]{1,0:T(8,128)(2,1)} %get-tuple-element.81., ...), custom_call_target="tpu_custom_call" | custom-call | bytes 17500000 | tf_op jit(solution)/shard_map/assemble/pallas_call | solution.py:2338

commit v7 on v6

--- a/solution.py
+++ b/solution.py
@@ -1448,7 +1448,8 @@
     if first:
         head_ride.start()
     gather.start()
-    out_ride.start()
+    if first:
+        out_ride.start()
     mids = [r.mid_gain_all.at[pl.ds(layer, 1)], r.mid_bias_all.at[layer, pl.ds(0, 1)], r.mid_bias_all.at[layer, pl.ds(1, 1)]]
     unit_columns(mids, unit_slot, (r.mid_gain, r.mid_shift, r.mid_bias))
     head_bias = [own_head(biases[row], index) for row in (3, 4)] + [jnp.zeros((1, 64), jnp.float32)]
@@ -1465,12 +1466,19 @@
     if first:
         quads[0].finish()
         unit_ride.start()
-    out_ride.finish()
     out_rows = r.out_all.shape[0] // PLANE
-    for zz in range(LINE):
-        r.out_all[pl.ds(slot * out_rows + zz * 32, 32)] = r.out_got[zz]
     out_gather = PlaneGather(r.out_all, r.out_gather_sems)
-    out_gather.start()
+
+    def gather_out():
+        out_ride.finish()
+        for zz in range(LINE):
+            r.out_all[pl.ds(slot * out_rows + zz * 32, 32)] = r.out_got[zz]
+        out_gather.start()
+
+    if first:
+        gather_out()
+    else:
+        out_ride.start()
     dy_gather = None if first else PlaneGather(r.dy_all, r.dy_gather_sems)
     if first:
         head_ride.finish()
@@ -1539,7 +1547,9 @@
         r.pairs[i * per_tile : (i + 1) * per_tile] = pairs
         if i == 2 and first:
             unit_ride.step(1)
-        if i == 3:
+        if i == 1 and not first:
+            gather_out()
+        if i == (3 if first else tiles - 1):
             out_gather.near()
     if first:
         unit_ride.step(2)

time: 499 us -> 499 us (level)
  no operation moved by 1% of the time
where the time goes in v7:
time: 499 us; the launch traced here: 490 us
  Pallas kernels  486 us (97%)
    pallas_call x4, Pallas kernels, launch(): call(body, out_shape=[shape for shape, _ in outputs.values()], in_specs=[...  480 us

profile of v7, /device:TPU:0, one launch (start us, length us, event | category | flops | bytes accessed | tf_op | source)
XLA Modules:
  0.0 490.2 jit_solution(6614332241770063605)
XLA Ops:
  1.3 0.1 and_select_fusion.3
  1.4 0.7 select_reduce_fusion
  2.2 0.7 broadcast_in_dim.31
  2.9 0.1 reshape.49
  3.0 0.1 and_select_fusion
  3.1 0.6 pad_add_fusion.refs_0_
  3.8 130.2 %layer_forward.2 = (f32[160,1024]{1,0:T(8,128)}, f32[160,1024]{1,0:T(8,128)}, f32[160,1024]{1,0:T(8,128)}, bf16[160,1024]{1,0:T(8,128)(2,1)}, f32[1,2560]{1,0:T(...) custom-call(s32[161]{0:T(256)} %pad_add_fusion.refs_0_, ...), custom_call_target="tpu_custom_call" | custom-call | bytes 332500000 | tf_op jit(solution)/shard_map/layer_forward/pallas_call | solution.py:1326
  134.0 112.2 %layer_forward.3 = (bf16[160,1024]{1,0:T(8,128)(2,1)}, f32[160,1024]{1,0:T(8,128)}, f32[160,1024]{1,0:T(8,128)}, bf16[160,1024]{1,0:T(8,128)(2,1)}, f32[1,2560]{...) custom-call(s32[161]{0:T(256)} %pad_add_fusion.refs_0_, ...), custom_call_target="tpu_custom_call" | custom-call | bytes 332500000 | tf_op jit(solution)/shard_map/layer_forward/pallas_call | solution.py:1326
  246.2 98.5 %layer_backward.2 = (f32[160,1024]{1,0:T(8,128)}, bf16[16,64,512]{2,1,0:T(8,128)(2,1)}, bf16[4,128,1024]{2,1,0:T(8,128)(2,1)}, bf16[4,32,1024]{2,1,0:T(8,128)(2,...) custom-call(s32[161]{0:T(256)} %pad_add_fusion.refs_0_, ...), custom_call_target="tpu_custom_call" | custom-call | bytes 367500000 | tf_op jit(solution)/shard_map/layer_backward/pallas_call | solution.py:1326
  344.7 139.1 %layer_backward.3 = (f32[160,1024]{1,0:T(8,128)}, bf16[16,64,512]{2,1,0:T(8,128)(2,1)}, bf16[4,128,1024]{2,1,0:T(8,128)(2,1)}, bf16[4,32,1024]{2,1,0:T(8,128)(2,...) custom-call(s32[161]{0:T(256)} %pad_add_fusion.refs_0_, ...), custom_call_target="tpu_custom_call" | custom-call | bytes 367500000 | tf_op jit(solution)/shard_map/layer_backward/pallas_call | solution.py:1326
  483.8 6.1 %assemble.1 = (bf16[160,1024]{1,0:T(8,128)(2,1)}, f32[160,1024]{1,0:T(8,128)}, f32[2,64,3072]{2,1,0:T(8,128)}, f32[2,64,1024]{2,1,0:T(8,128)}, f32[2,64,4096]{2,...) custom-call(bf16[160,1024]{1,0:T(8,128)(2,1)} %get-tuple-element.81., ...), custom_call_target="tpu_custom_call" | custom-call | bytes 17500000 | tf_op jit(solution)/shard_map/assemble/pallas_call | solution.py:2348
